TPU v7x, 128 devices: a whole 4x4x4 slice. The times are simulated.
128 devices in a mesh: side: 2 (over y_hi), grp: 32 (over x, z, y_lo), tp: 2 (over core).
Axes of the slice: x: 4, y: 4 (y_hi: 2, y_lo: 2; y = y_hi * 2 + y_lo), z: 4, core: 2. Of those that a mesh axis runs over, the one named last changes fastest.
Arguments:
- residual: bfloat16 [2, 512, 7168], P('side', 'grp'), may hold values from -14 to 14
- moe_gain: bfloat16 [2, 7168], P('side'), may hold values from 0.5 to 1.5
- router: bfloat16 [2, 16, 7168], P('side'), may hold values from -0.0625 to 0.0625
- routes: int32 [2, 512, 8], P('side', 'grp'), may hold values from 0 to 15, all different within a row; in each aligned block of 8 rows (0 to 7, 8 to 15, ..., all dimensions but the last counted through in order) at most 5 rows name the same one
- gate_w: bfloat16 [2, 7168, 16384], P('side', None, ('grp', 'tp')), may hold values from -0.0625 to 0.0625
- up_w: bfloat16 [2, 7168, 16384], P('side', None, ('grp', 'tp')), may hold values from -0.0625 to 0.0625
- down_w: bfloat16 [2, 16384, 7168], P('side', ('grp', 'tp')), may hold values from -0.1875 to 0.1875
- attn_gain: bfloat16 [2, 7168], P('side', 'tp'), may hold values from 0.5 to 1.5
- kv_proj: bfloat16 [2, 576, 7168], P('side', None, 'tp'), may hold values from -0.0625 to 0.0625
- kv_gain: bfloat16 [2, 512], P('side'), may hold values from 0.5 to 1.5
- cache_latent: bfloat16 [2, 512, 128, 512], P('side', 'grp'), may hold values from -5 to 5
- cache_rope: bfloat16 [2, 512, 64, 128], P('side', 'grp'), may hold values from -5 to 5
- lengths: int32 [2, 512], P('side', 'grp'), may hold values from 2 to 128, as said below
- query_latent: bfloat16 [2, 512, 64, 512], P('side', 'grp', 'tp'), may hold values from -34 to 34
- query_rope: bfloat16 [2, 512, 4096], P('side', 'grp', 'tp'), may hold values from -5 to 5
Outputs:
- resid_out: bfloat16 [2, 512, 7168], P('side', 'grp')
- new_latent: bfloat16 [2, 512, 512], P('side', 'grp')
- new_rope: bfloat16 [2, 512, 64], P('side', 'grp')
- attn_latent: bfloat16 [2, 512, 64, 512], P('side', 'grp', 'tp')
Inputs may be any that keep to these rules, and one draw needn't show every extreme that they name: `routes`: within each aligned block of 8 rows every row names 8 different experts and no expert is named by more than 5 rows of the block. `lengths`: every attention group's 16 sequences include one with exactly 128 cached tokens.
All inputs are finite; a program needn't handle non-finite values.
Results may differ from a plain program's by a relative error of at most 0.015.
Values may be sent and summed in bfloat16 or wider, within the bound.
No kernel may reach another device: no remote copies, remote signals or barrier semaphores. Data moves between devices by JAX's collectives and lax.ppermute only.
A program may use at most 128 MiB of HBM per device.

v0:
```python
import jax
import jax.numpy as jnp
from jax import lax
from jax.sharding import PartitionSpec as P

NMB = 2
CAP = 5


NORM_EPS = 1e-06
ROUTE_SCALE = 2.5
ROPE_BASE = 10000.0
SCORE_SCALE = 192.0 ** (-0.5)


def rms_scale(values):
    return lax.rsqrt(jnp.mean(values * values, axis=-1, keepdims=True) + NORM_EPS)


def rotate(pair_part, position):
    half_width = pair_part.shape[-1] // 2
    step_ids = lax.broadcasted_iota(jnp.int32, (1, half_width), 1).astype(jnp.float32)
    inverse_freq = jnp.exp(-(2.0 * step_ids / pair_part.shape[-1]) * jnp.log(ROPE_BASE))
    angles = position.astype(jnp.float32)[:, None] * inverse_freq
    first_half = pair_part[:, :half_width]
    second_half = pair_part[:, half_width:]
    cosine = jnp.cos(angles)
    sine_part = jnp.sin(angles)
    return jnp.concatenate(
        [
            first_half * cosine - second_half * sine_part,
            first_half * sine_part + second_half * cosine,
        ],
        axis=-1,
    )


def mixing_tables(chosen, weight, targets, experts, capacity):
    expert_iota = lax.broadcasted_iota(jnp.int32, (1, 1, experts), 2)
    matches = (chosen[:, :, None] == expert_iota).astype(jnp.int32)
    per_row = jnp.sum(matches, axis=1)
    before = jnp.cumsum(per_row, axis=0) - per_row
    slots = jnp.sum(matches * before[:, None, :], axis=2)
    places = chosen * capacity + slots
    matching = places[None, None, :, :] == targets[:, :, None, None]
    row_count = chosen.shape[0]
    selector = jnp.any(matching, axis=3).astype(jnp.bfloat16).reshape(-1, row_count)
    mixing = jnp.einsum(
        "jcik,ik->ijc", matching.astype(jnp.bfloat16), weight, preferred_element_type=jnp.float32
    )
    return (selector, mixing.astype(jnp.bfloat16).reshape(row_count, -1))


def attend(operands):
    query_lat, query_rot, cache_lat, cache_rot, seq_lengths, fresh_lat, fresh_rot = operands
    head_count = query_lat.shape[1]
    query_rot = query_rot.reshape(query_rot.shape[0], head_count, -1)
    cache_scores = (
        jnp.einsum("thl,tpl->thp", query_lat, cache_lat, preferred_element_type=jnp.float32)
        + jnp.einsum("thr,trp->thp", query_rot, cache_rot, preferred_element_type=jnp.float32)
    ) * SCORE_SCALE
    own_scores = (
        jnp.einsum("thl,tl->th", query_lat, fresh_lat, preferred_element_type=jnp.float32)
        + jnp.einsum("thr,tr->th", query_rot, fresh_rot, preferred_element_type=jnp.float32)
    ) * SCORE_SCALE
    position_ids = lax.broadcasted_iota(jnp.int32, cache_scores.shape, 2)
    usable = position_ids < seq_lengths[:, None, None]
    cache_scores = jnp.where(usable, cache_scores, -1e30)
    peak = jnp.maximum(jnp.max(cache_scores, axis=2), own_scores)
    cache_weights = jnp.where(usable, jnp.exp(cache_scores - peak[:, :, None]), 0.0)
    own_weight = jnp.exp(own_scores - peak)
    denominator = jnp.sum(cache_weights, axis=2) + own_weight
    cache_probs = (cache_weights / denominator[:, :, None]).astype(jnp.bfloat16)
    own_probs = (own_weight / denominator).astype(jnp.bfloat16)
    mixed = jnp.einsum("thp,tpl->thl", cache_probs, cache_lat, preferred_element_type=jnp.float32)
    mixed = (
        mixed
        + own_probs.astype(jnp.float32)[:, :, None] * fresh_lat.astype(jnp.float32)[:, None, :]
    )
    return mixed.astype(jnp.bfloat16)


def body(
    residual,
    moe_gain,
    router,
    routes,
    gate_w,
    up_w,
    down_w,
    attn_gain,
    kv_proj,
    kv_gain,
    cache_latent,
    cache_rope,
    lengths,
    query_latent,
    query_rope,
):
    is_attn = lax.axis_index("side") == 0
    tp_index = lax.axis_index("tp")
    n_grp = lax.axis_size("grp")
    n_tp = lax.axis_size("tp")
    model_width = residual.shape[2]
    group_rows = residual.shape[1]
    rows_mb = group_rows // NMB
    experts = router.shape[1]
    expert_span = n_grp * n_tp // experts
    half_width = attn_gain.shape[1]
    latent_width = kv_gain.shape[1]
    heads_here = query_latent.shape[2]
    x_rows = residual[0].astype(jnp.float32)
    normed = x_rows * rms_scale(x_rows) * moe_gain[0].astype(jnp.float32)
    logits = jnp.dot(normed, router[0].astype(jnp.float32).T, precision=lax.Precision.HIGHEST)
    moe_in = normed.astype(jnp.bfloat16)
    scores = jax.nn.sigmoid(logits)
    chosen = routes[0]
    expert_iota = lax.broadcasted_iota(jnp.int32, (1, 1, experts), 2)
    picked = jnp.sum(jnp.where(chosen[:, :, None] == expert_iota, scores[:, None, :], 0.0), axis=2)
    weight = (ROUTE_SCALE * picked / jnp.sum(picked, axis=1, keepdims=True)).astype(jnp.bfloat16)
    dest_ids = lax.broadcasted_iota(jnp.int32, (n_grp, 1), 0)
    dest_expert = (dest_ids * n_tp + tp_index) // expert_span
    targets = dest_expert * CAP + lax.broadcasted_iota(jnp.int32, (n_grp, CAP), 1)
    outgoing_rows = []
    mixings = []
    for micro in range(NMB):
        start = micro * rows_mb
        selector, mixing = mixing_tables(
            chosen[start : start + rows_mb], weight[start : start + rows_mb], targets, experts, CAP
        )
        packed = jnp.dot(
            selector, moe_in[start : start + rows_mb], preferred_element_type=jnp.float32
        ).astype(jnp.bfloat16)
        packed = packed.reshape(n_grp, CAP, model_width)
        outgoing_rows.append(jnp.where(is_attn, packed, jnp.zeros_like(packed)))
        mixings.append(mixing)
    moe_parts = []
    for micro in range(NMB):
        empty_part = jnp.zeros_like(outgoing_rows[micro])
        sending = jnp.concatenate([empty_part, outgoing_rows[micro]], axis=0)
        arrived = lax.all_to_all(sending, ("side", "grp"), split_axis=0, concat_axis=0, tiled=True)[
            :n_grp
        ]
        flat_rows = arrived.reshape(-1, model_width)

        def compute_rows(flat_in):
            gate_val = jnp.dot(flat_in, gate_w[0], preferred_element_type=jnp.float32)
            up_val = jnp.dot(flat_in, up_w[0], preferred_element_type=jnp.float32)
            hidden = (jax.nn.silu(gate_val) * up_val).astype(jnp.bfloat16)
            return jnp.dot(hidden, down_w[0], preferred_element_type=jnp.float32).astype(
                jnp.bfloat16
            )

        def skip_rows(flat_in):
            return jnp.zeros_like(flat_in)

        answer = lax.cond(is_attn, skip_rows, compute_rows, flat_rows).reshape(arrived.shape)
        backward = jnp.concatenate([answer, jnp.zeros_like(answer)], axis=0)
        arrived_back = lax.all_to_all(
            backward, ("side", "grp"), split_axis=0, concat_axis=0, tiled=True
        )
        moe_parts.append(
            jnp.dot(
                mixings[micro],
                arrived_back[n_grp:].reshape(-1, model_width),
                preferred_element_type=jnp.float32,
            )
        )
    resid_parts = []
    latent_parts = []
    rope_parts = []
    attn_parts = []
    for micro in range(NMB):
        start = micro * rows_mb
        moe_total = lax.psum(moe_parts[micro].astype(jnp.bfloat16), "tp").astype(jnp.float32)
        updated = (x_rows[start : start + rows_mb] + moe_total).astype(jnp.bfloat16)
        updated_half = lax.dynamic_slice_in_dim(
            updated, tp_index * half_width, half_width, 1
        ).astype(jnp.float32)
        scaled = (updated_half * attn_gain[0].astype(jnp.float32)).astype(jnp.bfloat16)
        square_sums = jnp.sum(updated_half * updated_half, axis=1)
        partial_kv = lax.dot_general(
            scaled, kv_proj[0], (((1,), (1,)), ((), ())), preferred_element_type=jnp.float32
        )
        square_sums, kv_raw = lax.psum((square_sums, partial_kv), "tp")
        kv_raw = kv_raw * lax.rsqrt(square_sums / model_width + NORM_EPS)[:, None]
        latent = kv_raw[:, :latent_width]
        fresh_lat = (latent * rms_scale(latent) * kv_gain[0].astype(jnp.float32)).astype(
            jnp.bfloat16
        )
        seq_lengths = lengths[0, start : start + rows_mb]
        fresh_rot = rotate(kv_raw[:, latent_width:], seq_lengths).astype(jnp.bfloat16)
        operands = (
            query_latent[0, start : start + rows_mb],
            query_rope[0, start : start + rows_mb],
            cache_latent[0, start : start + rows_mb],
            cache_rope[0, start : start + rows_mb],
            seq_lengths,
            fresh_lat,
            fresh_rot,
        )

        def skip_attention(unused):
            return jnp.zeros((rows_mb, heads_here, latent_width), jnp.bfloat16)

        attended = lax.cond(is_attn, attend, skip_attention, operands)
        resid_parts.append(updated)
        latent_parts.append(fresh_lat)
        rope_parts.append(fresh_rot)
        attn_parts.append(attended)

    def keep_role(value):
        return jnp.where(is_attn, value, jnp.zeros_like(value))[None]

    return (
        keep_role(jnp.concatenate(resid_parts, axis=0)),
        keep_role(jnp.concatenate(latent_parts, axis=0)),
        keep_role(jnp.concatenate(rope_parts, axis=0)),
        keep_role(jnp.concatenate(attn_parts, axis=0)),
    )


def solution(mesh):
    in_specs = (
        P("side", "grp", None),
        P("side", None),
        P("side", None, None),
        P("side", "grp", None),
        P("side", None, ("grp", "tp")),
        P("side", None, ("grp", "tp")),
        P("side", ("grp", "tp"), None),
        P("side", "tp"),
        P("side", None, "tp"),
        P("side", None),
        P("side", "grp", None, None),
        P("side", "grp", None, None),
        P("side", "grp"),
        P("side", "grp", "tp", None),
        P("side", "grp", "tp"),
    )
    out_specs = (
        P("side", "grp", None),
        P("side", "grp", None),
        P("side", "grp", None),
        P("side", "grp", "tp", None),
    )
    return jax.shard_map(body, mesh=mesh, in_specs=in_specs, out_specs=out_specs, check_vma=False)
```

profile of v0, /device:TPU:1, one launch (start us, length us, event | category | flops | bytes accessed | tf_op | source)
XLA Modules:
  0.0 506.9 jit_solution(1746146278294257364)
XLA Ops:
  13.3 2.8 select_n.114
  16.1 6.2 %concatenate.92 = bf16[64,5,7168]{2,1,0:T(8,128)(2,1)} pad(bf16[32,5,7168]{2,1,0:T(8,128)(2,1)} %select_n.114, bf16[]{:T(256)} %constant.99.clone.1), padding=32_0x0_0x0_0 | pad | bytes 6881282 | tf_op jit(solution)/shard_map/concatenate | solution.py:140
  22.3 12.2 %all-to-all-start = ((bf16[64,5,7168]{2,1,0:T(8,128)(2,1)}), bf16[64,5,7168]{2,1,0:T(8,128)(2,1)}, u32[]{:S(2)}, u32[]{:S(2)}) async-start(bf16[64,5,7168]{2,1,0:T(8,128)(2,1)} %concatenate.92), calls=%async_computation | async-start | bytes 14680064 | tf_op jit(solution)/shard_map/all_to_all | solution.py:141
  35.6 2.8 select_n.116
  38.5 6.2 %concatenate.95 = bf16[64,5,7168]{2,1,0:T(8,128)(2,1)} pad(bf16[32,5,7168]{2,1,0:T(8,128)(2,1)} %select_n.116, bf16[]{:T(256)} %constant.99.clone.1), padding=32_0x0_0x0_0 | pad | bytes 6881282 | tf_op jit(solution)/shard_map/concatenate | solution.py:140
  44.7 78.2 %all-to-all-done = bf16[64,5,7168]{2,1,0:T(8,128)(2,1)} async-done(((bf16[64,5,7168]{2,1,0:T(8,128)(2,1)}), bf16[64,5,7168]{2,1,0:T(8,128)(2,1)}, u32[]{:S(2)}, u32[]{:S(2)}) %all-to-all-start) | async-done | bytes 4587552 | tf_op jit(solution)/shard_map/all_to_all | solution.py:141
  122.9 18.2 %all-to-all-start.2 = ((bf16[64,5,7168]{2,1,0:T(8,128)(2,1)}), bf16[64,5,7168]{2,1,0:T(8,128)(2,1)}, u32[]{:S(2)}, u32[]{:S(2)}) async-start(bf16[64,5,7168]{2,1,0:T(8,128)(2,1)} %concatenate.95), calls=%async_computation.2 | async-start | bytes 14680064 | tf_op jit(solution)/shard_map/all_to_all | solution.py:141
  142.8 4.6 reshape.361
  147.4 6.1 %concatenate.93 = bf16[64,5,7168]{2,1,0:T(8,128)(2,1)} pad(bf16[32,5,7168]{2,1,0:T(8,128)(2,1)} %reshape.361, bf16[]{:T(256)} %constant.99.clone.1), padding=0_32x0_0x0_0 | pad | bytes 6881282 | tf_op jit(solution)/shard_map/concatenate | solution.py:158
  153.6 73.8 %all-to-all-done.2 = bf16[64,5,7168]{2,1,0:T(8,128)(2,1)} async-done(((bf16[64,5,7168]{2,1,0:T(8,128)(2,1)}), bf16[64,5,7168]{2,1,0:T(8,128)(2,1)}, u32[]{:S(2)}, u32[]{:S(2)}) %all-to-all-start.2) | async-done | bytes 4587552 | tf_op jit(solution)/shard_map/all_to_all | solution.py:141
  227.4 18.2 %all-to-all-start.1 = ((bf16[64,5,7168]{2,1,0:T(8,128)(2,1)}), bf16[64,5,7168]{2,1,0:T(8,128)(2,1)}, u32[]{:S(2)}, u32[]{:S(2)}) async-start(bf16[64,5,7168]{2,1,0:T(8,128)(2,1)} %concatenate.93), calls=%async_computation.1 | async-start | bytes 14680064 | tf_op jit(solution)/shard_map/all_to_all | solution.py:159
  247.3 4.6 reshape.364
  252.0 6.2 %concatenate.96 = bf16[64,5,7168]{2,1,0:T(8,128)(2,1)} pad(bf16[32,5,7168]{2,1,0:T(8,128)(2,1)} %reshape.364, bf16[]{:T(256)} %constant.99.clone.1), padding=0_32x0_0x0_0 | pad | bytes 6881282 | tf_op jit(solution)/shard_map/concatenate | solution.py:158
  258.2 77.3 %all-to-all-done.1 = bf16[64,5,7168]{2,1,0:T(8,128)(2,1)} async-done(((bf16[64,5,7168]{2,1,0:T(8,128)(2,1)}), bf16[64,5,7168]{2,1,0:T(8,128)(2,1)}, u32[]{:S(2)}, u32[]{:S(2)}) %all-to-all-start.1) | async-done | bytes 4587552 | tf_op jit(solution)/shard_map/all_to_all | solution.py:159
  335.5 14.6 %all-to-all-start.3 = ((bf16[64,5,7168]{2,1,0:T(8,128)(2,1)}), bf16[64,5,7168]{2,1,0:T(8,128)(2,1)}, u32[]{:S(2)}, u32[]{:S(2)}) async-start(bf16[64,5,7168]{2,1,0:T(8,128)(2,1)} %concatenate.96), calls=%async_computation.3 | async-start | bytes 14680064 | tf_op jit(solution)/shard_map/all_to_all | solution.py:159
  351.6 2.3 slice.139
  356.1 82.6 %all-to-all-done.3 = bf16[64,5,7168]{2,1,0:T(8,128)(2,1)} async-done(((bf16[64,5,7168]{2,1,0:T(8,128)(2,1)}), bf16[64,5,7168]{2,1,0:T(8,128)(2,1)}, u32[]{:S(2)}, u32[]{:S(2)}) %all-to-all-start.3) | async-done | bytes 4587552 | tf_op jit(solution)/shard_map/all_to_all | solution.py:159
  438.7 2.3 slice.143
  441.0 2.2 fusion.99
  443.4 34.8 %all-reduce.8.cloned.1.call-done = (bf16[8,7168]{1,0:T(8,128)(2,1)}, bf16[8,7168]{1,0:T(8,128)(2,1)}) async-done(((bf16[8,7168]{1,0:T(8,128)(2,1)}, bf16[8,7168]{1,0:T(8,128)(2,1)}), (bf16[8,7168]{1,0:T(8,128)(2,1)}, bf16[8,7168]{1,0:T(8,128)(2,1)})) %all-reduce.8.cloned.1.call-update) | async-done | bytes 229392 | tf_op jit(solution)/shard_map/psum | solution.py:175
  479.5 3.4 fusion.102
  484.3 3.5 all-reduce.4
  488.8 4.2 conditional.6
  493.1 4.2 conditional.7
  (108 shorter events, 32.4 us)
Async XLA Ops:
  7.2 343.1 %copy-start = (bf16[1,16,7168]{2,1,0:T(8,128)(2,1)S(1)}, bf16[1,16,7168]{2,1,0:T(8,128)(2,1)}, u32[]{:S(2)}) copy-start(bf16[1,16,7168]{2,1,0:T(8,128)(2,1)} %param.25) | copy-start | bytes 688132
  22.3 100.6 %all-to-all-start = ((bf16[64,5,7168]{2,1,0:T(8,128)(2,1)}), bf16[64,5,7168]{2,1,0:T(8,128)(2,1)}, u32[]{:S(2)}, u32[]{:S(2)}) async-start(bf16[64,5,7168]{2,1,0:T(8,128)(2,1)} %concatenate.92), calls=%async_computation | async-start | bytes 14680064 | tf_op jit(solution)/shard_map/all_to_all | solution.py:141
  122.9 104.5 %all-to-all-start.2 = ((bf16[64,5,7168]{2,1,0:T(8,128)(2,1)}), bf16[64,5,7168]{2,1,0:T(8,128)(2,1)}, u32[]{:S(2)}, u32[]{:S(2)}) async-start(bf16[64,5,7168]{2,1,0:T(8,128)(2,1)} %concatenate.95), calls=%async_computation.2 | async-start | bytes 14680064 | tf_op jit(solution)/shard_map/all_to_all | solution.py:141
  227.4 108.1 %all-to-all-start.1 = ((bf16[64,5,7168]{2,1,0:T(8,128)(2,1)}), bf16[64,5,7168]{2,1,0:T(8,128)(2,1)}, u32[]{:S(2)}, u32[]{:S(2)}) async-start(bf16[64,5,7168]{2,1,0:T(8,128)(2,1)} %concatenate.93), calls=%async_computation.1 | async-start | bytes 14680064 | tf_op jit(solution)/shard_map/all_to_all | solution.py:159
  258.2 92.0 %copy-start.5 = (s32[1,16,8]{1,2,0:T(8,128)S(1)}, s32[1,16,8]{1,2,0:T(8,128)}, u32[]{:S(2)}) copy-start(s32[1,16,8]{1,2,0:T(8,128)} %param.26) | copy-start | bytes 1540
  258.2 92.1 %copy-start.6 = (bf16[1,3584]{1,0:T(2,128)(2,1)S(1)}, bf16[1,3584]{1,0:T(2,128)(2,1)}, u32[]{:S(2)}) copy-start(bf16[1,3584]{1,0:T(2,128)(2,1)} %param.30) | copy-start | bytes 21508
  258.2 92.1 %copy-start.2 = (bf16[1,16,7168]{2,1,0:T(8,128)(2,1)S(1)}, bf16[1,16,7168]{2,1,0:T(8,128)(2,1)}, u32[]{:S(2)}) copy-start(bf16[1,16,7168]{2,1,0:T(8,128)(2,1)} %param.23) | copy-start | bytes 688132
  335.5 103.2 %all-to-all-start.3 = ((bf16[64,5,7168]{2,1,0:T(8,128)(2,1)}), bf16[64,5,7168]{2,1,0:T(8,128)(2,1)}, u32[]{:S(2)}, u32[]{:S(2)}) async-start(bf16[64,5,7168]{2,1,0:T(8,128)(2,1)} %concatenate.96), calls=%async_computation.3 | async-start | bytes 14680064 | tf_op jit(solution)/shard_map/all_to_all | solution.py:159
  350.1 128.1 %all-reduce.8.cloned.1.call-start = ((), (), s32[]{:S(2)}) async-start(), calls=%async_computation.4 | async-start | bytes 458752 | tf_op jit(solution)/shard_map/psum | solution.py:175
  356.1 87.2 %copy-start.8 = (bf16[1,512]{1,0:T(2,128)(2,1)S(1)}, bf16[1,512]{1,0:T(2,128)(2,1)}, u32[]{:S(2)}) copy-start(bf16[1,512]{1,0:T(2,128)(2,1)} %param.32) | copy-start | bytes 3076
  356.1 87.2 %copy-start.7 = (s32[1,16]{1,0:T(1,128)S(1)}, s32[1,16]{1,0:T(1,128)}, u32[]{:S(2)}) copy-start(s32[1,16]{1,0:T(1,128)} %param.35) | copy-start | bytes 196
  478.2 4.7 copy-start.1
  479.5 9.3 %copy-start.3 = (bf16[1,16,64,128]{3,2,1,0:T(8,128)(2,1)S(1)}, bf16[1,16,64,128]{3,2,1,0:T(8,128)(2,1)}, u32[]{:S(2)}) copy-start(bf16[1,16,64,128]{3,2,1,0:T(8,128)(2,1)} %param.34) | copy-start | bytes 786436
  479.5 9.3 %copy-start.4 = (bf16[1,16,2048]{2,1,0:T(8,128)(2,1)S(1)}, bf16[1,16,2048]{2,1,0:T(8,128)(2,1)}, u32[]{:S(2)}) copy-start(bf16[1,16,2048]{2,1,0:T(8,128)(2,1)} %param.37) | copy-start | bytes 196612
  479.5 9.3 %copy-start.9 = (bf16[1,16,32,512]{3,2,1,0:T(8,128)(2,1)S(1)}, bf16[1,16,32,512]{3,2,1,0:T(8,128)(2,1)}, u32[]{:S(2)}) copy-start(bf16[1,16,32,512]{3,2,1,0:T(8,128)(2,1)} %param.36) | copy-start | bytes 1572868
Sparse Core Ops, SparseCore 0:
  443.3 34.8 all-reduce.7
where the time goes:
time: 508 us; the launch traced here: 507 us
  waiting for transfers between devices  347 us (68%)
  starting transfers between devices  63.2 us (12%)
  local copies, waits for them, and re-layouts  49.6 us (10%)
  matrix products  19 us (4%)
  between operations  14.4 us (3%)
  other arithmetic  10.2 us (2%)
    all_to_all x2, waiting for transfers between devices, body(): lax.all_to_all(backward, ('side', 'grp'), split_axis=0, concat_axis=0, ti...  160 us
    all_to_all x2, waiting for transfers between devices, body(): lax.all_to_all(sending, ('side', 'grp'), split_axis=0, concat_axis=0, til...  152 us
    psum x1, waiting for transfers between devices, body(): lax.psum(moe_parts[micro].astype(jnp.bfloat16), 'tp').astype(jnp.float32)  34.8 us
    all_to_all x2, starting transfers between devices, body(): lax.all_to_all(backward, ('side', 'grp'), split_axis=0, concat_axis=0, ti...  32.8 us
    all_to_all x2, starting transfers between devices, body(): lax.all_to_all(sending, ('side', 'grp'), split_axis=0, concat_axis=0, til...  30.4 us
    concatenate x2, local copies, waits for them, and re-layouts, body(): sending = jnp.concatenate([empty_part, outgoing_rows[micro]], axis=0)  12.4 us
    concatenate x2, local copies, waits for them, and re-layouts, body(): backward = jnp.concatenate([answer, jnp.zeros_like(answer)], axis=0)  12.3 us
  transfers between devices with their start and end apart: 5, of which 5 were waited for; matrix products, arithmetic and copies ran while one was open for 8% of the time, Pallas kernels for 0%

commit v1 on v0

v1 whole, which is shorter than its diff:
```python
import jax
import jax.numpy as jnp
from jax import lax
from jax.sharding import PartitionSpec as P

SIDES = 2
NX = 4
NZ = 4
NY = 2
NT = 2
AXES = ("side", "grp", "tp")

NORM_EPS = 1e-06
ROUTE_SCALE = 2.5
ROPE_BASE = 10000.0
SCORE_SCALE = 192.0 ** (-0.5)
WEIGHT_LANES = 128

BF16 = jnp.bfloat16
F32 = jnp.float32


def place(side, x, z, y, t):
    return side * (NX * NZ * NY * NT) + ((x * NZ + z) * NY + y) * NT + t


def columns():
    return [(x, z, y, t) for x in range(NX) for z in range(NZ) for y in range(NY) for t in range(NT)]


def cross_pairs(source, flip):
    return [
        (place(source, x, z, y, t), place(1 - source, x, z, (y + flip) % NY, t))
        for x, z, y, t in columns()
    ]


def ring_pairs(leg, step):
    pairs = []
    for x, z, y, t in columns():
        along_x = leg == t
        to = ((x + step) % NX, z) if along_x else (x, (z + step) % NZ)
        pairs.append((place(1, x, z, y, t), place(1, to[0], to[1], y, t)))
    return pairs


def core_pairs(side):
    return [(place(side, x, z, y, t), place(side, x, z, y, 1 - t)) for x, z, y, t in columns()]


def send(value, pairs):
    return lax.ppermute(value, AXES, pairs)


def gather_ring(own, leg):
    half = own.shape[0] // 2
    before = send(own, ring_pairs(leg, 1))
    after = send(own, ring_pairs(leg, -1))
    far_a = send(before[:half], ring_pairs(leg, 1))
    far_b = send(after[half:], ring_pairs(leg, -1))
    return jnp.concatenate([own, before, after, far_a, far_b], axis=0)


def add(*values):
    total = values[0].astype(F32)
    for value in values[1:]:
        total = total + value.astype(F32)
    return total.astype(BF16)


def scatter_ring(parts, leg):
    rows = parts.shape[0] // 4
    half = rows // 2
    own, before, after = (parts[i * rows : (i + 1) * rows] for i in range(3))
    far_a, far_b = parts[3 * rows : 3 * rows + half], parts[3 * rows + half :]
    from_after = send(far_a, ring_pairs(leg, -1))
    from_before = send(far_b, ring_pairs(leg, 1))
    before = jnp.concatenate([add(before[:half], from_after), before[half:]], axis=0)
    after = jnp.concatenate([after[:half], add(after[half:], from_before)], axis=0)
    return add(own, send(before, ring_pairs(leg, -1)), send(after, ring_pairs(leg, 1)))


def rms_scale(values):
    return lax.rsqrt(jnp.mean(values * values, axis=-1, keepdims=True) + NORM_EPS)


def rotate(pair_part, position):
    half_width = pair_part.shape[-1] // 2
    step_ids = lax.broadcasted_iota(jnp.int32, (1, half_width), 1).astype(F32)
    inverse_freq = jnp.exp(-(2.0 * step_ids / pair_part.shape[-1]) * jnp.log(ROPE_BASE))
    angles = position.astype(F32)[:, None] * inverse_freq
    first_half = pair_part[:, :half_width]
    second_half = pair_part[:, half_width:]
    cosine = jnp.cos(angles)
    sine_part = jnp.sin(angles)
    return jnp.concatenate(
        [
            first_half * cosine - second_half * sine_part,
            first_half * sine_part + second_half * cosine,
        ],
        axis=-1,
    )


def attend_cache(operands):
    query_lat, query_rot, cache_lat, cache_rot, seq_lengths = operands
    scores = (
        jnp.einsum("thl,tpl->thp", query_lat, cache_lat, preferred_element_type=F32)
        + jnp.einsum("thr,trp->thp", query_rot, cache_rot, preferred_element_type=F32)
    ) * SCORE_SCALE
    usable = lax.broadcasted_iota(jnp.int32, scores.shape, 2) < seq_lengths[:, None, None]
    scores = jnp.where(usable, scores, -1e30)
    peak = jnp.max(scores, axis=2)
    weights = jnp.where(usable, jnp.exp(scores - peak[:, :, None]), 0.0)
    mixed = jnp.einsum("thp,tpl->thl", weights.astype(BF16), cache_lat, preferred_element_type=F32)
    return mixed, peak, jnp.sum(weights, axis=2)


def body(
    residual,
    moe_gain,
    router,
    routes,
    gate_w,
    up_w,
    down_w,
    attn_gain,
    kv_proj,
    kv_gain,
    cache_latent,
    cache_rope,
    lengths,
    query_latent,
    query_rope,
):
    is_attn = lax.axis_index("side") == 0
    tp_index = lax.axis_index("tp")
    own_expert = lax.axis_index("grp") // NY
    model_width = residual.shape[2]
    group_rows = residual.shape[1]
    rows = group_rows // NT
    experts = router.shape[1]
    half_width = attn_gain.shape[1]
    latent_width = kv_gain.shape[1]
    heads_here = query_latent.shape[2]

    def own_rows(value):
        return lax.dynamic_slice_in_dim(value, tp_index * rows, rows, 0)

    x_rows = own_rows(residual[0]).astype(F32)
    normed = x_rows * rms_scale(x_rows) * moe_gain[0].astype(F32)
    logits = jnp.dot(normed, router[0].astype(F32).T, precision=lax.Precision.HIGHEST)
    scores = jax.nn.sigmoid(logits)
    chosen = own_rows(routes[0])
    expert_iota = lax.broadcasted_iota(jnp.int32, (1, 1, experts), 2)
    named = jnp.any(chosen[:, :, None] == expert_iota, axis=1)
    picked = jnp.where(named, scores, 0.0)
    weight = (ROUTE_SCALE * picked / jnp.sum(picked, axis=1, keepdims=True)).astype(BF16)
    outgoing = jnp.concatenate(
        [normed.astype(BF16), jnp.pad(weight, ((0, 0), (0, WEIGHT_LANES - experts)))], axis=1
    )

    gate_other, up_other, down_other = (
        send(value[0], core_pairs(1)) for value in (gate_w, up_w, down_w)
    )
    kv_other = send(kv_proj[0], core_pairs(0))
    gain_other = send(attn_gain, core_pairs(0))

    arrived = jnp.concatenate(
        [send(outgoing, cross_pairs(0, 0)), send(outgoing, cross_pairs(0, 1))], axis=0
    )
    everything = gather_ring(gather_ring(arrived, 0), 1)
    flat = everything[:, :model_width]
    all_weights = everything[:, model_width : model_width + experts].astype(F32)
    mine = lax.broadcasted_iota(jnp.int32, (1, experts), 1) == own_expert
    row_weight = jnp.sum(jnp.where(mine, all_weights, 0.0), axis=1, keepdims=True)

    def hidden_of(gate_part, up_part):
        gate_val = jnp.dot(flat, gate_part, preferred_element_type=F32)
        up_val = jnp.dot(flat, up_part, preferred_element_type=F32)
        return (jax.nn.silu(gate_val) * up_val).astype(BF16)

    answer = jnp.dot(hidden_of(gate_w[0], up_w[0]), down_w[0], preferred_element_type=F32) + jnp.dot(
        hidden_of(gate_other, up_other), down_other, preferred_element_type=F32
    )
    answer = (answer * row_weight).astype(BF16)
    answer = scatter_ring(scatter_ring(answer, 1), 0)
    back_same = send(answer[:rows], cross_pairs(1, 0))
    back_flip = send(answer[rows:], cross_pairs(1, 1))

    operands = (
        query_latent[0],
        query_rope[0].reshape(group_rows, heads_here, -1),
        cache_latent[0],
        cache_rope[0],
        lengths[0],
    )

    def skip_attention(unused):
        return (
            jnp.zeros((group_rows, heads_here, latent_width), F32),
            jnp.zeros((group_rows, heads_here), F32),
            jnp.ones((group_rows, heads_here), F32),
        )

    mixed, peak, mass = lax.cond(is_attn, attend_cache, skip_attention, operands)

    moe_total = back_same.astype(F32) + back_flip.astype(F32)
    updated = (x_rows + moe_total).astype(BF16)
    updated_other = send(updated, core_pairs(0))
    updated_f = updated.astype(F32)

    def project(start, gain_part, proj_part):
        part = lax.dynamic_slice_in_dim(updated, start, half_width, 1).astype(F32)
        scaled = (part * gain_part.astype(F32)).astype(BF16)
        return lax.dot_general(
            scaled, proj_part, (((1,), (1,)), ((), ())), preferred_element_type=F32
        )

    kv_raw = project(tp_index * half_width, attn_gain[0], kv_proj[0]) + project(
        (1 - tp_index) * half_width, gain_other[0], kv_other
    )
    kv_raw = kv_raw * rms_scale(updated_f)
    latent = kv_raw[:, :latent_width]
    fresh_lat = (latent * rms_scale(latent) * kv_gain[0].astype(F32)).astype(BF16)
    fresh_rot = rotate(kv_raw[:, latent_width:], own_rows(lengths[0])).astype(BF16)
    fresh = jnp.concatenate([fresh_lat, fresh_rot], axis=1)
    fresh_other = send(fresh, core_pairs(0))

    def both(own, other):
        first = tp_index == 0
        return jnp.concatenate([jnp.where(first, own, other), jnp.where(first, other, own)], axis=0)

    fresh = both(fresh, fresh_other)
    fresh_lat, fresh_rot = fresh[:, :latent_width], fresh[:, latent_width:]
    own_scores = (
        jnp.sum(query_latent[0].astype(F32) * fresh_lat.astype(F32)[:, None, :], axis=2)
        + jnp.sum(operands[1].astype(F32) * fresh_rot.astype(F32)[:, None, :], axis=2)
    ) * SCORE_SCALE
    top = jnp.maximum(peak, own_scores)
    kept = jnp.exp(peak - top)
    own_weight = jnp.exp(own_scores - top)
    denominator = mass * kept + own_weight
    attended = (
        mixed * (kept / denominator)[:, :, None]
        + (own_weight / denominator)[:, :, None] * fresh_lat.astype(F32)[:, None, :]
    ).astype(BF16)

    def keep_role(value):
        return jnp.where(is_attn, value, jnp.zeros_like(value))[None]

    return (
        keep_role(both(updated, updated_other)),
        keep_role(fresh_lat),
        keep_role(fresh_rot),
        keep_role(attended),
    )


def solution(mesh):
    in_specs = (
        P("side", "grp", None),
        P("side", None),
        P("side", None, None),
        P("side", "grp", None),
        P("side", None, ("grp", "tp")),
        P("side", None, ("grp", "tp")),
        P("side", ("grp", "tp"), None),
        P("side", "tp"),
        P("side", None, "tp"),
        P("side", None),
        P("side", "grp", None, None),
        P("side", "grp", None, None),
        P("side", "grp"),
        P("side", "grp", "tp", None),
        P("side", "grp", "tp"),
    )
    out_specs = (
        P("side", "grp", None),
        P("side", "grp", None),
        P("side", "grp", None),
        P("side", "grp", "tp", None),
    )
    return jax.shard_map(body, mesh=mesh, in_specs=in_specs, out_specs=out_specs, check_vma=False)
```

time: 508 us -> 199 us (0.39)
  waiting for transfers between devices: 347 us -> 81.3 us
  local copies, waits for them, and re-layouts: 49.6 us -> 10.8 us
  matrix products: 19 us -> 45 us
  starting transfers between devices: 63.2 us -> 46.7 us
  between operations: 14.4 us -> 1.31 us
    all_to_all x4 -> x0, waiting for transfers between devices: 312 us -> none  [the longest x2 160 us: body(): lax.all_to_all(backward, ('side', 'grp'), split_axis=0, concat_axis=0, ti...]
    ppermute x0 -> x27, waiting for transfers between devices: none -> 81.3 us  [send(): return lax.ppermute(value, AXES, pairs)]
    all_to_all x4 -> x0, starting transfers between devices: 63.2 us -> none  [the longest x2 32.8 us: body(): lax.all_to_all(backward, ('side', 'grp'), split_axis=0, concat_axis=0, ti...]
    ppermute x0 -> x27, starting transfers between devices: none -> 46.7 us  [send(): return lax.ppermute(value, AXES, pairs)]
    psum x1 -> x0, waiting for transfers between devices: 34.8 us -> none  [body(): lax.psum(moe_parts[micro].astype(jnp.bfloat16), 'tp').astype(jnp.float32)]
    dot_general x19 -> x10, matrix products: 19 us -> 45 us  [the longest x1 12.2 us: body(): jnp.dot(hidden_of(gate_other, up_other), down_other, preferred_element_ty...]
    concatenate x4 -> x2, local copies, waits for them, and re-layouts: 24.7 us -> 1.5 us  [gather_ring(): return jnp.concatenate([own, before, after, far_a, far_b], axis=0)]
    reshape x4 -> x0, local copies, waits for them, and re-layouts: 9.56 us -> none  [the longest x2 9.3 us: body(): lax.cond(is_attn, skip_rows, compute_rows, flat_rows).reshape(arrived.shape)]
  transfers between devices with their start and end apart: 5 -> 27, of which waited for: 5 -> 5; matrix products, arithmetic and copies ran while one was open for 8% -> 21% of each run, Pallas kernels for 0% -> 0%
where the time goes in v1:
time: 199 us; the launch traced here: 198 us
  waiting for transfers between devices  81.3 us (41%)
  starting transfers between devices  46.7 us (23%)
  matrix products  45 us (23%)
  other arithmetic  12.7 us (6%)
  local copies, waits for them, and re-layouts  10.8 us (5%)
    ppermute x27, waiting for transfers between devices, send(): return lax.ppermute(value, AXES, pairs)  81.3 us
    ppermute x27, starting transfers between devices, send(): return lax.ppermute(value, AXES, pairs)  46.7 us
    dot_general x1, matrix products, body(): jnp.dot(hidden_of(gate_other, up_other), down_other, preferred_element_ty...  12.2 us
    dot_general x1, matrix products, body(): jnp.dot(hidden_of(gate_w[0], up_w[0]), down_w[0], preferred_element_type=...  11.2 us
    dot_general x2, matrix products, hidden_of(): up_val = jnp.dot(flat, up_part, preferred_element_type=F32)  8.54 us
    dot_general x2, matrix products, project(): lax.dot_general(scaled, proj_part, (((1,), (1,)), ((), ())), preferred_el...  6.85 us
    unnamed x31, local copies, waits for them, and re-layouts  6.53 us
  transfers between devices with their start and end apart: 27, of which 5 were waited for; matrix products, arithmetic and copies ran while one was open for 21% of the time, Pallas kernels for 0%

profile of v1, /device:TPU:1, one launch (start us, length us, event | category | flops | bytes accessed | tf_op | source)
XLA Modules:
  0.0 197.8 jit_solution(15194959079811232252)
XLA Ops:
  4.5 1.4 fusion.104
  6.1 5.7 %collective-permute-start = (bf16[8,7296]{1,0:T(8,128)(2,1)S(1)}, bf16[8,7296]{1,0:T(8,128)(2,1)S(1)}, u32[]{:S(2)}, u32[]{:S(2)}) collective-permute-start(bf16[8,7296]{1,0:T(8,128)(2,1)S(1)} %fusion.62), channel_id=1, source_target_pairs={{0,64},{1,65},{2,66},{3,67},{4,68},{5,69},{6,70},{7,71},{8,72},{9,... | collective-permute-start | bytes 350216 | tf_op jit(solution)/shard_map/ppermute | solution.py:52
  11.7 1.3 collective-permute-start.1
  14.2 3.1 %collective-permute-done.1 = bf16[8,7296]{1,0:T(8,128)(2,1)S(1)} collective-permute-done((bf16[8,7296]{1,0:T(8,128)(2,1)S(1)}, bf16[8,7296]{1,0:T(8,128)(2,1)S(1)}, u32[]{:S(2)}, u32[]{:S(2)}) %collective-permute-start.1) | collective-permute-done | bytes 116768 | tf_op jit(solution)/shard_map/ppermute | solution.py:52
  24.9 2.5 %collective-permute-start.11 = (bf16[7168,256]{1,0:T(8,128)(2,1)}, bf16[7168,256]{1,0:T(8,128)(2,1)}, u32[]{:S(2)}, u32[]{:S(2)}) collective-permute-start(bf16[7168,256]{1,0:T(8,128)(2,1)} %bitcast.9), channel_id=1, source_target_pairs={{64,65},{65,64},{66,67},{67,66},{68,69},{69,68},{70,71},{71,70},{7... | collective-permute-start | bytes 11010056 | tf_op jit(solution)/shard_map/ppermute | solution.py:52
  27.5 2.5 %collective-permute-start.10 = (bf16[7168,256]{1,0:T(8,128)(2,1)}, bf16[7168,256]{1,0:T(8,128)(2,1)}, u32[]{:S(2)}, u32[]{:S(2)}) collective-permute-start(bf16[7168,256]{1,0:T(8,128)(2,1)} %bitcast.8), channel_id=1, source_target_pairs={{64,65},{65,64},{66,67},{67,66},{68,69},{69,68},{70,71},{71,70},{7... | collective-permute-start | bytes 11010056 | tf_op jit(solution)/shard_map/ppermute | solution.py:52
  29.9 2.5 %collective-permute-start.12 = (bf16[256,7168]{1,0:T(8,128)(2,1)}, bf16[256,7168]{1,0:T(8,128)(2,1)}, u32[]{:S(2)}, u32[]{:S(2)}) collective-permute-start(bf16[256,7168]{1,0:T(8,128)(2,1)} %bitcast.10), channel_id=1, source_target_pairs={{64,65},{65,64},{66,67},{67,66},{68,69},{69,68},{70,71},{71,70},{7... | collective-permute-start | bytes 11010056 | tf_op jit(solution)/shard_map/ppermute | solution.py:52
  38.7 4.3 %fusion.28 = f32[256,256]{1,0:T(8,128)S(1)} fusion(bf16[256,7296]{1,0:T(8,128)(2,1)} %constant_dynamic-update-slice_fusion.8, bf16[1,7168,256]{2,1,0:T(8,128)(2,1)} %param.22), kind=kOutput, calls=%fused_computation.24 | convolution fusion | flops 939524096 | bytes 7602176 | tf_op jit(solution)/shard_map/dot_general | solution.py:180
  42.9 11.2 %fusion.51 = f32[256,7168]{1,0:T(8,128)} fusion(f32[256,256]{1,0:T(8,128)S(1)} %fusion.28, bf16[256,7296]{1,0:T(8,128)(2,1)} %constant_dynamic-update-slice_fusion.8, bf16[1,256,7168]{2,1,0:T(8,128)(2,1)} %param.23, bf16[1,7168,256]{2,1,0:T(8,128)(2,1)} %param.21), kind=kOutput, calls=%fused_computation.68 | convolution fusion | flops 1879441408 | bytes 18612224 | tf_op jit(solution)/shard_map/dot_general | solution.py:183
  54.1 4.3 %fusion.24 = f32[256,256]{1,0:T(8,128)S(1)} fusion(bf16[7168,256]{1,0:T(8,128)(2,1)} %collective-permute-done.11, bf16[256,7296]{1,0:T(8,128)(2,1)} %constant_dynamic-update-slice_fusion.8), kind=kOutput, calls=%fused_computation.20 | convolution fusion | flops 939524096 | bytes 7602176 | tf_op jit(solution)/shard_map/dot_general | solution.py:180
  58.4 12.2 %fusion.23 = bf16[256,7168]{1,0:T(8,128)(2,1)} fusion(f32[256,7168]{1,0:T(8,128)} %fusion.51, bf16[256,7168]{1,0:T(8,128)(2,1)} %collective-permute-done.12, f32[256]{0:T(256)S(1)} %select_reduce_fusion, f32[256,256]{1,0:T(8,128)S(1)} %fusion.24, bf16[7168,256]{1,0:T(8,128)(2,1)} %collective-permute-done.10, ...), kind=kOutput, calls=%fused_computation.19 | convolution fusion | flops 1884946432 | bytes 22283264 | tf_op jit(solution)/shard_map/dot_general | solution.py:183
  70.6 1.7 fusion.101
  79.1 2.4 %collective-permute-start.25 = (bf16[576,3584]{1,0:T(8,128)(2,1)}, bf16[576,3584]{1,0:T(8,128)(2,1)}, u32[]{:S(2)}, u32[]{:S(2)}) collective-permute-start(bf16[576,3584]{1,0:T(8,128)(2,1)} %bitcast.13), channel_id=1, source_target_pairs={{0,1},{1,0},{2,3},{3,2},{4,5},{5,4},{6,7},{7,6},{8,9},{9,8},{10,11... | collective-permute-start | bytes 12386312 | tf_op jit(solution)/shard_map/ppermute | solution.py:52
  81.6 1.9 collective-permute-start.24
  83.7 1.3 collective-permute-start.21
  85.0 1.3 collective-permute-start.22
  86.4 1.9 collective-permute-done.24
  88.3 74.6 %collective-permute-done.21 = bf16[8,7168]{1,0:T(8,128)(2,1)S(1)} collective-permute-done((bf16[8,7168]{1,0:T(8,128)(2,1)S(1)}, bf16[8,7168]{1,0:T(8,128)(2,1)S(1)}, u32[]{:S(2)}, u32[]{:S(2)}) %collective-permute-start.21) | collective-permute-done | bytes 114720 | tf_op jit(solution)/shard_map/ppermute | solution.py:52
  164.3 3.5 %fusion.66 = f32[8,576]{1,0:T(8,128)S(1)} fusion(f32[3584]{0:T(1024)S(1)} %convert_reduce_fusion.1, bf16[8,7168]{1,0:T(8,128)(2,1)S(1)} %get-tuple-element.34, s32[]{:T(128)S(6)} %select_n.105, bf16[1,576,3584]{2,1,0:T(8,128)(2,1)} %param.25), kind=kOutput, calls=%fused_computation.80 | convolution fusion | flops 33116160 | bytes 4220932 | tf_op jit(solution)/shard_map/dot_general | solution.py:216
  167.8 3.4 %fusion.32 = f32[8,576]{1,0:T(8,128)S(1)} fusion(f32[8,576]{1,0:T(8,128)S(1)} %fusion.66, bf16[576,3584]{1,0:T(8,128)(2,1)} %collective-permute-done.25, f32[3584]{0:T(1024)S(1)} %convert_reduce_fusion, bf16[8,7168]{1,0:T(8,128)(2,1)S(1)} %get-tuple-element.34, s32[]{:T(128)S(6)} %select_n.106, f32[8]{0:T(128)S(1)} %add_rsqrt_fusion.1), kind=kOutput, calls=%fused_computation.30 | convolution fusion | flops 33125376 | bytes 4241924 | tf_op jit(solution)/shard_map/dot_general | solution.py:216
  171.6 12.0 %collective-permute-start.26 = (bf16[8,576]{1,0:T(8,128)(2,1)S(1)}, bf16[8,576]{1,0:T(8,128)(2,1)S(1)}, u32[]{:S(2)}, u32[]{:S(2)}) collective-permute-start(bf16[8,576]{1,0:T(8,128)(2,1)S(1)} %pad_maximum_fusion.4), channel_id=1, source_target_pairs={{0,1},{1,0},{2,3},{3,2},{4,5},{5,4},{6,7},{7,6},{8,9},{9,8},{10,11... | collective-permute-start | bytes 27656 | tf_op jit(solution)/shard_map/ppermute | solution.py:52
  183.8 5.9 %conditional.1 = (f32[16,32,512]{2,1,0:T(8,128)S(1)}, f32[16,32]{1,0:T(8,128)}, f32[16,32]{1,0:T(8,128)S(1)}) conditional(s32[]{:T(128)} %convert_element_type.211, () %tuple.16, (s32[1,16]{1,0:T(1,128)S(1)}, bf16[1,16,128,512]{3,2,1,0:T(8,128)(2,1)S(1)}, bf16[16,32,512]{2,1,0:T(8,128)(2,1)}, bf16[1,16,64,128]{3,2,1,0:T(8,128)(2,1)}, ...), branch_computations={%region_6.7_spmd, %region_7.10_spmd} | conditional | flops 143457280 | bytes 7413976 | solution.py:206
  185.0 2.5 %fusion.100 = (f32[16,32]{1,0:T(8,128)}, f32[16,32,128]{2,1,0:T(8,128)S(1)}) fusion(f32[16,32,128]{2,1,0:T(8,128)S(1)} %fusion.13, bf16[16,32,512]{2,1,0:T(8,128)(2,1)} %get-tuple-element.13, bf16[1,16,128,512]{3,2,1,0:T(8,128)(2,1)S(1)} %get-tuple-element.29, s32[16]{0:T(128)S(1)} %bitcast.85), kind=kOutput, calls=%fused_computation.157 | convolution fusion | flops 67436032 | bytes 3147840 | tf_op jit(solution)/shard_map/cond/branch_1_fun/thl,tpl->thp/dot_general | solution.py:108
  189.7 2.1 %collective-permute-start.23 = (bf16[8,7168]{1,0:T(8,128)(2,1)}, bf16[8,7168]{1,0:T(8,128)(2,1)S(1)}, u32[]{:S(2)}, u32[]{:S(2)}) collective-permute-start(bf16[8,7168]{1,0:T(8,128)(2,1)} %copy-done.4), channel_id=1, source_target_pairs={{0,1},{1,0},{2,3},{3,2},{4,5},{5,4},{6,7},{7,6},{8,9},{9,8},{10,11... | collective-permute-start | bytes 344072 | tf_op jit(solution)/shard_map/ppermute | solution.py:52
  (123 shorter events, 37.2 us)
Async XLA Ops:
  6.1 7.5 %collective-permute-start = (bf16[8,7296]{1,0:T(8,128)(2,1)S(1)}, bf16[8,7296]{1,0:T(8,128)(2,1)S(1)}, u32[]{:S(2)}, u32[]{:S(2)}) collective-permute-start(bf16[8,7296]{1,0:T(8,128)(2,1)S(1)} %fusion.62), channel_id=1, source_target_pairs={{0,64},{1,65},{2,66},{3,67},{4,68},{5,69},{6,70},{7,71},{8,72},{9,... | collective-permute-start | bytes 350216 | tf_op jit(solution)/shard_map/ppermute | solution.py:52
  11.7 5.5 %collective-permute-start.1 = (bf16[8,7296]{1,0:T(8,128)(2,1)S(1)}, bf16[8,7296]{1,0:T(8,128)(2,1)S(1)}, u32[]{:S(2)}, u32[]{:S(2)}) collective-permute-start(bf16[8,7296]{1,0:T(8,128)(2,1)S(1)} %fusion.62), channel_id=1, source_target_pairs={{0,66},{1,67},{2,64},{3,65},{4,70},{5,71},{6,68},{7,69},{8,74},{9,... | collective-permute-start | bytes 350216 | tf_op jit(solution)/shard_map/ppermute | solution.py:52
  17.9 1.4 collective-permute-start.2
  18.5 1.4 collective-permute-start.3
  19.3 2.9 %collective-permute-start.4 = (bf16[8,7296]{1,0:T(8,128)(2,1)S(1)}, bf16[8,7296]{1,0:T(8,128)(2,1)S(1)}, u32[]{:S(2)}, u32[]{:S(2)}) collective-permute-start(bf16[8,7296]{1,0:T(8,128)(2,1)S(1)} %slice.123), channel_id=1, source_target_pairs={{64,80},{65,69},{66,82},{67,71},{68,84},{69,73},{70,86},{71,75},{7... | collective-permute-start | bytes 350216 | tf_op jit(solution)/shard_map/ppermute | solution.py:52
  20.0 2.8 %collective-permute-start.5 = (bf16[8,7296]{1,0:T(8,128)(2,1)S(1)}, bf16[8,7296]{1,0:T(8,128)(2,1)S(1)}, u32[]{:S(2)}, u32[]{:S(2)}) collective-permute-start(bf16[8,7296]{1,0:T(8,128)(2,1)S(1)} %slice.124), channel_id=1, source_target_pairs={{64,112},{65,77},{66,114},{67,79},{68,116},{69,65},{70,118},{71,67... | collective-permute-start | bytes 350216 | tf_op jit(solution)/shard_map/ppermute | solution.py:52
  23.5 9.0 %collective-permute-start.6 = (bf16[64,7296]{1,0:T(8,128)(2,1)S(1)}, bf16[64,7296]{1,0:T(8,128)(2,1)S(1)}, u32[]{:S(2)}, u32[]{:S(2)}) collective-permute-start(bf16[64,7296]{1,0:T(8,128)(2,1)S(1)} %get-tuple-element.57), channel_id=1, source_target_pairs={{64,68},{65,81},{66,70},{67,83},{68,72},{69,85},{70,74},{71,87},{7... | collective-permute-start | bytes 2801672 | tf_op jit(solution)/shard_map/ppermute | solution.py:52
  24.2 9.0 %collective-permute-start.7 = (bf16[64,7296]{1,0:T(8,128)(2,1)S(1)}, bf16[64,7296]{1,0:T(8,128)(2,1)S(1)}, u32[]{:S(2)}, u32[]{:S(2)}) collective-permute-start(bf16[64,7296]{1,0:T(8,128)(2,1)S(1)} %get-tuple-element.57), channel_id=1, source_target_pairs={{64,76},{65,113},{66,78},{67,115},{68,64},{69,117},{70,66},{71,119... | collective-permute-start | bytes 2801672 | tf_op jit(solution)/shard_map/ppermute | solution.py:52
  24.9 29.2 %collective-permute-start.11 = (bf16[7168,256]{1,0:T(8,128)(2,1)}, bf16[7168,256]{1,0:T(8,128)(2,1)}, u32[]{:S(2)}, u32[]{:S(2)}) collective-permute-start(bf16[7168,256]{1,0:T(8,128)(2,1)} %bitcast.9), channel_id=1, source_target_pairs={{64,65},{65,64},{66,67},{67,66},{68,69},{69,68},{70,71},{71,70},{7... | collective-permute-start | bytes 11010056 | tf_op jit(solution)/shard_map/ppermute | solution.py:52
  27.5 30.9 %collective-permute-start.10 = (bf16[7168,256]{1,0:T(8,128)(2,1)}, bf16[7168,256]{1,0:T(8,128)(2,1)}, u32[]{:S(2)}, u32[]{:S(2)}) collective-permute-start(bf16[7168,256]{1,0:T(8,128)(2,1)} %bitcast.8), channel_id=1, source_target_pairs={{64,65},{65,64},{66,67},{67,66},{68,69},{69,68},{70,71},{71,70},{7... | collective-permute-start | bytes 11010056 | tf_op jit(solution)/shard_map/ppermute | solution.py:52
  29.9 28.5 %collective-permute-start.12 = (bf16[256,7168]{1,0:T(8,128)(2,1)}, bf16[256,7168]{1,0:T(8,128)(2,1)}, u32[]{:S(2)}, u32[]{:S(2)}) collective-permute-start(bf16[256,7168]{1,0:T(8,128)(2,1)} %bitcast.10), channel_id=1, source_target_pairs={{64,65},{65,64},{66,67},{67,66},{68,69},{69,68},{70,71},{71,70},{7... | collective-permute-start | bytes 11010056 | tf_op jit(solution)/shard_map/ppermute | solution.py:52
  32.5 3.5 %collective-permute-start.8 = (bf16[32,7296]{1,0:T(8,128)(2,1)S(1)}, bf16[32,7296]{1,0:T(8,128)(2,1)S(1)}, u32[]{:S(2)}, u32[]{:S(2)}) collective-permute-start(bf16[32,7296]{1,0:T(8,128)(2,1)S(1)} %slice.125), channel_id=1, source_target_pairs={{64,68},{65,81},{66,70},{67,83},{68,72},{69,85},{70,74},{71,87},{7... | collective-permute-start | bytes 1400840 | tf_op jit(solution)/shard_map/ppermute | solution.py:52
  33.3 3.6 %collective-permute-start.9 = (bf16[32,7296]{1,0:T(8,128)(2,1)S(1)}, bf16[32,7296]{1,0:T(8,128)(2,1)S(1)}, u32[]{:S(2)}, u32[]{:S(2)}) collective-permute-start(bf16[32,7296]{1,0:T(8,128)(2,1)S(1)} %slice.126), channel_id=1, source_target_pairs={{64,76},{65,113},{66,78},{67,115},{68,64},{69,117},{70,66},{71,119... | collective-permute-start | bytes 1400840 | tf_op jit(solution)/shard_map/ppermute | solution.py:52
  72.3 1.4 collective-permute-start.13
  74.0 1.9 collective-permute-start.14
  76.3 1.4 collective-permute-start.17
  77.8 5.8 %collective-permute-start.18 = (bf16[16,7168]{1,0:T(8,128)(2,1)S(1)}, bf16[16,7168]{1,0:T(8,128)(2,1)S(1)}, u32[]{:S(2)}, u32[]{:S(2)}) collective-permute-start(bf16[16,7168]{1,0:T(8,128)(2,1)S(1)} %pad_maximum_fusion.2), channel_id=1, source_target_pairs={{64,112},{65,77},{66,114},{67,79},{68,116},{69,65},{70,118},{71,67... | collective-permute-start | bytes 688136 | tf_op jit(solution)/shard_map/ppermute | solution.py:52
  78.5 5.1 %collective-permute-start.20 = (bf16[16,7168]{1,0:T(8,128)(2,1)S(1)}, bf16[16,7168]{1,0:T(8,128)(2,1)S(1)}, u32[]{:S(2)}, u32[]{:S(2)}) collective-permute-start(bf16[16,7168]{1,0:T(8,128)(2,1)S(1)} %pad_maximum_fusion.3), channel_id=1, source_target_pairs={{64,80},{65,69},{66,82},{67,71},{68,84},{69,73},{70,86},{71,75},{7... | collective-permute-start | bytes 688136 | tf_op jit(solution)/shard_map/ppermute | solution.py:52
  79.1 88.7 %collective-permute-start.25 = (bf16[576,3584]{1,0:T(8,128)(2,1)}, bf16[576,3584]{1,0:T(8,128)(2,1)}, u32[]{:S(2)}, u32[]{:S(2)}) collective-permute-start(bf16[576,3584]{1,0:T(8,128)(2,1)} %bitcast.13), channel_id=1, source_target_pairs={{0,1},{1,0},{2,3},{3,2},{4,5},{5,4},{6,7},{7,6},{8,9},{9,8},{10,11... | collective-permute-start | bytes 12386312 | tf_op jit(solution)/shard_map/ppermute | solution.py:52
  81.6 6.7 %collective-permute-start.24 = (bf16[1,3584]{1,0:T(2,128)(2,1)S(1)}, bf16[1,3584]{1,0:T(2,128)(2,1)S(1)}, u32[]{:S(2)}, u32[]{:S(2)}) collective-permute-start(bf16[1,3584]{1,0:T(2,128)(2,1)S(1)} %copy-done.7), channel_id=1, source_target_pairs={{0,1},{1,0},{2,3},{3,2},{4,5},{5,4},{6,7},{7,6},{8,9},{9,8},{10,11... | collective-permute-start | bytes 21512 | tf_op jit(solution)/shard_map/ppermute | solution.py:52
  83.7 79.2 %collective-permute-start.21 = (bf16[8,7168]{1,0:T(8,128)(2,1)S(1)}, bf16[8,7168]{1,0:T(8,128)(2,1)S(1)}, u32[]{:S(2)}, u32[]{:S(2)}) collective-permute-start(bf16[8,7168]{1,0:T(8,128)(2,1)S(1)} %get-tuple-element.55), channel_id=1, source_target_pairs={{64,0},{65,1},{66,2},{67,3},{68,4},{69,5},{70,6},{71,7},{72,8},{73... | collective-permute-start | bytes 344072 | tf_op jit(solution)/shard_map/ppermute | solution.py:52
  85.0 79.1 %collective-permute-start.22 = (bf16[8,7168]{1,0:T(8,128)(2,1)S(1)}, bf16[8,7168]{1,0:T(8,128)(2,1)S(1)}, u32[]{:S(2)}, u32[]{:S(2)}) collective-permute-start(bf16[8,7168]{1,0:T(8,128)(2,1)S(1)} %get-tuple-element.56), channel_id=1, source_target_pairs={{64,2},{65,3},{66,0},{67,1},{68,6},{69,7},{70,4},{71,5},{72,10},{7... | collective-permute-start | bytes 344072 | tf_op jit(solution)/shard_map/ppermute | solution.py:52
  171.6 20.1 %collective-permute-start.26 = (bf16[8,576]{1,0:T(8,128)(2,1)S(1)}, bf16[8,576]{1,0:T(8,128)(2,1)S(1)}, u32[]{:S(2)}, u32[]{:S(2)}) collective-permute-start(bf16[8,576]{1,0:T(8,128)(2,1)S(1)} %pad_maximum_fusion.4), channel_id=1, source_target_pairs={{0,1},{1,0},{2,3},{3,2},{4,5},{5,4},{6,7},{7,6},{8,9},{9,8},{10,11... | collective-permute-start | bytes 27656 | tf_op jit(solution)/shard_map/ppermute | solution.py:52
  189.7 6.5 %collective-permute-start.23 = (bf16[8,7168]{1,0:T(8,128)(2,1)}, bf16[8,7168]{1,0:T(8,128)(2,1)S(1)}, u32[]{:S(2)}, u32[]{:S(2)}) collective-permute-start(bf16[8,7168]{1,0:T(8,128)(2,1)} %copy-done.4), channel_id=1, source_target_pairs={{0,1},{1,0},{2,3},{3,2},{4,5},{5,4},{6,7},{7,6},{8,9},{9,8},{10,11... | collective-permute-start | bytes 344072 | tf_op jit(solution)/shard_map/ppermute | solution.py:52
  (14 other events, 201.9 us)

commit v2 on v1

--- a/solution.py
+++ b/solution.py
@@ -1,13 +1,15 @@
+import functools
+
 import jax
 import jax.numpy as jnp
 from jax import lax
+from jax.experimental import pallas as pl
+from jax.experimental.pallas import tpu as pltpu
 from jax.sharding import PartitionSpec as P
 
-SIDES = 2
 NX = 4
 NZ = 4
 NY = 2
-NT = 2
 AXES = ("side", "grp", "tp")
 
 NORM_EPS = 1e-06
@@ -15,50 +17,55 @@
 ROPE_BASE = 10000.0
 SCORE_SCALE = 192.0 ** (-0.5)
 WEIGHT_LANES = 128
+CHUNK = 1792
 
 BF16 = jnp.bfloat16
 F32 = jnp.float32
 
 
-def place(side, x, z, y, t):
-    return side * (NX * NZ * NY * NT) + ((x * NZ + z) * NY + y) * NT + t
-
-
-def columns():
-    return [(x, z, y, t) for x in range(NX) for z in range(NZ) for y in range(NY) for t in range(NT)]
-
-
-def cross_pairs(source, flip):
-    return [
-        (place(source, x, z, y, t), place(1 - source, x, z, (y + flip) % NY, t))
-        for x, z, y, t in columns()
+def pairs_of(partner):
+    cells = [
+        (side, x, z, y, t)
+        for side in range(2)
+        for x in range(NX)
+        for z in range(NZ)
+        for y in range(NY)
+        for t in range(2)
     ]
 
-
-def ring_pairs(leg, step):
-    pairs = []
-    for x, z, y, t in columns():
-        along_x = leg == t
-        to = ((x + step) % NX, z) if along_x else (x, (z + step) % NZ)
-        pairs.append((place(1, x, z, y, t), place(1, to[0], to[1], y, t)))
-    return pairs
-
-
-def core_pairs(side):
-    return [(place(side, x, z, y, t), place(side, x, z, y, 1 - t)) for x, z, y, t in columns()]
-
-
-def send(value, pairs):
-    return lax.ppermute(value, AXES, pairs)
+    def place(cell):
+        side, x, z, y, t = cell
+        return (((side * NX + x) * NZ + z) * NY + y) * 2 + t
+
+    return [(place(cell), place(partner(*cell))) for cell in cells]
+
+
+def send(value, partner):
+    return lax.ppermute(value, AXES, pairs_of(partner))
+
+
+def across(flip):
+    return lambda side, x, z, y, t: (1 - side, x, z, y ^ flip, t)
+
+
+def other_core(side, x, z, y, t):
+    return side, x, z, y, 1 - t
+
+
+def ring(leg, flip):
+    def partner(side, x, z, y, t):
+        return (side, x ^ flip, z, y, t) if leg == t else (side, x, z ^ flip, y, t)
+
+    return partner
 
 
 def gather_ring(own, leg):
     half = own.shape[0] // 2
-    before = send(own, ring_pairs(leg, 1))
-    after = send(own, ring_pairs(leg, -1))
-    far_a = send(before[:half], ring_pairs(leg, 1))
-    far_b = send(after[half:], ring_pairs(leg, -1))
-    return jnp.concatenate([own, before, after, far_a, far_b], axis=0)
+    one = send(own, ring(leg, 1))
+    three = send(own, ring(leg, 3))
+    far_a = send(one[:half], ring(leg, 3))
+    far_b = send(three[half:], ring(leg, 1))
+    return own, one, three, far_a, far_b
 
 
 def add(*values):
@@ -68,16 +75,115 @@
     return total.astype(BF16)
 
 
-def scatter_ring(parts, leg):
-    rows = parts.shape[0] // 4
+def scatter_ring(pieces, leg):
+    own, one, three, far_a, far_b = pieces
+    half = own.shape[0] // 2
+    late_a = send(far_a, ring(leg, 3))
+    late_b = send(far_b, ring(leg, 1))
+    one = jnp.concatenate([add(one[:half], late_a), one[half:]], axis=0)
+    three = jnp.concatenate([three[:half], add(three[half:], late_b)], axis=0)
+    return add(own, send(one, ring(leg, 1)), send(three, ring(leg, 3)))
+
+
+def cut(value):
+    rows = value.shape[0] // 4
     half = rows // 2
-    own, before, after = (parts[i * rows : (i + 1) * rows] for i in range(3))
-    far_a, far_b = parts[3 * rows : 3 * rows + half], parts[3 * rows + half :]
-    from_after = send(far_a, ring_pairs(leg, -1))
-    from_before = send(far_b, ring_pairs(leg, 1))
-    before = jnp.concatenate([add(before[:half], from_after), before[half:]], axis=0)
-    after = jnp.concatenate([after[:half], add(after[half:], from_before)], axis=0)
-    return add(own, send(before, ring_pairs(leg, -1)), send(after, ring_pairs(leg, 1)))
+    return (
+        value[:rows],
+        value[rows : 2 * rows],
+        value[2 * rows : 3 * rows],
+        value[3 * rows : 3 * rows + half],
+        value[3 * rows + half :],
+    )
+
+
+def expert_kernel(steps, expert_ref, *refs):
+    pieces, tails = refs[0:5], refs[5:10]
+    gate_a, gate_b, up_a, up_b, down_a, down_b = refs[10:16]
+    outs = refs[16:21]
+    gate_acc, up_acc, hidden, scale = refs[21:25]
+    step = pl.program_id(0)
+    width = gate_a.shape[1]
+
+    def dot(left, right):
+        return jnp.dot(left, right, preferred_element_type=F32)
+
+    @pl.when(step == 0)
+    def _():
+        gate_acc[...] = jnp.zeros_like(gate_acc)
+        up_acc[...] = jnp.zeros_like(up_acc)
+        lanes = jnp.concatenate([tail[...] for tail in tails], axis=0).astype(F32)
+        mine = lax.broadcasted_iota(jnp.int32, lanes.shape, 1) == expert_ref[0]
+        scale[...] = jnp.sum(jnp.where(mine, lanes, 0.0), axis=1, keepdims=True)
+
+    @pl.when(step < steps)
+    def _():
+        rows = jnp.concatenate([piece[...] for piece in pieces], axis=0)
+        gate_acc[:, :width] += dot(rows, gate_a[...])
+        gate_acc[:, width:] += dot(rows, gate_b[...])
+        up_acc[:, :width] += dot(rows, up_a[...])
+        up_acc[:, width:] += dot(rows, up_b[...])
+
+    @pl.when(step == steps - 1)
+    def _():
+        gate = gate_acc[...]
+        hidden[...] = (gate / (1.0 + jnp.exp(-gate)) * up_acc[...]).astype(BF16)
+
+    @pl.when(step >= steps)
+    def _():
+        answer = dot(hidden[:, :width], down_a[...]) + dot(hidden[:, width:], down_b[...])
+        answer = (answer * scale[...]).astype(BF16)
+        at = 0
+        for out in outs:
+            out[...] = answer[at : at + out.shape[0]]
+            at += out.shape[0]
+
+
+def experts(own_expert, pieces, gate_a, gate_b, up_a, up_b, down_a, down_b):
+    model_width, width = gate_a.shape
+    steps = model_width // CHUNK
+    total = sum(piece.shape[0] for piece in pieces)
+
+    def early(step, expert):
+        return jnp.minimum(step, steps - 1)
+
+    def late(step, expert):
+        return jnp.maximum(step - steps, 0)
+
+    piece_specs = [
+        pl.BlockSpec((piece.shape[0], CHUNK), lambda i, e: (0, early(i, e))) for piece in pieces
+    ]
+    tail_specs = [
+        pl.BlockSpec((piece.shape[0], WEIGHT_LANES), lambda i, e: (0, model_width // WEIGHT_LANES))
+        for piece in pieces
+    ]
+    in_specs = [pl.BlockSpec((CHUNK, width), lambda i, e: (early(i, e), 0))] * 4
+    down_specs = [pl.BlockSpec((width, CHUNK), lambda i, e: (0, late(i, e)))] * 2
+    return pl.pallas_call(
+        functools.partial(expert_kernel, steps),
+        out_shape=[jax.ShapeDtypeStruct((piece.shape[0], model_width), BF16) for piece in pieces],
+        grid_spec=pltpu.PrefetchScalarGridSpec(
+            num_scalar_prefetch=1,
+            grid=(2 * steps,),
+            in_specs=piece_specs + tail_specs + in_specs + down_specs,
+            out_specs=[
+                pl.BlockSpec((piece.shape[0], CHUNK), lambda i, e: (0, late(i, e)))
+                for piece in pieces
+            ],
+            scratch_shapes=[
+                pltpu.VMEM((total, 2 * width), F32),
+                pltpu.VMEM((total, 2 * width), F32),
+                pltpu.VMEM((total, 2 * width), BF16),
+                pltpu.VMEM((total, 1), F32),
+            ],
+        ),
+        compiler_params=pltpu.CompilerParams(vmem_limit_bytes=24 * 1024 * 1024),
+        cost_estimate=pl.CostEstimate(
+            flops=12 * total * model_width * width,
+            bytes_accessed=12 * model_width * width + 4 * total * model_width,
+            transcendentals=2 * total * width,
+        ),
+    )(own_expert, *pieces, *pieces, gate_a, gate_b, up_a, up_b, down_a, down_b)
 
 
 def rms_scale(values):
@@ -135,58 +241,43 @@
 ):
     is_attn = lax.axis_index("side") == 0
     tp_index = lax.axis_index("tp")
-    own_expert = lax.axis_index("grp") // NY
+    own_expert = (lax.axis_index("grp") // NY).astype(jnp.int32).reshape(1)
     model_width = residual.shape[2]
     group_rows = residual.shape[1]
-    rows = group_rows // NT
-    experts = router.shape[1]
+    rows = group_rows // 2
     half_width = attn_gain.shape[1]
     latent_width = kv_gain.shape[1]
     heads_here = query_latent.shape[2]
+    barrier = lax.optimization_barrier
 
     def own_rows(value):
         return lax.dynamic_slice_in_dim(value, tp_index * rows, rows, 0)
+
+    gate_other, up_other, down_other = (
+        send(value[0], other_core) for value in (gate_w, up_w, down_w)
+    )
+    kv_other = send(kv_proj[0], other_core)
+    gain_other = send(attn_gain, other_core)
 
     x_rows = own_rows(residual[0]).astype(F32)
     normed = x_rows * rms_scale(x_rows) * moe_gain[0].astype(F32)
     logits = jnp.dot(normed, router[0].astype(F32).T, precision=lax.Precision.HIGHEST)
     scores = jax.nn.sigmoid(logits)
     chosen = own_rows(routes[0])
-    expert_iota = lax.broadcasted_iota(jnp.int32, (1, 1, experts), 2)
+    expert_iota = lax.broadcasted_iota(jnp.int32, (1, 1, router.shape[1]), 2)
     named = jnp.any(chosen[:, :, None] == expert_iota, axis=1)
     picked = jnp.where(named, scores, 0.0)
     weight = (ROUTE_SCALE * picked / jnp.sum(picked, axis=1, keepdims=True)).astype(BF16)
     outgoing = jnp.concatenate(
-        [normed.astype(BF16), jnp.pad(weight, ((0, 0), (0, WEIGHT_LANES - experts)))], axis=1
-    )
-
-    gate_other, up_other, down_other = (
-        send(value[0], core_pairs(1)) for value in (gate_w, up_w, down_w)
-    )
-    kv_other = send(kv_proj[0], core_pairs(0))
-    gain_other = send(attn_gain, core_pairs(0))
-
-    arrived = jnp.concatenate(
-        [send(outgoing, cross_pairs(0, 0)), send(outgoing, cross_pairs(0, 1))], axis=0
-    )
-    everything = gather_ring(gather_ring(arrived, 0), 1)
-    flat = everything[:, :model_width]
-    all_weights = everything[:, model_width : model_width + experts].astype(F32)
-    mine = lax.broadcasted_iota(jnp.int32, (1, experts), 1) == own_expert
-    row_weight = jnp.sum(jnp.where(mine, all_weights, 0.0), axis=1, keepdims=True)
-
-    def hidden_of(gate_part, up_part):
-        gate_val = jnp.dot(flat, gate_part, preferred_element_type=F32)
-        up_val = jnp.dot(flat, up_part, preferred_element_type=F32)
-        return (jax.nn.silu(gate_val) * up_val).astype(BF16)
-
-    answer = jnp.dot(hidden_of(gate_w[0], up_w[0]), down_w[0], preferred_element_type=F32) + jnp.dot(
-        hidden_of(gate_other, up_other), down_other, preferred_element_type=F32
-    )
-    answer = (answer * row_weight).astype(BF16)
-    answer = scatter_ring(scatter_ring(answer, 1), 0)
-    back_same = send(answer[:rows], cross_pairs(1, 0))
-    back_flip = send(answer[rows:], cross_pairs(1, 1))
+        [normed.astype(BF16), jnp.pad(weight, ((0, 0), (0, WEIGHT_LANES - weight.shape[1])))],
+        axis=1,
+    )
+
+    arrived = jnp.concatenate([send(outgoing, across(0)), send(outgoing, across(1))], axis=0)
+    arrived, gate_other, up_other = barrier((arrived, gate_other, up_other))
+    column = jnp.concatenate(gather_ring(arrived, 0), axis=0)
+    column, down_other, kv_other, gain_other = barrier((column, down_other, kv_other, gain_other))
+    pieces = gather_ring(column, 1)
 
     operands = (
         query_latent[0],
@@ -196,18 +287,34 @@
         lengths[0],
     )
 
-    def skip_attention(unused):
-        return (
+    def attention_role(operands, pieces, weights):
+        return attend_cache(operands), tuple(
+            jnp.zeros((piece.shape[0], model_width), BF16) for piece in pieces
+        )
+
+    def expert_role(operands, pieces, weights):
+        idle = (
             jnp.zeros((group_rows, heads_here, latent_width), F32),
             jnp.zeros((group_rows, heads_here), F32),
             jnp.ones((group_rows, heads_here), F32),
         )
-
-    mixed, peak, mass = lax.cond(is_attn, attend_cache, skip_attention, operands)
+        return idle, tuple(experts(own_expert, pieces, *weights))
+
+    (mixed, peak, mass), answers = lax.cond(
+        is_attn,
+        attention_role,
+        expert_role,
+        operands,
+        pieces,
+        (gate_w[0], gate_other, up_w[0], up_other, down_w[0], down_other),
+    )
+    answer = scatter_ring(cut(scatter_ring(answers, 1)), 0)
+    back_same = send(answer[:rows], across(0))
+    back_flip = send(answer[rows:], across(1))
 
     moe_total = back_same.astype(F32) + back_flip.astype(F32)
     updated = (x_rows + moe_total).astype(BF16)
-    updated_other = send(updated, core_pairs(0))
+    updated_other = send(updated, other_core)
     updated_f = updated.astype(F32)
 
     def project(start, gain_part, proj_part):
@@ -225,7 +332,7 @@
     fresh_lat = (latent * rms_scale(latent) * kv_gain[0].astype(F32)).astype(BF16)
     fresh_rot = rotate(kv_raw[:, latent_width:], own_rows(lengths[0])).astype(BF16)
     fresh = jnp.concatenate([fresh_lat, fresh_rot], axis=1)
-    fresh_other = send(fresh, core_pairs(0))
+    fresh_other = send(fresh, other_core)
 
     def both(own, other):
         first = tp_index == 0

time: 199 us -> 138 us (0.69)
  matrix products: 45 us -> 11 us
  waiting for transfers between devices: 81.3 us -> 59.9 us
  local copies, waits for them, and re-layouts: 10.8 us -> 6.08 us
  other arithmetic: 12.7 us -> 9.8 us
  starting transfers between devices: 46.7 us -> 49.3 us
    dot_general x4 -> x0, matrix products: 31.9 us -> none  [the longest x1 12.2 us: body(): jnp.dot(hidden_of(gate_other, up_other), down_other, preferred_element_ty...]
    ppermute x27, waiting for transfers between devices: 81.3 us -> 59.9 us  [send(): return lax.ppermute(value, AXES, pairs_of(partner))]
    unnamed x31, local copies, waits for them, and re-layouts: 6.53 us -> 3.13 us
    ppermute x27, starting transfers between devices: 46.7 us -> 49.3 us  [send(): return lax.ppermute(value, AXES, pairs_of(partner))]
    dot_general x2, matrix products: 6.85 us -> 4.69 us  [project(): lax.dot_general(scaled, proj_part, (((1,), (1,)), ((), ())), preferred_el...]
  transfers between devices with their start and end apart: 27 -> 27, of which waited for: 5 -> 17; matrix products, arithmetic and copies ran while one was open for 21% -> 8% of each run, Pallas kernels for 0% -> 0%
where the time goes in v2:
time: 138 us; the launch traced here: 137 us
  waiting for transfers between devices  59.9 us (43%)
  starting transfers between devices  49.3 us (36%)
  matrix products  11 us (8%)
  other arithmetic  9.8 us (7%)
  local copies, waits for them, and re-layouts  6.08 us (4%)
    ppermute x27, waiting for transfers between devices, send(): return lax.ppermute(value, AXES, pairs_of(partner))  59.9 us
    ppermute x27, starting transfers between devices, send(): return lax.ppermute(value, AXES, pairs_of(partner))  49.3 us
    dot_general x2, matrix products, project(): lax.dot_general(scaled, proj_part, (((1,), (1,)), ((), ())), preferred_el...  4.69 us
    unnamed x31, local copies, waits for them, and re-layouts  3.13 us
  transfers between devices with their start and end apart: 27, of which 17 were waited for; matrix products, arithmetic and copies ran while one was open for 8% of the time, Pallas kernels for 0%

profile of v2, /device:TPU:1, one launch (start us, length us, event | category | flops | bytes accessed | tf_op | source)
XLA Modules:
  0.0 137.1 jit_solution(6299084211243827086)
XLA Ops:
  7.6 3.1 %collective-permute-start = (bf16[8,7296]{1,0:T(8,128)(2,1)S(1)}, bf16[8,7296]{1,0:T(8,128)(2,1)S(1)}, u32[]{:S(2)}, u32[]{:S(2)}) collective-permute-start(bf16[8,7296]{1,0:T(8,128)(2,1)S(1)} %fusion.41), channel_id=1, source_target_pairs={{0,64},{1,65},{2,66},{3,67},{4,68},{5,69},{6,70},{7,71},{8,72},{9,... | collective-permute-start | bytes 350216 | tf_op jit(solution)/shard_map/ppermute | solution.py:44
  17.6 1.7 %collective-permute-start.4 = (bf16[16,7296]{1,0:T(8,128)(2,1)S(1)}, bf16[16,7296]{1,0:T(8,128)(2,1)S(1)}, u32[]{:S(2)}, u32[]{:S(2)}) collective-permute-start(bf16[16,7296]{1,0:T(8,128)(2,1)S(1)} %pad_maximum_fusion.2), channel_id=1, source_target_pairs={{0,16},{1,5},{2,18},{3,7},{4,20},{5,1},{6,22},{7,3},{8,24},{9,13},... | collective-permute-start | bytes 700424 | tf_op jit(solution)/shard_map/ppermute | solution.py:44
  19.3 2.2 %collective-permute-start.5 = (bf16[16,7296]{1,0:T(8,128)(2,1)S(1)}, bf16[16,7296]{1,0:T(8,128)(2,1)S(1)}, u32[]{:S(2)}, u32[]{:S(2)}) collective-permute-start(bf16[16,7296]{1,0:T(8,128)(2,1)S(1)} %pad_maximum_fusion.2), channel_id=1, source_target_pairs={{0,48},{1,13},{2,50},{3,15},{4,52},{5,9},{6,54},{7,11},{8,56},{9,5... | collective-permute-start | bytes 700424 | tf_op jit(solution)/shard_map/ppermute | solution.py:44
  23.1 3.7 %collective-permute-start.6 = (bf16[8,7296]{1,0:T(8,128)(2,1)S(1)}, bf16[8,7296]{1,0:T(8,128)(2,1)S(1)}, u32[]{:S(2)}, u32[]{:S(2)}) collective-permute-start(bf16[8,7296]{1,0:T(8,128)(2,1)S(1)} %slice.97), channel_id=1, source_target_pairs={{0,48},{1,13},{2,50},{3,15},{4,52},{5,9},{6,54},{7,11},{8,56},{9,5... | collective-permute-start | bytes 350216 | tf_op jit(solution)/shard_map/ppermute | solution.py:44
  26.9 2.3 %collective-permute-done.6 = bf16[8,7296]{1,0:T(8,128)(2,1)S(1)} collective-permute-done((bf16[8,7296]{1,0:T(8,128)(2,1)S(1)}, bf16[8,7296]{1,0:T(8,128)(2,1)S(1)}, u32[]{:S(2)}, u32[]{:S(2)}) %collective-permute-start.6) | collective-permute-done | bytes 116768 | tf_op jit(solution)/shard_map/ppermute | solution.py:44
  29.2 1.5 %collective-permute-done.7 = bf16[8,7296]{1,0:T(8,128)(2,1)S(1)} collective-permute-done((bf16[8,7296]{1,0:T(8,128)(2,1)S(1)}, bf16[8,7296]{1,0:T(8,128)(2,1)S(1)}, u32[]{:S(2)}, u32[]{:S(2)}) %collective-permute-start.7) | collective-permute-done | bytes 116768 | tf_op jit(solution)/shard_map/ppermute | solution.py:44
  30.8 2.0 %copy-done.4 = bf16[576,3584]{1,0:T(8,128)(2,1)} copy-done((bf16[576,3584]{1,0:T(8,128)(2,1)}, bf16[576,3584]{1,0:T(8,128)(2,1)S(1)}, u32[]{:S(2)}) %copy-start.4) | copy-done | bytes 4128792
  33.7 1.8 %collective-permute-start.12 = (bf16[64,7296]{1,0:T(8,128)(2,1)S(1)}, bf16[64,7296]{1,0:T(8,128)(2,1)S(1)}, u32[]{:S(2)}, u32[]{:S(2)}) collective-permute-start(bf16[64,7296]{1,0:T(8,128)(2,1)S(1)} %constant_dynamic-update-slice_fusion), channel_id=1, source_target_pairs={{0,12},{1,49},{2,14},{3,51},{4,8},{5,53},{6,10},{7,55},{8,4},{9,57... | collective-permute-start | bytes 2801672 | tf_op jit(solution)/shard_map/ppermute | solution.py:44
  35.6 10.0 %collective-permute-done.11 = bf16[64,7296]{1,0:T(8,128)(2,1)S(1)} collective-permute-done((bf16[64,7296]{1,0:T(8,128)(2,1)S(1)}, bf16[64,7296]{1,0:T(8,128)(2,1)S(1)}, u32[]{:S(2)}, u32[]{:S(2)}) %collective-permute-start.11) | collective-permute-done | bytes 933920 | tf_op jit(solution)/shard_map/ppermute | solution.py:44
  46.3 2.2 %collective-permute-start.13 = (bf16[32,7296]{1,0:T(8,128)(2,1)}, bf16[32,7296]{1,0:T(8,128)(2,1)}, u32[]{:S(2)}, u32[]{:S(2)}) collective-permute-start(bf16[32,7296]{1,0:T(8,128)(2,1)} %slice.99), channel_id=1, source_target_pairs={{0,12},{1,49},{2,14},{3,51},{4,8},{5,53},{6,10},{7,55},{8,4},{9,57... | collective-permute-start | bytes 1400840 | tf_op jit(solution)/shard_map/ppermute | solution.py:44
  50.5 5.1 %collective-permute-done.13 = bf16[32,7296]{1,0:T(8,128)(2,1)} collective-permute-done((bf16[32,7296]{1,0:T(8,128)(2,1)}, bf16[32,7296]{1,0:T(8,128)(2,1)}, u32[]{:S(2)}, u32[]{:S(2)}) %collective-permute-start.13) | collective-permute-done | bytes 466976 | tf_op jit(solution)/shard_map/ppermute | solution.py:44
  55.6 2.7 %collective-permute-done.14 = bf16[32,7296]{1,0:T(8,128)(2,1)} collective-permute-done((bf16[32,7296]{1,0:T(8,128)(2,1)}, bf16[32,7296]{1,0:T(8,128)(2,1)}, u32[]{:S(2)}, u32[]{:S(2)}) %collective-permute-start.14) | collective-permute-done | bytes 466976 | tf_op jit(solution)/shard_map/ppermute | solution.py:44
  58.3 6.1 %conditional.1 = (f32[16,32,512]{2,1,0:T(8,128)S(1)}, f32[16,32]{1,0:T(8,128)}, f32[16,32]{1,0:T(8,128)S(1)}, bf16[64,7168]{1,0:T(8,128)(2,1)S(1)}, bf16[64,7168...) conditional(s32[]{:T(128)} %convert_element_type.160, ...), branch_computations={%region_3.4_spmd, %region_4.7_spmd} | conditional | flops 5637144576 | bytes 30413026 | solution.py:303
  59.5 2.5 %fusion.73 = (f32[16,32]{1,0:T(8,128)}, f32[16,32,128]{2,1,0:T(8,128)S(1)}) fusion(f32[16,32,128]{2,1,0:T(8,128)S(1)} %fusion.13, bf16[16,32,512]{2,1,0:T(8,128)(2,1)} %get-tuple-element.142, bf16[1,16,128,512]{3,2,1,0:T(8,128)(2,1)S(1)} %get-tuple-element.184, s32[16]{0:T(128)S(1)} %bitcast.83), kind=kOutput, calls=%fused_computation.122 | convolution fusion | flops 67436032 | bytes 3147840 | tf_op jit(solution)/shard_map/cond/branch_1_fun/thl,tpl->thp/dot_general | solution.py:214
  65.7 7.7 %collective-permute-done.15 = bf16[32,7168]{1,0:T(8,128)(2,1)S(1)} collective-permute-done((bf16[32,7168]{1,0:T(8,128)(2,1)S(1)}, bf16[32,7168]{1,0:T(8,128)(2,1)S(1)}, u32[]{:S(2)}, u32[]{:S(2)}) %collective-permute-start.15) | collective-permute-done | bytes 458784 | tf_op jit(solution)/shard_map/ppermute | solution.py:44
  75.2 11.0 %collective-permute-done.16 = bf16[64,7168]{1,0:T(8,128)(2,1)S(1)} collective-permute-done((bf16[64,7168]{1,0:T(8,128)(2,1)S(1)}, bf16[64,7168]{1,0:T(8,128)(2,1)S(1)}, u32[]{:S(2)}, u32[]{:S(2)}) %collective-permute-start.16) | collective-permute-done | bytes 917536 | tf_op jit(solution)/shard_map/ppermute | solution.py:44
  88.1 1.6 %collective-permute-start.19 = (bf16[8,7168]{1,0:T(8,128)(2,1)S(1)}, bf16[8,7168]{1,0:T(8,128)(2,1)S(1)}, u32[]{:S(2)}, u32[]{:S(2)}) collective-permute-start(bf16[8,7168]{1,0:T(8,128)(2,1)S(1)} %get-tuple-element.194), channel_id=1, source_target_pairs={{0,48},{1,13},{2,50},{3,15},{4,52},{5,9},{6,54},{7,11},{8,56},{9,5... | collective-permute-start | bytes 344072 | tf_op jit(solution)/shard_map/ppermute | solution.py:44
  89.7 4.7 %collective-permute-done.19 = bf16[8,7168]{1,0:T(8,128)(2,1)S(1)} collective-permute-done((bf16[8,7168]{1,0:T(8,128)(2,1)S(1)}, bf16[8,7168]{1,0:T(8,128)(2,1)S(1)}, u32[]{:S(2)}, u32[]{:S(2)}) %collective-permute-start.19) | collective-permute-done | bytes 114720 | tf_op jit(solution)/shard_map/ppermute | solution.py:44
  94.6 1.7 %collective-permute-start.22 = (bf16[16,7168]{1,0:T(8,128)(2,1)S(1)}, bf16[16,7168]{1,0:T(8,128)(2,1)S(1)}, u32[]{:S(2)}, u32[]{:S(2)}) collective-permute-start(bf16[16,7168]{1,0:T(8,128)(2,1)S(1)} %pad_maximum_fusion.4), channel_id=1, source_target_pairs={{0,48},{1,13},{2,50},{3,15},{4,52},{5,9},{6,54},{7,11},{8,56},{9,5... | collective-permute-start | bytes 688136 | tf_op jit(solution)/shard_map/ppermute | solution.py:44
  96.4 3.3 %collective-permute-done.20 = bf16[16,7168]{1,0:T(8,128)(2,1)S(1)} collective-permute-done((bf16[16,7168]{1,0:T(8,128)(2,1)S(1)}, bf16[16,7168]{1,0:T(8,128)(2,1)S(1)}, u32[]{:S(2)}, u32[]{:S(2)}) %collective-permute-start.20) | collective-permute-done | bytes 229408 | tf_op jit(solution)/shard_map/ppermute | solution.py:44
  101.0 10.8 %collective-permute-start.23 = (bf16[8,7168]{1,0:T(8,128)(2,1)S(1)}, bf16[8,7168]{1,0:T(8,128)(2,1)S(1)}, u32[]{:S(2)}, u32[]{:S(2)}) collective-permute-start(bf16[8,7168]{1,0:T(8,128)(2,1)S(1)} %get-tuple-element.200), channel_id=1, source_target_pairs={{0,64},{1,65},{2,66},{3,67},{4,68},{5,69},{6,70},{7,71},{8,72},{9,... | collective-permute-start | bytes 344072 | tf_op jit(solution)/shard_map/ppermute | solution.py:44
  114.0 2.7 %collective-permute-done.24 = bf16[8,7168]{1,0:T(8,128)(2,1)S(1)} collective-permute-done((bf16[8,7168]{1,0:T(8,128)(2,1)S(1)}, bf16[8,7168]{1,0:T(8,128)(2,1)S(1)}, u32[]{:S(2)}, u32[]{:S(2)}) %collective-permute-start.24) | collective-permute-done | bytes 114720 | tf_op jit(solution)/shard_map/ppermute | solution.py:44
  116.8 3.5 %fusion.45 = f32[8,576]{1,0:T(8,128)S(1)} fusion(f32[3584]{0:T(1024)S(1)} %convert_reduce_fusion.1, bf16[8,7168]{1,0:T(8,128)(2,1)S(1)} %get-tuple-element.189, s32[]{:T(128)S(6)} %select_n.102, bf16[1,576,3584]{2,1,0:T(8,128)(2,1)} %param.25), kind=kOutput, calls=%fused_computation.64 | convolution fusion | flops 33116160 | bytes 4220932 | tf_op jit(solution)/shard_map/dot_general | solution.py:323
  121.9 10.2 %collective-permute-start.26 = (bf16[8,576]{1,0:T(8,128)(2,1)S(1)}, bf16[8,576]{1,0:T(8,128)(2,1)S(1)}, u32[]{:S(2)}, u32[]{:S(2)}) collective-permute-start(bf16[8,576]{1,0:T(8,128)(2,1)S(1)} %pad_maximum_fusion.5), channel_id=1, source_target_pairs={{0,1},{1,0},{2,3},{3,2},{4,5},{5,4},{6,7},{7,6},{8,9},{9,8},{10,11... | collective-permute-start | bytes 27656 | tf_op jit(solution)/shard_map/ppermute | solution.py:44
  (124 shorter events, 38.0 us)
Async XLA Ops:
  0.6 16.9 %collective-permute-start.2 = (bf16[7168,256]{1,0:T(8,128)(2,1)}, bf16[7168,256]{1,0:T(8,128)(2,1)}, u32[]{:S(2)}, u32[]{:S(2)}) collective-permute-start(bf16[7168,256]{1,0:T(8,128)(2,1)} %bitcast.72), channel_id=1, source_target_pairs={{0,1},{1,0},{2,3},{3,2},{4,5},{5,4},{6,7},{7,6},{8,9},{9,8},{10,11... | collective-permute-start | bytes 11010056 | tf_op jit(solution)/shard_map/ppermute | solution.py:44
  2.1 15.4 %collective-permute-start.3 = (bf16[7168,256]{1,0:T(8,128)(2,1)}, bf16[7168,256]{1,0:T(8,128)(2,1)}, u32[]{:S(2)}, u32[]{:S(2)}) collective-permute-start(bf16[7168,256]{1,0:T(8,128)(2,1)} %bitcast.74), channel_id=1, source_target_pairs={{0,1},{1,0},{2,3},{3,2},{4,5},{5,4},{6,7},{7,6},{8,9},{9,8},{10,11... | collective-permute-start | bytes 11010056 | tf_op jit(solution)/shard_map/ppermute | solution.py:44
  7.6 6.0 %collective-permute-start = (bf16[8,7296]{1,0:T(8,128)(2,1)S(1)}, bf16[8,7296]{1,0:T(8,128)(2,1)S(1)}, u32[]{:S(2)}, u32[]{:S(2)}) collective-permute-start(bf16[8,7296]{1,0:T(8,128)(2,1)S(1)} %fusion.41), channel_id=1, source_target_pairs={{0,64},{1,65},{2,66},{3,67},{4,68},{5,69},{6,70},{7,71},{8,72},{9,... | collective-permute-start | bytes 350216 | tf_op jit(solution)/shard_map/ppermute | solution.py:44
  10.7 5.5 %collective-permute-start.1 = (bf16[8,7296]{1,0:T(8,128)(2,1)S(1)}, bf16[8,7296]{1,0:T(8,128)(2,1)S(1)}, u32[]{:S(2)}, u32[]{:S(2)}) collective-permute-start(bf16[8,7296]{1,0:T(8,128)(2,1)S(1)} %fusion.41), channel_id=1, source_target_pairs={{0,66},{1,67},{2,64},{3,65},{4,70},{5,71},{6,68},{7,69},{8,74},{9,... | collective-permute-start | bytes 350216 | tf_op jit(solution)/shard_map/ppermute | solution.py:44
  11.4 19.4 %collective-permute-start.8 = (bf16[256,7168]{1,0:T(8,128)(2,1)}, bf16[256,7168]{1,0:T(8,128)(2,1)S(1)}, u32[]{:S(2)}, u32[]{:S(2)}) collective-permute-start(bf16[256,7168]{1,0:T(8,128)(2,1)} %bitcast.76), channel_id=1, source_target_pairs={{0,1},{1,0},{2,3},{3,2},{4,5},{5,4},{6,7},{7,6},{8,9},{9,8},{10,11... | collective-permute-start | bytes 11010056 | tf_op jit(solution)/shard_map/ppermute | solution.py:44
  13.6 17.2 %collective-permute-start.9 = (bf16[576,3584]{1,0:T(8,128)(2,1)}, bf16[576,3584]{1,0:T(8,128)(2,1)S(1)}, u32[]{:S(2)}, u32[]{:S(2)}) collective-permute-start(bf16[576,3584]{1,0:T(8,128)(2,1)} %bitcast.71), channel_id=1, source_target_pairs={{0,1},{1,0},{2,3},{3,2},{4,5},{5,4},{6,7},{7,6},{8,9},{9,8},{10,11... | collective-permute-start | bytes 12386312 | tf_op jit(solution)/shard_map/ppermute | solution.py:44
  16.2 14.6 %collective-permute-start.10 = (bf16[1,3584]{1,0:T(2,128)(2,1)}, bf16[1,3584]{1,0:T(2,128)(2,1)S(1)}, u32[]{:S(2)}, u32[]{:S(2)}) collective-permute-start(bf16[1,3584]{1,0:T(2,128)(2,1)} %param.24), channel_id=1, source_target_pairs={{0,1},{1,0},{2,3},{3,2},{4,5},{5,4},{6,7},{7,6},{8,9},{9,8},{10,11... | collective-permute-start | bytes 21512 | tf_op jit(solution)/shard_map/ppermute | solution.py:44
  17.6 5.5 %collective-permute-start.4 = (bf16[16,7296]{1,0:T(8,128)(2,1)S(1)}, bf16[16,7296]{1,0:T(8,128)(2,1)S(1)}, u32[]{:S(2)}, u32[]{:S(2)}) collective-permute-start(bf16[16,7296]{1,0:T(8,128)(2,1)S(1)} %pad_maximum_fusion.2), channel_id=1, source_target_pairs={{0,16},{1,5},{2,18},{3,7},{4,20},{5,1},{6,22},{7,3},{8,24},{9,13},... | collective-permute-start | bytes 700424 | tf_op jit(solution)/shard_map/ppermute | solution.py:44
  19.3 7.4 %collective-permute-start.5 = (bf16[16,7296]{1,0:T(8,128)(2,1)S(1)}, bf16[16,7296]{1,0:T(8,128)(2,1)S(1)}, u32[]{:S(2)}, u32[]{:S(2)}) collective-permute-start(bf16[16,7296]{1,0:T(8,128)(2,1)S(1)} %pad_maximum_fusion.2), channel_id=1, source_target_pairs={{0,48},{1,13},{2,50},{3,15},{4,52},{5,9},{6,54},{7,11},{8,56},{9,5... | collective-permute-start | bytes 700424 | tf_op jit(solution)/shard_map/ppermute | solution.py:44
  23.1 6.2 %collective-permute-start.6 = (bf16[8,7296]{1,0:T(8,128)(2,1)S(1)}, bf16[8,7296]{1,0:T(8,128)(2,1)S(1)}, u32[]{:S(2)}, u32[]{:S(2)}) collective-permute-start(bf16[8,7296]{1,0:T(8,128)(2,1)S(1)} %slice.97), channel_id=1, source_target_pairs={{0,48},{1,13},{2,50},{3,15},{4,52},{5,9},{6,54},{7,11},{8,56},{9,5... | collective-permute-start | bytes 350216 | tf_op jit(solution)/shard_map/ppermute | solution.py:44
  32.8 12.7 %collective-permute-start.11 = (bf16[64,7296]{1,0:T(8,128)(2,1)S(1)}, bf16[64,7296]{1,0:T(8,128)(2,1)S(1)}, u32[]{:S(2)}, u32[]{:S(2)}) collective-permute-start(bf16[64,7296]{1,0:T(8,128)(2,1)S(1)} %constant_dynamic-update-slice_fusion), channel_id=1, source_target_pairs={{0,4},{1,17},{2,6},{3,19},{4,0},{5,21},{6,2},{7,23},{8,12},{9,25},... | collective-permute-start | bytes 2801672 | tf_op jit(solution)/shard_map/ppermute | solution.py:44
  33.7 14.8 %collective-permute-start.12 = (bf16[64,7296]{1,0:T(8,128)(2,1)S(1)}, bf16[64,7296]{1,0:T(8,128)(2,1)S(1)}, u32[]{:S(2)}, u32[]{:S(2)}) collective-permute-start(bf16[64,7296]{1,0:T(8,128)(2,1)S(1)} %constant_dynamic-update-slice_fusion), channel_id=1, source_target_pairs={{0,12},{1,49},{2,14},{3,51},{4,8},{5,53},{6,10},{7,55},{8,4},{9,57... | collective-permute-start | bytes 2801672 | tf_op jit(solution)/shard_map/ppermute | solution.py:44
  46.3 9.2 %collective-permute-start.13 = (bf16[32,7296]{1,0:T(8,128)(2,1)}, bf16[32,7296]{1,0:T(8,128)(2,1)}, u32[]{:S(2)}, u32[]{:S(2)}) collective-permute-start(bf16[32,7296]{1,0:T(8,128)(2,1)} %slice.99), channel_id=1, source_target_pairs={{0,12},{1,49},{2,14},{3,51},{4,8},{5,53},{6,10},{7,55},{8,4},{9,57... | collective-permute-start | bytes 1400840 | tf_op jit(solution)/shard_map/ppermute | solution.py:44
  50.3 8.0 %collective-permute-start.14 = (bf16[32,7296]{1,0:T(8,128)(2,1)}, bf16[32,7296]{1,0:T(8,128)(2,1)}, u32[]{:S(2)}, u32[]{:S(2)}) collective-permute-start(bf16[32,7296]{1,0:T(8,128)(2,1)} %slice.100), channel_id=1, source_target_pairs={{0,4},{1,17},{2,6},{3,19},{4,0},{5,21},{6,2},{7,23},{8,12},{9,25},... | collective-permute-start | bytes 1400840 | tf_op jit(solution)/shard_map/ppermute | solution.py:44
  64.5 8.9 %collective-permute-start.15 = (bf16[32,7168]{1,0:T(8,128)(2,1)S(1)}, bf16[32,7168]{1,0:T(8,128)(2,1)S(1)}, u32[]{:S(2)}, u32[]{:S(2)}) collective-permute-start(bf16[32,7168]{1,0:T(8,128)(2,1)S(1)} %get-tuple-element.172), channel_id=1, source_target_pairs={{0,12},{1,49},{2,14},{3,51},{4,8},{5,53},{6,10},{7,55},{8,4},{9,57... | collective-permute-start | bytes 1376264 | tf_op jit(solution)/shard_map/ppermute | solution.py:44
  65.5 8.1 %collective-permute-start.17 = (bf16[32,7168]{1,0:T(8,128)(2,1)S(1)}, bf16[32,7168]{1,0:T(8,128)(2,1)S(1)}, u32[]{:S(2)}, u32[]{:S(2)}) collective-permute-start(bf16[32,7168]{1,0:T(8,128)(2,1)S(1)} %get-tuple-element.174), channel_id=1, source_target_pairs={{0,4},{1,17},{2,6},{3,19},{4,0},{5,21},{6,2},{7,23},{8,12},{9,25},... | collective-permute-start | bytes 1376264 | tf_op jit(solution)/shard_map/ppermute | solution.py:44
  73.6 12.6 %collective-permute-start.16 = (bf16[64,7168]{1,0:T(8,128)(2,1)S(1)}, bf16[64,7168]{1,0:T(8,128)(2,1)S(1)}, u32[]{:S(2)}, u32[]{:S(2)}) collective-permute-start(bf16[64,7168]{1,0:T(8,128)(2,1)S(1)} %pad_maximum_fusion), channel_id=1, source_target_pairs={{0,4},{1,17},{2,6},{3,19},{4,0},{5,21},{6,2},{7,23},{8,12},{9,25},... | collective-permute-start | bytes 2752520 | tf_op jit(solution)/shard_map/ppermute | solution.py:44
  73.9 13.8 %collective-permute-start.18 = (bf16[64,7168]{1,0:T(8,128)(2,1)S(1)}, bf16[64,7168]{1,0:T(8,128)(2,1)S(1)}, u32[]{:S(2)}, u32[]{:S(2)}) collective-permute-start(bf16[64,7168]{1,0:T(8,128)(2,1)S(1)} %pad_maximum_fusion.1), channel_id=1, source_target_pairs={{0,12},{1,49},{2,14},{3,51},{4,8},{5,53},{6,10},{7,55},{8,4},{9,57... | collective-permute-start | bytes 2752520 | tf_op jit(solution)/shard_map/ppermute | solution.py:44
  88.1 6.3 %collective-permute-start.19 = (bf16[8,7168]{1,0:T(8,128)(2,1)S(1)}, bf16[8,7168]{1,0:T(8,128)(2,1)S(1)}, u32[]{:S(2)}, u32[]{:S(2)}) collective-permute-start(bf16[8,7168]{1,0:T(8,128)(2,1)S(1)} %get-tuple-element.194), channel_id=1, source_target_pairs={{0,48},{1,13},{2,50},{3,15},{4,52},{5,9},{6,54},{7,11},{8,56},{9,5... | collective-permute-start | bytes 344072 | tf_op jit(solution)/shard_map/ppermute | solution.py:44
  94.5 5.2 %collective-permute-start.20 = (bf16[16,7168]{1,0:T(8,128)(2,1)S(1)}, bf16[16,7168]{1,0:T(8,128)(2,1)S(1)}, u32[]{:S(2)}, u32[]{:S(2)}) collective-permute-start(bf16[16,7168]{1,0:T(8,128)(2,1)S(1)} %pad_maximum_fusion.3), channel_id=1, source_target_pairs={{0,16},{1,5},{2,18},{3,7},{4,20},{5,1},{6,22},{7,3},{8,24},{9,13},... | collective-permute-start | bytes 688136 | tf_op jit(solution)/shard_map/ppermute | solution.py:44
  94.6 6.3 %collective-permute-start.22 = (bf16[16,7168]{1,0:T(8,128)(2,1)S(1)}, bf16[16,7168]{1,0:T(8,128)(2,1)S(1)}, u32[]{:S(2)}, u32[]{:S(2)}) collective-permute-start(bf16[16,7168]{1,0:T(8,128)(2,1)S(1)} %pad_maximum_fusion.4), channel_id=1, source_target_pairs={{0,48},{1,13},{2,50},{3,15},{4,52},{5,9},{6,54},{7,11},{8,56},{9,5... | collective-permute-start | bytes 688136 | tf_op jit(solution)/shard_map/ppermute | solution.py:44
  101.0 12.9 %collective-permute-start.23 = (bf16[8,7168]{1,0:T(8,128)(2,1)S(1)}, bf16[8,7168]{1,0:T(8,128)(2,1)S(1)}, u32[]{:S(2)}, u32[]{:S(2)}) collective-permute-start(bf16[8,7168]{1,0:T(8,128)(2,1)S(1)} %get-tuple-element.200), channel_id=1, source_target_pairs={{0,64},{1,65},{2,66},{3,67},{4,68},{5,69},{6,70},{7,71},{8,72},{9,... | collective-permute-start | bytes 344072 | tf_op jit(solution)/shard_map/ppermute | solution.py:44
  111.8 4.9 %collective-permute-start.24 = (bf16[8,7168]{1,0:T(8,128)(2,1)S(1)}, bf16[8,7168]{1,0:T(8,128)(2,1)S(1)}, u32[]{:S(2)}, u32[]{:S(2)}) collective-permute-start(bf16[8,7168]{1,0:T(8,128)(2,1)S(1)} %get-tuple-element.201), channel_id=1, source_target_pairs={{0,66},{1,67},{2,64},{3,65},{4,70},{5,71},{6,68},{7,69},{8,74},{9,... | collective-permute-start | bytes 344072 | tf_op jit(solution)/shard_map/ppermute | solution.py:44
  121.9 11.0 %collective-permute-start.26 = (bf16[8,576]{1,0:T(8,128)(2,1)S(1)}, bf16[8,576]{1,0:T(8,128)(2,1)S(1)}, u32[]{:S(2)}, u32[]{:S(2)}) collective-permute-start(bf16[8,576]{1,0:T(8,128)(2,1)S(1)} %pad_maximum_fusion.5), channel_id=1, source_target_pairs={{0,1},{1,0},{2,3},{3,2},{4,5},{5,4},{6,7},{7,6},{8,9},{9,8},{10,11... | collective-permute-start | bytes 27656 | tf_op jit(solution)/shard_map/ppermute | solution.py:44
  (16 other events, 252.0 us)

commit v3 on v1

v3 whole, which is shorter than its diff:
```python
import functools

import jax
import jax.numpy as jnp
from jax import lax
from jax.experimental import pallas as pl
from jax.experimental.pallas import tpu as pltpu
from jax.sharding import PartitionSpec as P

NX = 4
NZ = 4
NY = 2
AXES = ("side", "grp", "tp")

NORM_EPS = 1e-06
ROUTE_SCALE = 2.5
ROPE_BASE = 10000.0
SCORE_SCALE = 192.0 ** (-0.5)
WEIGHT_LANES = 128
CHUNK = 1792
KERNEL_VMEM = 16 * 1024 * 1024
ROLES_VMEM = 16 * 1024 * 1024
STAGE_VMEM = 1024 * 1024

BF16 = jnp.bfloat16
F32 = jnp.float32


def pairs_of(partner):
    cells = [
        (side, x, z, y, t)
        for side in range(2)
        for x in range(NX)
        for z in range(NZ)
        for y in range(NY)
        for t in range(2)
    ]

    def place(cell):
        side, x, z, y, t = cell
        return (((side * NX + x) * NZ + z) * NY + y) * 2 + t

    return [(place(cell), place(partner(*cell))) for cell in cells]


def send(value, partner):
    return lax.ppermute(value, AXES, pairs_of(partner))


def across(flip):
    return lambda side, x, z, y, t: (1 - side, x, z, y ^ flip, t)


def other_core(side, x, z, y, t):
    return side, x, z, y, 1 - t


def ring(leg, flip):
    def partner(side, x, z, y, t):
        return (side, x ^ flip, z, y, t) if leg == t else (side, x, z ^ flip, y, t)

    return partner


def add(*values):
    total = values[0].astype(F32)
    for value in values[1:]:
        total = total + value.astype(F32)
    return total.astype(BF16)


def gather_ring(first, second, leg, beside=()):
    one_a = send(first, ring(leg, 1))
    three_b = send(second, ring(leg, 3))
    three_a = send(first, ring(leg, 3))
    one_b = send(second, ring(leg, 1))
    one_a, three_b, beside = lax.optimization_barrier((one_a, three_b, beside))
    far_a = send(one_a, ring(leg, 3))
    far_b = send(three_b, ring(leg, 1))
    return first, second, one_a, one_b, three_a, three_b, far_a, far_b, beside


def scatter_ring(pieces, leg):
    first, second, one_a, one_b, three_a, three_b, far_a, far_b = pieces
    late_a = send(far_a, ring(leg, 3))
    late_b = send(far_b, ring(leg, 1))
    from_one_b = send(one_b, ring(leg, 1))
    from_three_a = send(three_a, ring(leg, 3))
    from_one_a = send(add(one_a, late_a), ring(leg, 1))
    from_three_b = send(add(three_b, late_b), ring(leg, 3))
    return add(first, from_one_a, from_three_a), add(second, from_one_b, from_three_b)


def join_pairs(values):
    half = len(values) // 2
    return jnp.concatenate(values[:half], axis=0), jnp.concatenate(values[half:], axis=0)


def split_pairs(first, second):
    rows = first.shape[0] // 4
    return [value[i * rows : (i + 1) * rows] for value in (first, second) for i in range(4)]


def pick_rows(core, value):
    rows = value.shape[0] // 2
    return jnp.where(core == 0, value[:rows], value[rows:])


def hold(values, space=pltpu.VMEM):
    return [pltpu.with_memory_space_constraint(value, space) for value in values]


def stage_kernel(wanted, place_ref, *refs):
    count = len(refs) // 2

    @pl.when(place_ref[0] == wanted)
    def _():
        copies = [
            pltpu.make_async_copy(refs[k], refs[count + k], refs[-1].at[k]) for k in range(count)
        ]
        for copy in copies:
            copy.start()
        for copy in copies:
            copy.wait()


def stage(wanted, place, values):
    return pl.pallas_call(
        functools.partial(stage_kernel, wanted),
        out_shape=[pltpu.VMEM(value.shape, value.dtype) for value in values],
        in_specs=[pl.BlockSpec(memory_space=pltpu.SMEM)]
        + [pl.BlockSpec(memory_space=pltpu.HBM)] * len(values),
        out_specs=[pl.BlockSpec(memory_space=pltpu.VMEM)] * len(values),
        scratch_shapes=[pltpu.SemaphoreType.DMA((len(values),))],
        compiler_params=pltpu.CompilerParams(vmem_limit_bytes=STAGE_VMEM),
        cost_estimate=pl.CostEstimate(
            flops=0, bytes_accessed=4 * sum(value.size for value in values), transcendentals=0
        ),
    )(place, *hold(values, pltpu.HBM))


def call_inside(kernel, out_shapes, scalars, operands):
    inside = pl.BlockSpec(memory_space=pltpu.VMEM)
    return pl.pallas_call(
        kernel,
        out_shape=out_shapes,
        in_specs=[pl.BlockSpec(memory_space=pltpu.SMEM)] + [inside] * len(operands),
        out_specs=jax.tree.map(lambda out: inside, out_shapes),
        compiler_params=pltpu.CompilerParams(vmem_limit_bytes=KERNEL_VMEM),
    )(scalars, *hold(operands))


def front_kernel(place_ref, residual_hbm, gain_hbm, router_hbm, routes, out, *scratch):
    residual, gain, router, arrived = scratch
    copies = [
        pltpu.make_async_copy(source, target, arrived.at[k])
        for k, (source, target) in enumerate(
            ((residual_hbm, residual), (gain_hbm, gain), (router_hbm, router))
        )
    ]
    for copy in copies:
        copy.start()
    for copy in copies:
        copy.wait()
    core = place_ref[1]
    x_rows = pick_rows(core, residual[0].astype(F32))
    normed = x_rows * rms_scale(x_rows) * gain[...].astype(F32)
    logits = lax.dot_general(
        router[0].astype(F32),
        normed,
        (((1,), (1,)), ((), ())),
        precision=lax.Precision.HIGHEST,
        preferred_element_type=F32,
    )
    scores = 1.0 / (1.0 + jnp.exp(-logits))
    experts, rows = scores.shape
    chosen = routes[0]
    chosen = jnp.where(core == 0, chosen[:, :rows], chosen[:, rows:])
    expert_ids = lax.broadcasted_iota(jnp.int32, scores.shape, 0)
    named = jnp.zeros(scores.shape, F32)
    for k in range(chosen.shape[0]):
        named = jnp.where(chosen[k : k + 1] == expert_ids, 1.0, named)
    picked = named * scores
    weight = (ROUTE_SCALE * picked / jnp.sum(picked, axis=0, keepdims=True)).T
    width = normed.shape[1]
    spare = jnp.zeros((weight.shape[0], out.shape[1] - width - weight.shape[1]), F32)
    out[:, :width] = normed.astype(BF16)
    out[:, width:] = jnp.concatenate([weight, spare], axis=1).astype(BF16)


def front(place, residual, moe_gain, router, routes):
    shape = (residual.shape[1] // 2, residual.shape[2] + WEIGHT_LANES)
    anywhere = pl.BlockSpec(memory_space=pltpu.HBM)
    return pl.pallas_call(
        front_kernel,
        out_shape=jax.ShapeDtypeStruct(shape, BF16),
        in_specs=[pl.BlockSpec(memory_space=pltpu.SMEM)]
        + [anywhere] * 3
        + [pl.BlockSpec(memory_space=pltpu.VMEM)],
        out_specs=pl.BlockSpec(memory_space=pltpu.VMEM),
        scratch_shapes=[
            pltpu.VMEM(residual.shape, BF16),
            pltpu.VMEM(moe_gain.shape, BF16),
            pltpu.VMEM(router.shape, BF16),
            pltpu.SemaphoreType.DMA((3,)),
        ],
        compiler_params=pltpu.CompilerParams(vmem_limit_bytes=KERNEL_VMEM),
    )(place, *hold((residual, moe_gain, router), pltpu.HBM), jnp.swapaxes(routes, 1, 2))


def project_kernel(
    place_ref,
    residual,
    back_same,
    back_flip,
    gain_own,
    gain_other,
    proj_own,
    proj_other,
    kv_gain,
    cosine,
    sine,
    updated_out,
    fresh_out,
):
    core = place_ref[1]
    moe_out = back_same[...].astype(F32) + back_flip[...].astype(F32)
    updated = (pick_rows(core, residual[0].astype(F32)) + moe_out).astype(BF16)
    updated_out[...] = updated
    updated = updated.astype(F32)
    half = gain_own.shape[1]
    low, high = updated[:, :half], updated[:, half:]
    total = 0.0
    for part, gain, proj in (
        (jnp.where(core == 0, low, high), gain_own, proj_own),
        (jnp.where(core == 0, high, low), gain_other, proj_other),
    ):
        scaled = (part * gain[...].astype(F32)).astype(BF16)
        total = total + lax.dot_general(
            scaled, proj[...], (((1,), (1,)), ((), ())), preferred_element_type=F32
        )
    kv = total * rms_scale(updated)
    width = kv_gain.shape[1]
    latent, rope = kv[:, :width], kv[:, width:]
    turn = rope.shape[1] // 2
    a, c = rope[:, :turn], rope[:, turn:]
    fresh_out[:, :width] = (latent * rms_scale(latent) * kv_gain[...].astype(F32)).astype(BF16)
    fresh_out[:, width:] = jnp.concatenate(
        [a * cosine[...] - c * sine[...], a * sine[...] + c * cosine[...]], axis=1
    ).astype(BF16)


def merge_kernel(
    place_ref,
    fresh_own,
    fresh_other,
    updated_own,
    updated_other,
    mixed,
    peak,
    mass,
    query_rot,
    query_lat,
    resid_out,
    latent_out,
    rope_out,
    attn_out,
):
    role, core = place_ref[0], place_ref[1]

    def both(own, other):
        own, other = own[...].astype(F32), other[...].astype(F32)
        first = jnp.where(core == 0, own, other)
        second = jnp.where(core == 0, other, own)
        return jnp.concatenate([first, second], axis=0)

    @pl.when(role == 0)
    def _():
        resid_out[0] = both(updated_own, updated_other).astype(BF16)
        fresh = both(fresh_own, fresh_other)
        width = latent_out.shape[2]
        latent, rope = fresh[:, :width], fresh[:, width:]
        latent_out[0] = latent.astype(BF16)
        rope_out[0] = rope.astype(BF16)
        for t in range(latent.shape[0]):
            lat = latent[t : t + 1]
            own = jnp.sum(query_lat[0, t].astype(F32) * lat, axis=1, keepdims=True)
            own += jnp.sum(query_rot[t].astype(F32) * rope[t : t + 1], axis=1, keepdims=True)
            own *= SCORE_SCALE
            held = peak[t, :, :1]
            top = jnp.maximum(held, own)
            kept = jnp.exp(held - top)
            own = jnp.exp(own - top)
            total = mass[t, :, :1] * kept + own
            attn_out[0, t] = (mixed[t] * (kept / total) + (own / total) * lat).astype(BF16)

    @pl.when(role == 1)
    def _():
        for out in (resid_out, latent_out, rope_out, attn_out):
            out[...] = jnp.zeros_like(out)


def dot(left, right):
    return jnp.dot(left, right, preferred_element_type=F32)


def attend_cache(lengths, query_lat, query_rot, cache_lat, cache_rot, mixed, peak, mass, turned):
    heads, rope = turned.shape[1:]
    flat = heads * rope
    lane = lax.broadcasted_iota(jnp.int32, (heads, flat), 1)
    own_lanes = lane // rope == lax.broadcasted_iota(jnp.int32, (heads, flat), 0)
    fold = lax.broadcasted_iota(jnp.int32, (flat, rope), 0) % rope
    fold = (fold == lax.broadcasted_iota(jnp.int32, (flat, rope), 1)).astype(F32).astype(BF16)
    rotary = query_rot[...].astype(F32)
    for t in range(rotary.shape[0]):
        rot = dot(jnp.where(own_lanes, rotary[t : t + 1], 0.0).astype(BF16), fold).astype(BF16)
        turned[t] = rot
        scores = lax.dot_general(
            query_lat[t], cache_lat[t], (((1,), (1,)), ((), ())), preferred_element_type=F32
        )
        scores = (scores + dot(rot, cache_rot[t])) * SCORE_SCALE
        usable = lax.broadcasted_iota(jnp.int32, scores.shape, 1) < lengths[0, t]
        scores = jnp.where(usable, scores, -1e30)
        top = jnp.max(scores, axis=1, keepdims=True)
        weights = jnp.where(usable, jnp.exp(scores - top), 0.0)
        mixed[t] = dot(weights.astype(BF16), cache_lat[t])
        peak[t] = jnp.broadcast_to(top, peak.shape[1:])
        mass[t] = jnp.broadcast_to(jnp.sum(weights, axis=1, keepdims=True), mass.shape[1:])


def roles_kernel(place_ref, lengths, *refs):
    pieces, weights, far = refs[0:8], refs[8:14], refs[14:20]
    outs, cached, projections = refs[20:28], refs[28:32], refs[32:34]
    near, arrived = refs[34:38], refs[38]
    down_a, down_b = weights[4:]
    width, model_width = down_a.shape
    spans = [slice(start, start + CHUNK) for start in range(0, model_width, CHUNK)]

    @pl.when(place_ref[0] == 0)
    def _():
        sources = [far[k].at[0] for k in range(4)] + list(far[4:])
        copies = [
            pltpu.make_async_copy(source, target, arrived.at[k])
            for k, (source, target) in enumerate(zip(sources, (*near, *projections)))
        ]
        for copy in copies:
            copy.start()
        for copy in copies[:4]:
            copy.wait()
        attend_cache(lengths, *near, *cached)
        for copy in copies[4:]:
            copy.wait()

    @pl.when(place_ref[0] == 1)
    def _():
        sums = None
        for span in spans:
            rows = jnp.concatenate([piece[:, span] for piece in pieces], axis=0)
            parts = [dot(rows, weight[span, :]) for weight in weights[:4]]
            sums = parts if sums is None else [a + b for a, b in zip(sums, parts)]
        hidden = [
            (sums[k] / (1.0 + jnp.exp(-sums[k])) * sums[2 + k]).astype(BF16) for k in range(2)
        ]
        lanes = jnp.concatenate([piece[:, model_width:] for piece in pieces], axis=0).astype(F32)
        mine = lax.broadcasted_iota(jnp.int32, lanes.shape, 1) == place_ref[2]
        scale = jnp.sum(jnp.where(mine, lanes, 0.0), axis=1, keepdims=True)
        for span in spans:
            total = dot(hidden[0], down_a[:, span]) + dot(hidden[1], down_b[:, span])
            answer = (total * scale).astype(BF16)
            for k, out in enumerate(outs):
                size = out.shape[0]
                out[:, span] = answer[k * size : (k + 1) * size]


def roles(place, lengths, pieces, weights, attended, projections):
    model_width = weights[0].shape[0]
    _, tokens, heads, latent = attended[0].shape
    rope = attended[3].shape[2]
    smem = pl.BlockSpec(memory_space=pltpu.SMEM)
    inside = pl.BlockSpec(memory_space=pltpu.VMEM)
    anywhere = pl.BlockSpec(memory_space=pltpu.HBM)
    wide = jax.ShapeDtypeStruct((tokens, heads, WEIGHT_LANES), F32)
    results = pl.pallas_call(
        roles_kernel,
        out_shape=[jax.ShapeDtypeStruct((piece.shape[0], model_width), BF16) for piece in pieces]
        + [jax.ShapeDtypeStruct((tokens, heads, latent), F32), wide, wide]
        + [jax.ShapeDtypeStruct((tokens, heads, rope), BF16)]
        + [pltpu.VMEM(value.shape, value.dtype) for value in projections],
        in_specs=[smem, smem] + [inside] * 14 + [anywhere] * 6,
        out_specs=[inside] * 14,
        scratch_shapes=[pltpu.VMEM(value.shape[1:], BF16) for value in attended]
        + [pltpu.SemaphoreType.DMA((6,))],
        compiler_params=pltpu.CompilerParams(vmem_limit_bytes=ROLES_VMEM),
        cost_estimate=pl.CostEstimate(
            flops=3072 * model_width * weights[0].shape[1],
            bytes_accessed=12 * model_width * weights[0].shape[1],
            transcendentals=0,
        ),
    )(place, lengths, *hold(pieces), *hold(weights), *hold(attended, pltpu.HBM), *hold(projections, pltpu.HBM))
    return results[:8], results[8:12], results[12:]


def rms_scale(values):
    return lax.rsqrt(jnp.mean(values * values, axis=-1, keepdims=True) + NORM_EPS)


def turns(width, position):
    step_ids = lax.broadcasted_iota(jnp.int32, (1, width // 2), 1).astype(F32)
    inverse_freq = jnp.exp(-(2.0 * step_ids / width) * jnp.log(ROPE_BASE))
    angles = position.astype(F32)[:, None] * inverse_freq
    return jnp.cos(angles), jnp.sin(angles)


def body(
    residual,
    moe_gain,
    router,
    routes,
    gate_w,
    up_w,
    down_w,
    attn_gain,
    kv_proj,
    kv_gain,
    cache_latent,
    cache_rope,
    lengths,
    query_latent,
    query_rope,
):
    role = lax.axis_index("side").astype(jnp.int32)
    core = lax.axis_index("tp").astype(jnp.int32)
    own_expert = (lax.axis_index("grp") // NY).astype(jnp.int32)
    place = jnp.stack([role, core, own_expert])
    model_width = residual.shape[2]
    group_rows = residual.shape[1]
    rows = group_rows // 2
    latent_width = kv_gain.shape[1]
    rope_width = kv_proj.shape[1] - latent_width
    heads_here = query_latent.shape[2]
    barrier = lax.optimization_barrier

    gate_other, up_other = (send(value[0], other_core) for value in (gate_w, up_w))
    gain_other = send(attn_gain, other_core)

    outgoing = front(place, residual, moe_gain, router, routes)
    arrived = send(outgoing, across(0)), send(outgoing, across(1))
    gates = stage(1, place, (gate_w[0], up_w[0], down_w[0]))
    own_lengths = lax.dynamic_slice_in_dim(lengths[0], core * rows, rows, 0)
    cosine, sine = turns(rope_width, own_lengths)
    arrived, gates, gate_other, up_other, gain_other, cosine, sine, down_own = barrier(
        (arrived, gates, gate_other, up_other, gain_other, cosine, sine, down_w[0])
    )
    down_other = send(down_own, other_core)
    column = join_pairs(gather_ring(*arrived, 0)[:-1])
    column, down_other, kv_own = barrier((column, down_other, kv_proj[0]))
    kv_other = send(kv_own, other_core)
    others = stage(1, place, (gate_other, up_other, down_other))
    *pieces, others = gather_ring(*column, 1, others)

    answers, cached, projections = roles(
        place,
        lengths,
        pieces,
        (gates[0], others[0], gates[1], others[1], gates[2], others[2]),
        (query_latent, query_rope, cache_latent, cache_rope),
        (kv_own, kv_other),
    )
    back_same, back_flip = scatter_ring(split_pairs(*scatter_ring(answers, 1)), 0)
    back_same = send(back_same, across(0))
    back_flip = send(back_flip, across(1))

    updated, fresh = call_inside(
        project_kernel,
        [
            jax.ShapeDtypeStruct((rows, model_width), BF16),
            jax.ShapeDtypeStruct((rows, latent_width + rope_width), BF16),
        ],
        place,
        (
            residual,
            back_same,
            back_flip,
            attn_gain,
            gain_other,
            *projections,
            kv_gain,
            cosine,
            sine,
        ),
    )
    updated_other = send(updated, other_core)
    fresh_other = send(fresh, other_core)
    return call_inside(
        merge_kernel,
        [
            jax.ShapeDtypeStruct((1, group_rows, model_width), BF16),
            jax.ShapeDtypeStruct((1, group_rows, latent_width), BF16),
            jax.ShapeDtypeStruct((1, group_rows, rope_width), BF16),
            jax.ShapeDtypeStruct((1, group_rows, heads_here, latent_width), BF16),
        ],
        place,
        (fresh, fresh_other, updated, updated_other, *cached, query_latent),
    )


def solution(mesh):
    in_specs = (
        P("side", "grp", None),
        P("side", None),
        P("side", None, None),
        P("side", "grp", None),
        P("side", None, ("grp", "tp")),
        P("side", None, ("grp", "tp")),
        P("side", ("grp", "tp"), None),
        P("side", "tp"),
        P("side", None, "tp"),
        P("side", None),
        P("side", "grp", None, None),
        P("side", "grp", None, None),
        P("side", "grp"),
        P("side", "grp", "tp", None),
        P("side", "grp", "tp"),
    )
    out_specs = (
        P("side", "grp", None),
        P("side", "grp", None),
        P("side", "grp", None),
        P("side", "grp", "tp", None),
    )
    return jax.shard_map(body, mesh=mesh, in_specs=in_specs, out_specs=out_specs, check_vma=False)
```

time: 199 us -> 112 us (0.56)
  matrix products: 45 us -> 0 us
  waiting for transfers between devices: 81.3 us -> 49.2 us
  Pallas kernels: 0 us -> 18.4 us
  other arithmetic: 12.7 us -> 1.68 us
  local copies, waits for them, and re-layouts: 10.8 us -> 0.76 us
  starting transfers between devices: 46.7 us -> 40.5 us
    dot_general x10 -> x0, matrix products: 45 us -> none  [the longest x1 12.2 us: body(): jnp.dot(hidden_of(gate_other, up_other), down_other, preferred_element_ty...]
    ppermute x27 -> x35, waiting for transfers between devices: 81.3 us -> 49.2 us  [send(): return lax.ppermute(value, AXES, pairs_of(partner))]
    pallas_call x0 -> x6, Pallas kernels: none -> 18.4 us  [the longest x1 9.87 us: roles(): pl.pallas_call(roles_kernel, out_shape=[jax.ShapeDtypeStruct((piece.shape...]
    ppermute x27 -> x35, starting transfers between devices: 46.7 us -> 40.5 us  [send(): return lax.ppermute(value, AXES, pairs_of(partner))]
    unnamed x31 -> x18, local copies, waits for them, and re-layouts: 6.53 us -> 0.73 us
    reduce_sum x7 -> x0, other arithmetic: 4.7 us -> none  [the longest x3 1.42 us: rms_scale(): jnp.mean(values * values, axis=-1, keepdims=True) + NORM_EPS]
  transfers between devices with their start and end apart: 27 -> 35, of which waited for: 5 -> 20; matrix products, arithmetic and copies ran while one was open for 21% -> 2% of each run, Pallas kernels for 0% -> 3%
where the time goes in v3:
time: 112 us; the launch traced here: 111 us
  waiting for transfers between devices  49.2 us (44%)
  starting transfers between devices  40.5 us (36%)
  Pallas kernels  18.4 us (16%)
  other arithmetic  1.68 us (2%)
    ppermute x35, waiting for transfers between devices, send(): return lax.ppermute(value, AXES, pairs_of(partner))  49.2 us
    ppermute x35, starting transfers between devices, send(): return lax.ppermute(value, AXES, pairs_of(partner))  40.5 us
    pallas_call x1, Pallas kernels, roles(): pl.pallas_call(roles_kernel, out_shape=[jax.ShapeDtypeStruct((piece.shape...  9.87 us
    pallas_call x2, Pallas kernels, call_inside(): pl.pallas_call(kernel, out_shape=out_shapes, in_specs=[pl.BlockSpec(memor...  4.8 us
    pallas_call x1, Pallas kernels, front(): pl.pallas_call(front_kernel, out_shape=jax.ShapeDtypeStruct(shape, BF16),...  2.54 us
  transfers between devices with their start and end apart: 35, of which 20 were waited for; matrix products, arithmetic and copies ran while one was open for 2% of the time, Pallas kernels for 3%

profile of v3, /device:TPU:1, one launch (start us, length us, event | category | flops | bytes accessed | tf_op | source)
XLA Modules:
  0.0 111.3 jit_solution(9072451381049541754)
XLA Ops:
  3.0 2.5 %shard_map.174 = bf16[8,7296]{1,0:T(8,128)(2,1)S(1)} custom-call(s32[3]{0:T(128)S(1)} %pad_add_fusion.place_ref, bf16[1,16,7168]{2,1,0:T(8,128)(2,1)} %residual.1, bf16[1,7168]{1,0:T(2,128)(2,1)} %gain_hbm.1, bf16[1,16,7168]{2,1,0:T(8,128)(2,1)} %router_hbm.1, s32[1,8,16]{2,1,0:T(8,128)S(1)} %bitcast.10), custom_call_target="tpu_custom_call" | custom-call | tf_op jit(solution)/shard_map/pallas_call | solution.py:194
  5.5 2.9 %collective-permute-start.1 = (bf16[8,7296]{1,0:T(8,128)(2,1)S(1)}, bf16[8,7296]{1,0:T(8,128)(2,1)S(1)}, u32[]{:S(2)}, u32[]{:S(2)}) collective-permute-start(bf16[8,7296]{1,0:T(8,128)(2,1)S(1)} %shard_map.174), channel_id=1, source_target_pairs={{0,66},{1,67},{2,64},{3,65},{4,70},{5,71},{6,68},{7,69},{8,74},{9,... | collective-permute-start | bytes 350216 | tf_op jit(solution)/shard_map/ppermute | solution.py:47
  11.2 2.4 %collective-permute-done.4.gain_other = bf16[1,3584]{1,0:T(2,128)(2,1)S(1)} collective-permute-done((bf16[1,3584]{1,0:T(2,128)(2,1)}, bf16[1,3584]{1,0:T(2,128)(2,1)S(1)}, u32[]{:S(2)}, u32[]{:S(2)}) %collective-permute-start.4) | collective-permute-done | bytes 7200 | tf_op jit(solution)/shard_map/ppermute | solution.py:47
  17.3 2.2 %collective-permute-start.6 = (bf16[8,7296]{1,0:T(8,128)(2,1)S(1)}, bf16[8,7296]{1,0:T(8,128)(2,1)S(1)}, u32[]{:S(2)}, u32[]{:S(2)}) collective-permute-start(bf16[8,7296]{1,0:T(8,128)(2,1)S(1)} %collective-permute-done.1), channel_id=1, source_target_pairs={{0,48},{1,13},{2,50},{3,15},{4,52},{5,9},{6,54},{7,11},{8,56},{9,5... | collective-permute-start | bytes 350216 | tf_op jit(solution)/shard_map/ppermute | solution.py:47
  22.4 1.9 %collective-permute-start.9 = (bf16[8,7296]{1,0:T(8,128)(2,1)S(1)}, bf16[8,7296]{1,0:T(8,128)(2,1)S(1)}, u32[]{:S(2)}, u32[]{:S(2)}) collective-permute-start(bf16[8,7296]{1,0:T(8,128)(2,1)S(1)} %collective-permute-done.5), channel_id=1, source_target_pairs={{0,48},{1,13},{2,50},{3,15},{4,52},{5,9},{6,54},{7,11},{8,56},{9,5... | collective-permute-start | bytes 350216 | tf_op jit(solution)/shard_map/ppermute | solution.py:47
  25.4 1.9 %collective-permute-done.9 = bf16[8,7296]{1,0:T(8,128)(2,1)S(1)} collective-permute-done((bf16[8,7296]{1,0:T(8,128)(2,1)S(1)}, bf16[8,7296]{1,0:T(8,128)(2,1)S(1)}, u32[]{:S(2)}, u32[]{:S(2)}) %collective-permute-start.9) | collective-permute-done | bytes 116768 | tf_op jit(solution)/shard_map/ppermute | solution.py:47
  28.4 1.9 %collective-permute-start.18 = (bf16[576,3584]{1,0:T(8,128)(2,1)S(1)}, bf16[576,3584]{1,0:T(8,128)(2,1)}, u32[]{:S(2)}, u32[]{:S(2)}) collective-permute-start(bf16[576,3584]{1,0:T(8,128)(2,1)S(1)} %bitcast.12), channel_id=1, source_target_pairs={{0,1},{1,0},{2,3},{3,2},{4,5},{5,4},{6,7},{7,6},{8,9},{9,8},{10,11... | collective-permute-start | bytes 12386312 | tf_op jit(solution)/shard_map/ppermute | solution.py:47
  33.8 4.2 %collective-permute-done.12.refs_2_ = bf16[32,7296]{1,0:T(8,128)(2,1)S(1)} collective-permute-done((bf16[32,7296]{1,0:T(8,128)(2,1)S(1)}, bf16[32,7296]{1,0:T(8,128)(2,1)S(1)}, u32[]{:S(2)}, u32[]{:S(2)}) %collective-permute-start.12) | collective-permute-done | bytes 466976 | tf_op jit(solution)/shard_map/ppermute | solution.py:47
  40.3 4.0 %collective-permute-done.15.refs_4_ = bf16[32,7296]{1,0:T(8,128)(2,1)S(1)} collective-permute-done((bf16[32,7296]{1,0:T(8,128)(2,1)S(1)}, bf16[32,7296]{1,0:T(8,128)(2,1)S(1)}, u32[]{:S(2)}, u32[]{:S(2)}) %collective-permute-start.15) | collective-permute-done | bytes 466976 | tf_op jit(solution)/shard_map/ppermute | solution.py:47
  44.2 5.0 %collective-permute-done.16.refs_6_ = bf16[32,7296]{1,0:T(8,128)(2,1)S(1)} collective-permute-done((bf16[32,7296]{1,0:T(8,128)(2,1)S(1)}, bf16[32,7296]{1,0:T(8,128)(2,1)S(1)}, u32[]{:S(2)}, u32[]{:S(2)}) %collective-permute-start.16) | collective-permute-done | bytes 466976 | tf_op jit(solution)/shard_map/ppermute | solution.py:47
  49.3 9.9 %shard_map.177 = (bf16[32,7168]{1,0:T(8,128)(2,1)S(1)}, bf16[32,7168]{1,0:T(8,128)(2,1)S(1)}, bf16[32,7168]{1,0:T(8,128)(2,1)S(1)}, bf16[32,7168]{1,0:T(8,128)(2...) custom-call(s32[3]{0:T(128)S(1)} %pad_add_fusion.place_ref, ...), custom_call_target="tpu_custom_call" | custom-call | flops 5637144576 | bytes 22020096 | tf_op jit(solution)/shard_map/pallas_call | solution.py:383
  60.4 1.7 %collective-permute-start.21 = (bf16[32,7168]{1,0:T(8,128)(2,1)S(1)}, bf16[32,7168]{1,0:T(8,128)(2,1)S(1)}, u32[]{:S(2)}, u32[]{:S(2)}) collective-permute-start(bf16[32,7168]{1,0:T(8,128)(2,1)S(1)} %get-tuple-element.76), channel_id=1, source_target_pairs={{0,12},{1,49},{2,14},{3,51},{4,8},{5,53},{6,10},{7,55},{8,4},{9,57... | collective-permute-start | bytes 1376264 | tf_op jit(solution)/shard_map/ppermute | solution.py:47
  62.2 4.7 %collective-permute-done.23 = bf16[32,7168]{1,0:T(8,128)(2,1)S(1)} collective-permute-done((bf16[32,7168]{1,0:T(8,128)(2,1)S(1)}, bf16[32,7168]{1,0:T(8,128)(2,1)S(1)}, u32[]{:S(2)}, u32[]{:S(2)}) %collective-permute-start.23) | collective-permute-done | bytes 458784 | tf_op jit(solution)/shard_map/ppermute | solution.py:47
  68.5 3.2 %collective-permute-done.22 = bf16[32,7168]{1,0:T(8,128)(2,1)S(1)} collective-permute-done((bf16[32,7168]{1,0:T(8,128)(2,1)S(1)}, bf16[32,7168]{1,0:T(8,128)(2,1)S(1)}, u32[]{:S(2)}, u32[]{:S(2)}) %collective-permute-start.22) | collective-permute-done | bytes 458784 | tf_op jit(solution)/shard_map/ppermute | solution.py:47
  71.8 6.4 %collective-permute-done.24 = bf16[32,7168]{1,0:T(8,128)(2,1)S(1)} collective-permute-done((bf16[32,7168]{1,0:T(8,128)(2,1)S(1)}, bf16[32,7168]{1,0:T(8,128)(2,1)S(1)}, u32[]{:S(2)}, u32[]{:S(2)}) %collective-permute-start.24) | collective-permute-done | bytes 458784 | tf_op jit(solution)/shard_map/ppermute | solution.py:47
  80.2 3.8 %collective-permute-start.25 = (bf16[8,7168]{1,0:T(8,128)(2,1)S(1)}, bf16[8,7168]{1,0:T(8,128)(2,1)S(1)}, u32[]{:S(2)}, u32[]{:S(2)}) collective-permute-start(bf16[8,7168]{1,0:T(8,128)(2,1)S(1)} %get-tuple-element.96), channel_id=1, source_target_pairs={{0,48},{1,13},{2,50},{3,15},{4,52},{5,9},{6,54},{7,11},{8,56},{9,5... | collective-permute-start | bytes 344072 | tf_op jit(solution)/shard_map/ppermute | solution.py:47
  84.0 2.0 %collective-permute-start.31 = (bf16[8,7168]{1,0:T(8,128)(2,1)S(1)}, bf16[8,7168]{1,0:T(8,128)(2,1)S(1)}, u32[]{:S(2)}, u32[]{:S(2)}) collective-permute-start(bf16[8,7168]{1,0:T(8,128)(2,1)S(1)} %add_convert_fusion.5), channel_id=1, source_target_pairs={{0,48},{1,13},{2,50},{3,15},{4,52},{5,9},{6,54},{7,11},{8,56},{9,5... | collective-permute-start | bytes 344072 | tf_op jit(solution)/shard_map/ppermute | solution.py:47
  86.7 2.2 %collective-permute-done.31 = bf16[8,7168]{1,0:T(8,128)(2,1)S(1)} collective-permute-done((bf16[8,7168]{1,0:T(8,128)(2,1)S(1)}, bf16[8,7168]{1,0:T(8,128)(2,1)S(1)}, u32[]{:S(2)}, u32[]{:S(2)}) %collective-permute-start.31) | collective-permute-done | bytes 114720 | tf_op jit(solution)/shard_map/ppermute | solution.py:47
  89.1 1.8 %collective-permute-done.27 = bf16[8,7168]{1,0:T(8,128)(2,1)S(1)} collective-permute-done((bf16[8,7168]{1,0:T(8,128)(2,1)S(1)}, bf16[8,7168]{1,0:T(8,128)(2,1)S(1)}, u32[]{:S(2)}, u32[]{:S(2)}) %collective-permute-start.27) | collective-permute-done | bytes 114720 | tf_op jit(solution)/shard_map/ppermute | solution.py:47
  90.9 2.1 %collective-permute-done.26 = bf16[8,7168]{1,0:T(8,128)(2,1)S(1)} collective-permute-done((bf16[8,7168]{1,0:T(8,128)(2,1)S(1)}, bf16[8,7168]{1,0:T(8,128)(2,1)S(1)}, u32[]{:S(2)}, u32[]{:S(2)}) %collective-permute-start.26) | collective-permute-done | bytes 114720 | tf_op jit(solution)/shard_map/ppermute | solution.py:47
  94.3 4.0 %collective-permute-done.28.back_same = bf16[8,7168]{1,0:T(8,128)(2,1)S(1)} collective-permute-done((bf16[8,7168]{1,0:T(8,128)(2,1)S(1)}, bf16[8,7168]{1,0:T(8,128)(2,1)S(1)}, u32[]{:S(2)}, u32[]{:S(2)}) %collective-permute-start.28) | collective-permute-done | bytes 114720 | tf_op jit(solution)/shard_map/ppermute | solution.py:47
  98.3 2.9 %shard_map.178 = (bf16[8,7168]{1,0:T(8,128)(2,1)S(1)}, bf16[8,576]{1,0:T(8,128)(2,1)S(1)}) custom-call(s32[3]{0:T(128)S(1)} %pad_add_fusion.place_ref, bf16[1,16,7168]{2,1,0:T(8,128)(2,1)S(1)} %copy-done.1, bf16[8,7168]{1,0:T(8,128)(2,1)S(1)} %collective-permute-done.28.back_same, bf16[8,7168]{1,0:T(8,128)(2,1)S(1)} %collective-permute-done.32.back_flip, ...), custom_call_target="tpu_custom_call" | custom-call | tf_op jit(solution)/shard_map/pallas_call | solution.py:144
  101.2 7.1 %collective-permute-start.34 = (bf16[8,7168]{1,0:T(8,128)(2,1)S(1)}, bf16[8,7168]{1,0:T(8,128)(2,1)S(1)}, u32[]{:S(2)}, u32[]{:S(2)}) collective-permute-start(bf16[8,7168]{1,0:T(8,128)(2,1)S(1)} %get-tuple-element.87.updated_own), channel_id=1, source_target_pairs={{0,1},{1,0},{2,3},{3,2},{4,5},{5,4},{6,7},{7,6},{8,9},{9,8},{10,11... | collective-permute-start | bytes 344072 | tf_op jit(solution)/shard_map/ppermute | solution.py:47
  109.4 1.9 %shard_map.179 = (bf16[1,16,7168]{2,1,0:T(8,128)(2,1)}, bf16[1,16,512]{2,1,0:T(8,128)(2,1)}, bf16[1,16,64]{2,1,0:T(8,128)(2,1)}, bf16[1,16,32,512]{3,2,1,0:T(8,128)(2,1)}) custom-call(s32[3]{0:T(128)S(1)} %pad_add_fusion.place_ref, bf16[8,576]{1,0:T(8,128)(2,1)S(1)} %get-tuple-element.86.fresh_own, bf16[8,576]{1,0:T(8,128)(2,1)S(1)} %collective-permute-done.33.fresh_other, ...), custom_call_target="tpu_custom_call" | custom-call | tf_op jit(solution)/shard_map/pallas_call | solution.py:144
  (85 shorter events, 28.0 us)
Async XLA Ops:
  0.6 13.3 %collective-permute-start.2 = (bf16[7168,256]{1,0:T(8,128)(2,1)}, bf16[7168,256]{1,0:T(8,128)(2,1)}, u32[]{:S(2)}, u32[]{:S(2)}) collective-permute-start(bf16[7168,256]{1,0:T(8,128)(2,1)} %bitcast.13), channel_id=1, source_target_pairs={{0,1},{1,0},{2,3},{3,2},{4,5},{5,4},{6,7},{7,6},{8,9},{9,8},{10,11... | collective-permute-start | bytes 11010056 | tf_op jit(solution)/shard_map/ppermute | solution.py:47
  2.1 11.8 %collective-permute-start.3 = (bf16[7168,256]{1,0:T(8,128)(2,1)}, bf16[7168,256]{1,0:T(8,128)(2,1)}, u32[]{:S(2)}, u32[]{:S(2)}) collective-permute-start(bf16[7168,256]{1,0:T(8,128)(2,1)} %bitcast.15), channel_id=1, source_target_pairs={{0,1},{1,0},{2,3},{3,2},{4,5},{5,4},{6,7},{7,6},{8,9},{9,8},{10,11... | collective-permute-start | bytes 11010056 | tf_op jit(solution)/shard_map/ppermute | solution.py:47
  5.5 8.1 %collective-permute-start.1 = (bf16[8,7296]{1,0:T(8,128)(2,1)S(1)}, bf16[8,7296]{1,0:T(8,128)(2,1)S(1)}, u32[]{:S(2)}, u32[]{:S(2)}) collective-permute-start(bf16[8,7296]{1,0:T(8,128)(2,1)S(1)} %shard_map.174), channel_id=1, source_target_pairs={{0,66},{1,67},{2,64},{3,65},{4,70},{5,71},{6,68},{7,69},{8,74},{9,... | collective-permute-start | bytes 350216 | tf_op jit(solution)/shard_map/ppermute | solution.py:47
  8.4 5.5 %collective-permute-start = (bf16[8,7296]{1,0:T(8,128)(2,1)S(1)}, bf16[8,7296]{1,0:T(8,128)(2,1)S(1)}, u32[]{:S(2)}, u32[]{:S(2)}) collective-permute-start(bf16[8,7296]{1,0:T(8,128)(2,1)S(1)} %shard_map.174), channel_id=1, source_target_pairs={{0,64},{1,65},{2,66},{3,67},{4,68},{5,69},{6,70},{7,71},{8,72},{9,... | collective-permute-start | bytes 350216 | tf_op jit(solution)/shard_map/ppermute | solution.py:47
  14.0 14.4 %collective-permute-start.11 = (bf16[256,7168]{1,0:T(8,128)(2,1)S(1)}, bf16[256,7168]{1,0:T(8,128)(2,1)S(1)}, u32[]{:S(2)}, u32[]{:S(2)}) collective-permute-start(bf16[256,7168]{1,0:T(8,128)(2,1)S(1)} %bitcast.18), channel_id=1, source_target_pairs={{0,1},{1,0},{2,3},{3,2},{4,5},{5,4},{6,7},{7,6},{8,9},{9,8},{10,11... | collective-permute-start | bytes 11010056 | tf_op jit(solution)/shard_map/ppermute | solution.py:47
  15.6 5.2 %collective-permute-start.5 = (bf16[8,7296]{1,0:T(8,128)(2,1)S(1)}, bf16[8,7296]{1,0:T(8,128)(2,1)S(1)}, u32[]{:S(2)}, u32[]{:S(2)}) collective-permute-start(bf16[8,7296]{1,0:T(8,128)(2,1)S(1)} %collective-permute-done), channel_id=1, source_target_pairs={{0,16},{1,5},{2,18},{3,7},{4,20},{5,1},{6,22},{7,3},{8,24},{9,13},... | collective-permute-start | bytes 350216 | tf_op jit(solution)/shard_map/ppermute | solution.py:47
  28.4 20.8 %collective-permute-start.18 = (bf16[576,3584]{1,0:T(8,128)(2,1)S(1)}, bf16[576,3584]{1,0:T(8,128)(2,1)}, u32[]{:S(2)}, u32[]{:S(2)}) collective-permute-start(bf16[576,3584]{1,0:T(8,128)(2,1)S(1)} %bitcast.12), channel_id=1, source_target_pairs={{0,1},{1,0},{2,3},{3,2},{4,5},{5,4},{6,7},{7,6},{8,9},{9,8},{10,11... | collective-permute-start | bytes 12386312 | tf_op jit(solution)/shard_map/ppermute | solution.py:47
  30.3 7.7 %collective-permute-start.12 = (bf16[32,7296]{1,0:T(8,128)(2,1)S(1)}, bf16[32,7296]{1,0:T(8,128)(2,1)S(1)}, u32[]{:S(2)}, u32[]{:S(2)}) collective-permute-start(bf16[32,7296]{1,0:T(8,128)(2,1)S(1)} %pad_maximum_fusion.refs_0_), channel_id=1, source_target_pairs={{0,4},{1,17},{2,6},{3,19},{4,0},{5,21},{6,2},{7,23},{8,12},{9,25},... | collective-permute-start | bytes 1400840 | tf_op jit(solution)/shard_map/ppermute | solution.py:47
  30.3 8.9 %collective-permute-start.13 = (bf16[32,7296]{1,0:T(8,128)(2,1)S(1)}, bf16[32,7296]{1,0:T(8,128)(2,1)S(1)}, u32[]{:S(2)}, u32[]{:S(2)}) collective-permute-start(bf16[32,7296]{1,0:T(8,128)(2,1)S(1)} %pad_maximum_fusion.1.refs_1_), channel_id=1, source_target_pairs={{0,12},{1,49},{2,14},{3,51},{4,8},{5,53},{6,10},{7,55},{8,4},{9,57... | collective-permute-start | bytes 1400840 | tf_op jit(solution)/shard_map/ppermute | solution.py:47
  31.3 12.9 %collective-permute-start.15 = (bf16[32,7296]{1,0:T(8,128)(2,1)S(1)}, bf16[32,7296]{1,0:T(8,128)(2,1)S(1)}, u32[]{:S(2)}, u32[]{:S(2)}) collective-permute-start(bf16[32,7296]{1,0:T(8,128)(2,1)S(1)} %pad_maximum_fusion.refs_0_), channel_id=1, source_target_pairs={{0,12},{1,49},{2,14},{3,51},{4,8},{5,53},{6,10},{7,55},{8,4},{9,57... | collective-permute-start | bytes 1400840 | tf_op jit(solution)/shard_map/ppermute | solution.py:47
  33.0 11.3 %collective-permute-start.14 = (bf16[32,7296]{1,0:T(8,128)(2,1)S(1)}, bf16[32,7296]{1,0:T(8,128)(2,1)S(1)}, u32[]{:S(2)}, u32[]{:S(2)}) collective-permute-start(bf16[32,7296]{1,0:T(8,128)(2,1)S(1)} %pad_maximum_fusion.1.refs_1_), channel_id=1, source_target_pairs={{0,4},{1,17},{2,6},{3,19},{4,0},{5,21},{6,2},{7,23},{8,12},{9,25},... | collective-permute-start | bytes 1400840 | tf_op jit(solution)/shard_map/ppermute | solution.py:47
  39.2 10.0 %collective-permute-start.16 = (bf16[32,7296]{1,0:T(8,128)(2,1)S(1)}, bf16[32,7296]{1,0:T(8,128)(2,1)S(1)}, u32[]{:S(2)}, u32[]{:S(2)}) collective-permute-start(bf16[32,7296]{1,0:T(8,128)(2,1)S(1)} %collective-permute-done.12.refs_2_), channel_id=1, source_target_pairs={{0,12},{1,49},{2,14},{3,51},{4,8},{5,53},{6,10},{7,55},{8,4},{9,57... | collective-permute-start | bytes 1400840 | tf_op jit(solution)/shard_map/ppermute | solution.py:47
  40.3 9.0 %collective-permute-start.17 = (bf16[32,7296]{1,0:T(8,128)(2,1)S(1)}, bf16[32,7296]{1,0:T(8,128)(2,1)S(1)}, u32[]{:S(2)}, u32[]{:S(2)}) collective-permute-start(bf16[32,7296]{1,0:T(8,128)(2,1)S(1)} %collective-permute-done.13.refs_5_), channel_id=1, source_target_pairs={{0,4},{1,17},{2,6},{3,19},{4,0},{5,21},{6,2},{7,23},{8,12},{9,25},... | collective-permute-start | bytes 1400840 | tf_op jit(solution)/shard_map/ppermute | solution.py:47
  59.1 7.7 %collective-permute-start.23 = (bf16[32,7168]{1,0:T(8,128)(2,1)S(1)}, bf16[32,7168]{1,0:T(8,128)(2,1)S(1)}, u32[]{:S(2)}, u32[]{:S(2)}) collective-permute-start(bf16[32,7168]{1,0:T(8,128)(2,1)S(1)} %get-tuple-element.80), channel_id=1, source_target_pairs={{0,4},{1,17},{2,6},{3,19},{4,0},{5,21},{6,2},{7,23},{8,12},{9,25},... | collective-permute-start | bytes 1376264 | tf_op jit(solution)/shard_map/ppermute | solution.py:47
  59.5 8.8 %collective-permute-start.19 = (bf16[32,7168]{1,0:T(8,128)(2,1)S(1)}, bf16[32,7168]{1,0:T(8,128)(2,1)S(1)}, u32[]{:S(2)}, u32[]{:S(2)}) collective-permute-start(bf16[32,7168]{1,0:T(8,128)(2,1)S(1)} %get-tuple-element.75), channel_id=1, source_target_pairs={{0,12},{1,49},{2,14},{3,51},{4,8},{5,53},{6,10},{7,55},{8,4},{9,57... | collective-permute-start | bytes 1376264 | tf_op jit(solution)/shard_map/ppermute | solution.py:47
  60.4 19.4 %collective-permute-start.21 = (bf16[32,7168]{1,0:T(8,128)(2,1)S(1)}, bf16[32,7168]{1,0:T(8,128)(2,1)S(1)}, u32[]{:S(2)}, u32[]{:S(2)}) collective-permute-start(bf16[32,7168]{1,0:T(8,128)(2,1)S(1)} %get-tuple-element.76), channel_id=1, source_target_pairs={{0,12},{1,49},{2,14},{3,51},{4,8},{5,53},{6,10},{7,55},{8,4},{9,57... | collective-permute-start | bytes 1376264 | tf_op jit(solution)/shard_map/ppermute | solution.py:47
  62.1 9.6 %collective-permute-start.22 = (bf16[32,7168]{1,0:T(8,128)(2,1)S(1)}, bf16[32,7168]{1,0:T(8,128)(2,1)S(1)}, u32[]{:S(2)}, u32[]{:S(2)}) collective-permute-start(bf16[32,7168]{1,0:T(8,128)(2,1)S(1)} %get-tuple-element.78), channel_id=1, source_target_pairs={{0,4},{1,17},{2,6},{3,19},{4,0},{5,21},{6,2},{7,23},{8,12},{9,25},... | collective-permute-start | bytes 1376264 | tf_op jit(solution)/shard_map/ppermute | solution.py:47
  67.0 11.2 %collective-permute-start.24 = (bf16[32,7168]{1,0:T(8,128)(2,1)S(1)}, bf16[32,7168]{1,0:T(8,128)(2,1)S(1)}, u32[]{:S(2)}, u32[]{:S(2)}) collective-permute-start(bf16[32,7168]{1,0:T(8,128)(2,1)S(1)} %add_convert_fusion.1), channel_id=1, source_target_pairs={{0,12},{1,49},{2,14},{3,51},{4,8},{5,53},{6,10},{7,55},{8,4},{9,57... | collective-permute-start | bytes 1376264 | tf_op jit(solution)/shard_map/ppermute | solution.py:47
  68.4 11.3 %collective-permute-start.20 = (bf16[32,7168]{1,0:T(8,128)(2,1)S(1)}, bf16[32,7168]{1,0:T(8,128)(2,1)S(1)}, u32[]{:S(2)}, u32[]{:S(2)}) collective-permute-start(bf16[32,7168]{1,0:T(8,128)(2,1)S(1)} %add_convert_fusion.3), channel_id=1, source_target_pairs={{0,4},{1,17},{2,6},{3,19},{4,0},{5,21},{6,2},{7,23},{8,12},{9,25},... | collective-permute-start | bytes 1376264 | tf_op jit(solution)/shard_map/ppermute | solution.py:47
  78.3 5.6 %collective-permute-start.30 = (bf16[8,7168]{1,0:T(8,128)(2,1)S(1)}, bf16[8,7168]{1,0:T(8,128)(2,1)S(1)}, u32[]{:S(2)}, u32[]{:S(2)}) collective-permute-start(bf16[8,7168]{1,0:T(8,128)(2,1)S(1)} %get-tuple-element.94), channel_id=1, source_target_pairs={{0,16},{1,5},{2,18},{3,7},{4,20},{5,1},{6,22},{7,3},{8,24},{9,13},... | collective-permute-start | bytes 344072 | tf_op jit(solution)/shard_map/ppermute | solution.py:47
  80.0 6.8 %collective-permute-start.29 = (bf16[8,7168]{1,0:T(8,128)(2,1)S(1)}, bf16[8,7168]{1,0:T(8,128)(2,1)S(1)}, u32[]{:S(2)}, u32[]{:S(2)}) collective-permute-start(bf16[8,7168]{1,0:T(8,128)(2,1)S(1)} %slice.37), channel_id=1, source_target_pairs={{0,16},{1,5},{2,18},{3,7},{4,20},{5,1},{6,22},{7,3},{8,24},{9,13},... | collective-permute-start | bytes 344072 | tf_op jit(solution)/shard_map/ppermute | solution.py:47
  80.2 6.6 %collective-permute-start.25 = (bf16[8,7168]{1,0:T(8,128)(2,1)S(1)}, bf16[8,7168]{1,0:T(8,128)(2,1)S(1)}, u32[]{:S(2)}, u32[]{:S(2)}) collective-permute-start(bf16[8,7168]{1,0:T(8,128)(2,1)S(1)} %get-tuple-element.96), channel_id=1, source_target_pairs={{0,48},{1,13},{2,50},{3,15},{4,52},{5,9},{6,54},{7,11},{8,56},{9,5... | collective-permute-start | bytes 344072 | tf_op jit(solution)/shard_map/ppermute | solution.py:47
  89.1 5.2 %collective-permute-start.32 = (bf16[8,7168]{1,0:T(8,128)(2,1)S(1)}, bf16[8,7168]{1,0:T(8,128)(2,1)S(1)}, u32[]{:S(2)}, u32[]{:S(2)}) collective-permute-start(bf16[8,7168]{1,0:T(8,128)(2,1)S(1)} %get-tuple-element.92), channel_id=1, source_target_pairs={{0,66},{1,67},{2,64},{3,65},{4,70},{5,71},{6,68},{7,69},{8,74},{9,... | collective-permute-start | bytes 344072 | tf_op jit(solution)/shard_map/ppermute | solution.py:47
  101.2 8.2 %collective-permute-start.34 = (bf16[8,7168]{1,0:T(8,128)(2,1)S(1)}, bf16[8,7168]{1,0:T(8,128)(2,1)S(1)}, u32[]{:S(2)}, u32[]{:S(2)}) collective-permute-start(bf16[8,7168]{1,0:T(8,128)(2,1)S(1)} %get-tuple-element.87.updated_own), channel_id=1, source_target_pairs={{0,1},{1,0},{2,3},{3,2},{4,5},{5,4},{6,7},{7,6},{8,9},{9,8},{10,11... | collective-permute-start | bytes 344072 | tf_op jit(solution)/shard_map/ppermute | solution.py:47
  (20 other events, 197.8 us)

commit v4 on v3

--- a/solution.py
+++ b/solution.py
@@ -69,12 +69,13 @@
     return total.astype(BF16)
 
 
-def gather_ring(first, second, leg, beside=()):
+def gather_ring(first, second, leg, beside=None):
     one_a = send(first, ring(leg, 1))
     three_b = send(second, ring(leg, 3))
     three_a = send(first, ring(leg, 3))
     one_b = send(second, ring(leg, 1))
-    one_a, three_b, beside = lax.optimization_barrier((one_a, three_b, beside))
+    if beside is not None:
+        one_a, three_b, beside = lax.optimization_barrier((one_a, three_b, beside))
     far_a = send(one_a, ring(leg, 3))
     far_b = send(three_b, ring(leg, 1))
     return first, second, one_a, one_b, three_a, three_b, far_a, far_b, beside
@@ -211,8 +212,8 @@
 def project_kernel(
     place_ref,
     residual,
-    back_same,
     back_flip,
+    back_straight,
     gain_own,
     gain_other,
     proj_own,
@@ -224,15 +225,16 @@
     fresh_out,
 ):
     core = place_ref[1]
-    moe_out = back_same[...].astype(F32) + back_flip[...].astype(F32)
-    updated = (pick_rows(core, residual[0].astype(F32)) + moe_out).astype(BF16)
+    x_rows = pick_rows(core, residual[0].astype(F32))
+    moe_out = back_flip[...].astype(F32) + back_straight[...].astype(F32)
+    updated = (x_rows + moe_out).astype(BF16)
     updated_out[...] = updated
     updated = updated.astype(F32)
     half = gain_own.shape[1]
     low, high = updated[:, :half], updated[:, half:]
     total = 0.0
     for part, gain, proj in (
-        (jnp.where(core == 0, low, high), gain_own, proj_own),
+        (jnp.where(core == 0, low, high), gain_own, proj_own.at[0]),
         (jnp.where(core == 0, high, low), gain_other, proj_other),
     ):
         scaled = (part * gain[...].astype(F32)).astype(BF16)
@@ -244,9 +246,10 @@
     latent, rope = kv[:, :width], kv[:, width:]
     turn = rope.shape[1] // 2
     a, c = rope[:, :turn], rope[:, turn:]
+    cos, sin = pick_rows(core, cosine[...]), pick_rows(core, sine[...])
     fresh_out[:, :width] = (latent * rms_scale(latent) * kv_gain[...].astype(F32)).astype(BF16)
     fresh_out[:, width:] = jnp.concatenate(
-        [a * cosine[...] - c * sine[...], a * sine[...] + c * cosine[...]], axis=1
+        [a * cos - c * sin, a * sin + c * cos], axis=1
     ).astype(BF16)
 
 
@@ -312,44 +315,51 @@
     fold = lax.broadcasted_iota(jnp.int32, (flat, rope), 0) % rope
     fold = (fold == lax.broadcasted_iota(jnp.int32, (flat, rope), 1)).astype(F32).astype(BF16)
     rotary = query_rot[...].astype(F32)
-    for t in range(rotary.shape[0]):
-        rot = dot(jnp.where(own_lanes, rotary[t : t + 1], 0.0).astype(BF16), fold).astype(BF16)
+    tokens = range(rotary.shape[0])
+    spread = [jnp.where(own_lanes, rotary[t : t + 1], 0.0).astype(BF16) for t in tokens]
+    folded = dot(jnp.concatenate(spread, axis=0), fold).astype(BF16)
+    scores, usable = [], []
+    for t in tokens:
+        rot = folded[t * heads : (t + 1) * heads]
         turned[t] = rot
-        scores = lax.dot_general(
+        latent_scores = lax.dot_general(
             query_lat[t], cache_lat[t], (((1,), (1,)), ((), ())), preferred_element_type=F32
         )
-        scores = (scores + dot(rot, cache_rot[t])) * SCORE_SCALE
-        usable = lax.broadcasted_iota(jnp.int32, scores.shape, 1) < lengths[0, t]
-        scores = jnp.where(usable, scores, -1e30)
-        top = jnp.max(scores, axis=1, keepdims=True)
-        weights = jnp.where(usable, jnp.exp(scores - top), 0.0)
-        mixed[t] = dot(weights.astype(BF16), cache_lat[t])
-        peak[t] = jnp.broadcast_to(top, peak.shape[1:])
-        mass[t] = jnp.broadcast_to(jnp.sum(weights, axis=1, keepdims=True), mass.shape[1:])
+        scores.append(latent_scores + dot(rot, cache_rot[t]))
+        slots = lax.broadcasted_iota(jnp.int32, scores[t].shape, 1)
+        usable.append((slots < lengths[0, t]).astype(F32))
+    usable = jnp.concatenate(usable, axis=0) > 0.0
+    scores = jnp.where(usable, jnp.concatenate(scores, axis=0) * SCORE_SCALE, -1e30)
+    top = jnp.max(scores, axis=1, keepdims=True)
+    weights = jnp.where(usable, jnp.exp(scores - top), 0.0)
+    total = jnp.sum(weights, axis=1, keepdims=True)
+    weights = weights.astype(BF16)
+    for t in tokens:
+        own = slice(t * heads, (t + 1) * heads)
+        mixed[t] = dot(weights[own], cache_lat[t])
+        peak[t] = jnp.broadcast_to(top[own], peak.shape[1:])
+        mass[t] = jnp.broadcast_to(total[own], mass.shape[1:])
 
 
 def roles_kernel(place_ref, lengths, *refs):
-    pieces, weights, far = refs[0:8], refs[8:14], refs[14:20]
-    outs, cached, projections = refs[20:28], refs[28:32], refs[32:34]
-    near, arrived = refs[34:38], refs[38]
+    pieces, weights, far = refs[0:8], refs[8:14], refs[14:18]
+    outs, cached = refs[18:26], refs[26:30]
+    near, arrived = refs[30:34], refs[34]
     down_a, down_b = weights[4:]
     width, model_width = down_a.shape
     spans = [slice(start, start + CHUNK) for start in range(0, model_width, CHUNK)]
 
     @pl.when(place_ref[0] == 0)
     def _():
-        sources = [far[k].at[0] for k in range(4)] + list(far[4:])
         copies = [
-            pltpu.make_async_copy(source, target, arrived.at[k])
-            for k, (source, target) in enumerate(zip(sources, (*near, *projections)))
+            pltpu.make_async_copy(source.at[0], target, arrived.at[k])
+            for k, (source, target) in enumerate(zip(far, near))
         ]
         for copy in copies:
             copy.start()
-        for copy in copies[:4]:
+        for copy in copies:
             copy.wait()
         attend_cache(lengths, *near, *cached)
-        for copy in copies[4:]:
-            copy.wait()
 
     @pl.when(place_ref[0] == 1)
     def _():
@@ -372,7 +382,7 @@
                 out[:, span] = answer[k * size : (k + 1) * size]
 
 
-def roles(place, lengths, pieces, weights, attended, projections):
+def roles(place, lengths, pieces, weights, attended):
     model_width = weights[0].shape[0]
     _, tokens, heads, latent = attended[0].shape
     rope = attended[3].shape[2]
@@ -384,20 +394,19 @@
         roles_kernel,
         out_shape=[jax.ShapeDtypeStruct((piece.shape[0], model_width), BF16) for piece in pieces]
         + [jax.ShapeDtypeStruct((tokens, heads, latent), F32), wide, wide]
-        + [jax.ShapeDtypeStruct((tokens, heads, rope), BF16)]
-        + [pltpu.VMEM(value.shape, value.dtype) for value in projections],
-        in_specs=[smem, smem] + [inside] * 14 + [anywhere] * 6,
-        out_specs=[inside] * 14,
+        + [jax.ShapeDtypeStruct((tokens, heads, rope), BF16)],
+        in_specs=[smem, smem] + [inside] * 14 + [anywhere] * 4,
+        out_specs=[inside] * 12,
         scratch_shapes=[pltpu.VMEM(value.shape[1:], BF16) for value in attended]
-        + [pltpu.SemaphoreType.DMA((6,))],
+        + [pltpu.SemaphoreType.DMA((4,))],
         compiler_params=pltpu.CompilerParams(vmem_limit_bytes=ROLES_VMEM),
         cost_estimate=pl.CostEstimate(
             flops=3072 * model_width * weights[0].shape[1],
             bytes_accessed=12 * model_width * weights[0].shape[1],
             transcendentals=0,
         ),
-    )(place, lengths, *hold(pieces), *hold(weights), *hold(attended, pltpu.HBM), *hold(projections, pltpu.HBM))
-    return results[:8], results[8:12], results[12:]
+    )(place, lengths, *hold(pieces), *hold(weights), *hold(attended, pltpu.HBM))
+    return results[:8], results[8:]
 
 
 def rms_scale(values):
@@ -440,35 +449,32 @@
     heads_here = query_latent.shape[2]
     barrier = lax.optimization_barrier
 
-    gate_other, up_other = (send(value[0], other_core) for value in (gate_w, up_w))
-    gain_other = send(attn_gain, other_core)
+    place, *swapped = barrier((place, gate_w[0], up_w[0], attn_gain))
+    gate_other, up_other, gain_other = (send(value, other_core) for value in swapped)
 
     outgoing = front(place, residual, moe_gain, router, routes)
-    arrived = send(outgoing, across(0)), send(outgoing, across(1))
-    gates = stage(1, place, (gate_w[0], up_w[0], down_w[0]))
-    own_lengths = lax.dynamic_slice_in_dim(lengths[0], core * rows, rows, 0)
-    cosine, sine = turns(rope_width, own_lengths)
-    arrived, gates, gate_other, up_other, gain_other, cosine, sine, down_own = barrier(
-        (arrived, gates, gate_other, up_other, gain_other, cosine, sine, down_w[0])
+    flipped, straight = send(outgoing, across(1)), send(outgoing, across(0))
+    gates = stage(1, place, (gate_w[0], up_w[0]))
+    cosine, sine = turns(rope_width, lengths[0])
+    flipped, straight, gates, cosine, sine, gain_other, gate_other, up_other, down_own = barrier(
+        (flipped, straight, gates, cosine, sine, gain_other, gate_other, up_other, down_w[0])
     )
     down_other = send(down_own, other_core)
-    column = join_pairs(gather_ring(*arrived, 0)[:-1])
+    column = join_pairs(gather_ring(flipped, straight, 0)[:-1])
     column, down_other, kv_own = barrier((column, down_other, kv_proj[0]))
     kv_other = send(kv_own, other_core)
-    others = stage(1, place, (gate_other, up_other, down_other))
-    *pieces, others = gather_ring(*column, 1, others)
-
-    answers, cached, projections = roles(
+    *pieces, downs = gather_ring(*column, 1, stage(1, place, (down_own,)))
+
+    answers, cached = roles(
         place,
         lengths,
         pieces,
-        (gates[0], others[0], gates[1], others[1], gates[2], others[2]),
+        (gates[0], gate_other, gates[1], up_other, downs[0], down_other),
         (query_latent, query_rope, cache_latent, cache_rope),
-        (kv_own, kv_other),
-    )
-    back_same, back_flip = scatter_ring(split_pairs(*scatter_ring(answers, 1)), 0)
-    back_same = send(back_same, across(0))
+    )
+    back_flip, back_straight = scatter_ring(split_pairs(*scatter_ring(answers, 1)), 0)
     back_flip = send(back_flip, across(1))
+    back_straight = send(back_straight, across(0))
 
     updated, fresh = call_inside(
         project_kernel,
@@ -479,11 +485,12 @@
         place,
         (
             residual,
-            back_same,
             back_flip,
+            back_straight,
             attn_gain,
             gain_other,
-            *projections,
+            kv_proj,
+            kv_other,
             kv_gain,
             cosine,
             sine,

time: 112 us -> 106 us (0.946)
  waiting for transfers between devices: 49.2 us -> 40.8 us
  starting transfers between devices: 40.5 us -> 47.9 us
  Pallas kernels: 18.4 us -> 13.8 us
    ppermute x35, waiting for transfers between devices: 49.2 us -> 40.8 us  [send(): return lax.ppermute(value, AXES, pairs_of(partner))]
    ppermute x35, starting transfers between devices: 40.5 us -> 47.9 us  [send(): return lax.ppermute(value, AXES, pairs_of(partner))]
    pallas_call x1, Pallas kernels: 9.87 us -> 5.32 us  [roles(): pl.pallas_call(roles_kernel, out_shape=[jax.ShapeDtypeStruct((piece.shape...]
where the time goes in v4:
time: 106 us
  starting transfers between devices  47.9 us (45%)
  waiting for transfers between devices  40.8 us (38%)
  Pallas kernels  13.8 us (13%)
  other arithmetic  1.64 us (2%)
    ppermute x35, starting transfers between devices, send(): return lax.ppermute(value, AXES, pairs_of(partner))  47.9 us
    ppermute x35, waiting for transfers between devices, send(): return lax.ppermute(value, AXES, pairs_of(partner))  40.8 us
    pallas_call x1, Pallas kernels, roles(): pl.pallas_call(roles_kernel, out_shape=[jax.ShapeDtypeStruct((piece.shape...  5.32 us
    pallas_call x2, Pallas kernels, call_inside(): pl.pallas_call(kernel, out_shape=out_shapes, in_specs=[pl.BlockSpec(memor...  4.81 us
    pallas_call x1, Pallas kernels, front(): pl.pallas_call(front_kernel, out_shape=jax.ShapeDtypeStruct(shape, BF16),...  2.54 us
  transfers between devices with their start and end apart: 35, of which 20 were waited for; matrix products, arithmetic and copies ran while one was open for 2% of the time, Pallas kernels for 3%

profile of v4, /device:TPU:1, one launch (start us, length us, event | category | flops | bytes accessed | tf_op | source)
XLA Modules:
  0.0 105.8 jit_solution(855671836575776946)
XLA Ops:
  2.9 2.5 %shard_map.174 = bf16[8,7296]{1,0:T(8,128)(2,1)S(1)} custom-call(s32[3]{0:T(128)S(1)} %pad_add_fusion.place_ref, bf16[1,16,7168]{2,1,0:T(8,128)(2,1)} %residual.1, bf16[1,7168]{1,0:T(2,128)(2,1)} %gain_hbm.1, bf16[1,16,7168]{2,1,0:T(8,128)(2,1)} %router_hbm.1, s32[1,8,16]{2,1,0:T(8,128)S(1)} %bitcast.11), custom_call_target="tpu_custom_call" | custom-call | tf_op jit(solution)/shard_map/pallas_call | solution.py:195
  5.5 3.1 %collective-permute-start.1 = (bf16[8,7296]{1,0:T(8,128)(2,1)S(1)}, bf16[8,7296]{1,0:T(8,128)(2,1)S(1)}, u32[]{:S(2)}, u32[]{:S(2)}) collective-permute-start(bf16[8,7296]{1,0:T(8,128)(2,1)S(1)} %shard_map.174), channel_id=1, source_target_pairs={{0,64},{1,65},{2,66},{3,67},{4,68},{5,69},{6,70},{7,71},{8,72},{9,... | collective-permute-start | bytes 350216 | tf_op jit(solution)/shard_map/ppermute | solution.py:47
  11.7 2.0 %collective-permute-done.2.gain_other = bf16[1,3584]{1,0:T(2,128)(2,1)S(1)} collective-permute-done((bf16[1,3584]{1,0:T(2,128)(2,1)}, bf16[1,3584]{1,0:T(2,128)(2,1)S(1)}, u32[]{:S(2)}, u32[]{:S(2)}) %collective-permute-start.2) | collective-permute-done | bytes 7200 | tf_op jit(solution)/shard_map/ppermute | solution.py:47
  17.1 2.2 %collective-permute-start.8 = (bf16[8,7296]{1,0:T(8,128)(2,1)S(1)}, bf16[8,7296]{1,0:T(8,128)(2,1)S(1)}, u32[]{:S(2)}, u32[]{:S(2)}) collective-permute-start(bf16[8,7296]{1,0:T(8,128)(2,1)S(1)} %collective-permute-done.1), channel_id=1, source_target_pairs={{0,48},{1,13},{2,50},{3,15},{4,52},{5,9},{6,54},{7,11},{8,56},{9,5... | collective-permute-start | bytes 350216 | tf_op jit(solution)/shard_map/ppermute | solution.py:47
  20.7 2.5 %collective-permute-start.9 = (bf16[8,7296]{1,0:T(8,128)(2,1)S(1)}, bf16[8,7296]{1,0:T(8,128)(2,1)S(1)}, u32[]{:S(2)}, u32[]{:S(2)}) collective-permute-start(bf16[8,7296]{1,0:T(8,128)(2,1)S(1)} %collective-permute-done.5), channel_id=1, source_target_pairs={{0,48},{1,13},{2,50},{3,15},{4,52},{5,9},{6,54},{7,11},{8,56},{9,5... | collective-permute-start | bytes 350216 | tf_op jit(solution)/shard_map/ppermute | solution.py:47
  23.4 1.9 %collective-permute-done.7 = bf16[8,7296]{1,0:T(8,128)(2,1)S(1)} collective-permute-done((bf16[8,7296]{1,0:T(8,128)(2,1)S(1)}, bf16[8,7296]{1,0:T(8,128)(2,1)S(1)}, u32[]{:S(2)}, u32[]{:S(2)}) %collective-permute-start.7) | collective-permute-done | bytes 116768 | tf_op jit(solution)/shard_map/ppermute | solution.py:47
  28.2 1.8 %collective-permute-start.13 = (bf16[32,7296]{1,0:T(8,128)(2,1)S(1)}, bf16[32,7296]{1,0:T(8,128)(2,1)S(1)}, u32[]{:S(2)}, u32[]{:S(2)}) collective-permute-start(bf16[32,7296]{1,0:T(8,128)(2,1)S(1)} %pad_maximum_fusion.1.refs_1_), channel_id=1, source_target_pairs={{0,12},{1,49},{2,14},{3,51},{4,8},{5,53},{6,10},{7,55},{8,4},{9,57... | collective-permute-start | bytes 1400840 | tf_op jit(solution)/shard_map/ppermute | solution.py:47
  31.5 3.5 %collective-permute-done.12.refs_2_ = bf16[32,7296]{1,0:T(8,128)(2,1)S(1)} collective-permute-done((bf16[32,7296]{1,0:T(8,128)(2,1)S(1)}, bf16[32,7296]{1,0:T(8,128)(2,1)S(1)}, u32[]{:S(2)}, u32[]{:S(2)}) %collective-permute-start.12) | collective-permute-done | bytes 466976 | tf_op jit(solution)/shard_map/ppermute | solution.py:47
  35.0 2.1 %collective-permute-done.13.refs_5_ = bf16[32,7296]{1,0:T(8,128)(2,1)S(1)} collective-permute-done((bf16[32,7296]{1,0:T(8,128)(2,1)S(1)}, bf16[32,7296]{1,0:T(8,128)(2,1)S(1)}, u32[]{:S(2)}, u32[]{:S(2)}) %collective-permute-start.13) | collective-permute-done | bytes 466976 | tf_op jit(solution)/shard_map/ppermute | solution.py:47
  37.1 1.8 %collective-permute-start.16 = (bf16[32,7296]{1,0:T(8,128)(2,1)S(1)}, bf16[32,7296]{1,0:T(8,128)(2,1)S(1)}, u32[]{:S(2)}, u32[]{:S(2)}) collective-permute-start(bf16[32,7296]{1,0:T(8,128)(2,1)S(1)} %collective-permute-done.12.refs_2_), channel_id=1, source_target_pairs={{0,12},{1,49},{2,14},{3,51},{4,8},{5,53},{6,10},{7,55},{8,4},{9,57... | collective-permute-start | bytes 1400840 | tf_op jit(solution)/shard_map/ppermute | solution.py:47
  39.0 3.2 %collective-permute-done.15.refs_4_ = bf16[32,7296]{1,0:T(8,128)(2,1)S(1)} collective-permute-done((bf16[32,7296]{1,0:T(8,128)(2,1)S(1)}, bf16[32,7296]{1,0:T(8,128)(2,1)S(1)}, u32[]{:S(2)}, u32[]{:S(2)}) %collective-permute-start.15) | collective-permute-done | bytes 466976 | tf_op jit(solution)/shard_map/ppermute | solution.py:47
  42.1 5.0 %collective-permute-done.16.refs_6_ = bf16[32,7296]{1,0:T(8,128)(2,1)S(1)} collective-permute-done((bf16[32,7296]{1,0:T(8,128)(2,1)S(1)}, bf16[32,7296]{1,0:T(8,128)(2,1)S(1)}, u32[]{:S(2)}, u32[]{:S(2)}) %collective-permute-start.16) | collective-permute-done | bytes 466976 | tf_op jit(solution)/shard_map/ppermute | solution.py:47
  47.1 5.3 %shard_map.177 = (bf16[32,7168]{1,0:T(8,128)(2,1)S(1)}, bf16[32,7168]{1,0:T(8,128)(2,1)S(1)}, bf16[32,7168]{1,0:T(8,128)(2,1)S(1)}, bf16[32,7168]{1,0:T(8,128)(2...) custom-call(s32[3]{0:T(128)S(1)} %pad_add_fusion.place_ref, ...), custom_call_target="tpu_custom_call" | custom-call | flops 5637144576 | bytes 22020096 | tf_op jit(solution)/shard_map/pallas_call | solution.py:393
  52.6 4.1 %collective-permute-start.32 = (bf16[576,3584]{1,0:T(8,128)(2,1)S(1)}, bf16[576,3584]{1,0:T(8,128)(2,1)S(1)}, u32[]{:S(2)}, u32[]{:S(2)}) collective-permute-start(bf16[576,3584]{1,0:T(8,128)(2,1)S(1)} %bitcast.10), channel_id=1, source_target_pairs={{0,1},{1,0},{2,3},{3,2},{4,5},{5,4},{6,7},{7,6},{8,9},{9,8},{10,11... | collective-permute-start | bytes 12386312 | tf_op jit(solution)/shard_map/ppermute | solution.py:47
  60.3 1.9 %collective-permute-start.23 = (bf16[32,7168]{1,0:T(8,128)(2,1)S(1)}, bf16[32,7168]{1,0:T(8,128)(2,1)S(1)}, u32[]{:S(2)}, u32[]{:S(2)}) collective-permute-start(bf16[32,7168]{1,0:T(8,128)(2,1)S(1)} %add_convert_fusion.1), channel_id=1, source_target_pairs={{0,12},{1,49},{2,14},{3,51},{4,8},{5,53},{6,10},{7,55},{8,4},{9,57... | collective-permute-start | bytes 1376264 | tf_op jit(solution)/shard_map/ppermute | solution.py:47
  62.2 3.3 %collective-permute-done.18 = bf16[32,7168]{1,0:T(8,128)(2,1)S(1)} collective-permute-done((bf16[32,7168]{1,0:T(8,128)(2,1)S(1)}, bf16[32,7168]{1,0:T(8,128)(2,1)S(1)}, u32[]{:S(2)}, u32[]{:S(2)}) %collective-permute-start.18) | collective-permute-done | bytes 458784 | tf_op jit(solution)/shard_map/ppermute | solution.py:47
  67.0 8.4 %collective-permute-done.23 = bf16[32,7168]{1,0:T(8,128)(2,1)S(1)} collective-permute-done((bf16[32,7168]{1,0:T(8,128)(2,1)S(1)}, bf16[32,7168]{1,0:T(8,128)(2,1)S(1)}, u32[]{:S(2)}, u32[]{:S(2)}) %collective-permute-start.23) | collective-permute-done | bytes 458784 | tf_op jit(solution)/shard_map/ppermute | solution.py:47
  82.2 2.3 %collective-permute-done.30 = bf16[8,7168]{1,0:T(8,128)(2,1)S(1)} collective-permute-done((bf16[8,7168]{1,0:T(8,128)(2,1)S(1)}, bf16[8,7168]{1,0:T(8,128)(2,1)S(1)}, u32[]{:S(2)}, u32[]{:S(2)}) %collective-permute-start.30) | collective-permute-done | bytes 114720 | tf_op jit(solution)/shard_map/ppermute | solution.py:47
  85.0 3.5 %collective-permute-start.31 = (bf16[8,7168]{1,0:T(8,128)(2,1)S(1)}, bf16[8,7168]{1,0:T(8,128)(2,1)S(1)}, u32[]{:S(2)}, u32[]{:S(2)}) collective-permute-start(bf16[8,7168]{1,0:T(8,128)(2,1)S(1)} %get-tuple-element.78), channel_id=1, source_target_pairs={{0,64},{1,65},{2,66},{3,67},{4,68},{5,69},{6,70},{7,71},{8,72},{9,... | collective-permute-start | bytes 344072 | tf_op jit(solution)/shard_map/ppermute | solution.py:47
  88.6 4.1 %collective-permute-start.27 = (bf16[8,7168]{1,0:T(8,128)(2,1)S(1)}, bf16[8,7168]{1,0:T(8,128)(2,1)S(1)}, u32[]{:S(2)}, u32[]{:S(2)}) collective-permute-start(bf16[8,7168]{1,0:T(8,128)(2,1)S(1)} %add_convert_fusion.6), channel_id=1, source_target_pairs={{0,66},{1,67},{2,64},{3,65},{4,70},{5,71},{6,68},{7,69},{8,74},{9,... | collective-permute-start | bytes 344072 | tf_op jit(solution)/shard_map/ppermute | solution.py:47
  92.8 2.7 %collective-permute-done.27.back_flip = bf16[8,7168]{1,0:T(8,128)(2,1)S(1)} collective-permute-done((bf16[8,7168]{1,0:T(8,128)(2,1)S(1)}, bf16[8,7168]{1,0:T(8,128)(2,1)S(1)}, u32[]{:S(2)}, u32[]{:S(2)}) %collective-permute-start.27) | collective-permute-done | bytes 114720 | tf_op jit(solution)/shard_map/ppermute | solution.py:47
  95.5 2.9 %shard_map.178 = (bf16[8,7168]{1,0:T(8,128)(2,1)S(1)}, bf16[8,576]{1,0:T(8,128)(2,1)S(1)}) custom-call(s32[3]{0:T(128)S(1)} %pad_add_fusion.place_ref, bf16[1,16,7168]{2,1,0:T(8,128)(2,1)S(1)} %copy-done.2, bf16[8,7168]{1,0:T(8,128)(2,1)S(1)} %collective-permute-done.27.back_flip, bf16[8,7168]{1,0:T(8,128)(2,1)S(1)} %collective-permute-done.31.back_straight, ...), custom_call_target="tpu_custom_call" | custom-call | tf_op jit(solution)/shard_map/pallas_call | solution.py:145
  98.4 4.2 %collective-permute-start.34 = (bf16[8,7168]{1,0:T(8,128)(2,1)S(1)}, bf16[8,7168]{1,0:T(8,128)(2,1)S(1)}, u32[]{:S(2)}, u32[]{:S(2)}) collective-permute-start(bf16[8,7168]{1,0:T(8,128)(2,1)S(1)} %get-tuple-element.73.updated_own), channel_id=1, source_target_pairs={{0,1},{1,0},{2,3},{3,2},{4,5},{5,4},{6,7},{7,6},{8,9},{9,8},{10,11... | collective-permute-start | bytes 344072 | tf_op jit(solution)/shard_map/ppermute | solution.py:47
  103.8 1.9 %shard_map.179 = (bf16[1,16,7168]{2,1,0:T(8,128)(2,1)}, bf16[1,16,512]{2,1,0:T(8,128)(2,1)}, bf16[1,16,64]{2,1,0:T(8,128)(2,1)}, bf16[1,16,32,512]{3,2,1,0:T(8,128)(2,1)}) custom-call(s32[3]{0:T(128)S(1)} %pad_add_fusion.place_ref, bf16[8,576]{1,0:T(8,128)(2,1)S(1)} %get-tuple-element.72.fresh_own, bf16[8,576]{1,0:T(8,128)(2,1)S(1)} %collective-permute-done.33.fresh_other, ...), custom_call_target="tpu_custom_call" | custom-call | tf_op jit(solution)/shard_map/pallas_call | solution.py:145
  (83 shorter events, 28.6 us)
Async XLA Ops:
  0.7 13.4 %collective-permute-start.3 = (bf16[7168,256]{1,0:T(8,128)(2,1)}, bf16[7168,256]{1,0:T(8,128)(2,1)S(1)}, u32[]{:S(2)}, u32[]{:S(2)}) collective-permute-start(bf16[7168,256]{1,0:T(8,128)(2,1)} %bitcast.12), channel_id=1, source_target_pairs={{0,1},{1,0},{2,3},{3,2},{4,5},{5,4},{6,7},{7,6},{8,9},{9,8},{10,11... | collective-permute-start | bytes 11010056 | tf_op jit(solution)/shard_map/ppermute | solution.py:47
  2.2 11.9 %collective-permute-start.4 = (bf16[7168,256]{1,0:T(8,128)(2,1)}, bf16[7168,256]{1,0:T(8,128)(2,1)S(1)}, u32[]{:S(2)}, u32[]{:S(2)}) collective-permute-start(bf16[7168,256]{1,0:T(8,128)(2,1)} %bitcast.14), channel_id=1, source_target_pairs={{0,1},{1,0},{2,3},{3,2},{4,5},{5,4},{6,7},{7,6},{8,9},{9,8},{10,11... | collective-permute-start | bytes 11010056 | tf_op jit(solution)/shard_map/ppermute | solution.py:47
  5.5 8.2 %collective-permute-start.1 = (bf16[8,7296]{1,0:T(8,128)(2,1)S(1)}, bf16[8,7296]{1,0:T(8,128)(2,1)S(1)}, u32[]{:S(2)}, u32[]{:S(2)}) collective-permute-start(bf16[8,7296]{1,0:T(8,128)(2,1)S(1)} %shard_map.174), channel_id=1, source_target_pairs={{0,64},{1,65},{2,66},{3,67},{4,68},{5,69},{6,70},{7,71},{8,72},{9,... | collective-permute-start | bytes 350216 | tf_op jit(solution)/shard_map/ppermute | solution.py:47
  8.6 5.5 %collective-permute-start = (bf16[8,7296]{1,0:T(8,128)(2,1)S(1)}, bf16[8,7296]{1,0:T(8,128)(2,1)S(1)}, u32[]{:S(2)}, u32[]{:S(2)}) collective-permute-start(bf16[8,7296]{1,0:T(8,128)(2,1)S(1)} %shard_map.174), channel_id=1, source_target_pairs={{0,66},{1,67},{2,64},{3,65},{4,70},{5,71},{6,68},{7,69},{8,74},{9,... | collective-permute-start | bytes 350216 | tf_op jit(solution)/shard_map/ppermute | solution.py:47
  14.1 13.1 %collective-permute-start.11 = (bf16[256,7168]{1,0:T(8,128)(2,1)S(1)}, bf16[256,7168]{1,0:T(8,128)(2,1)S(1)}, u32[]{:S(2)}, u32[]{:S(2)}) collective-permute-start(bf16[256,7168]{1,0:T(8,128)(2,1)S(1)} %bitcast.17), channel_id=1, source_target_pairs={{0,1},{1,0},{2,3},{3,2},{4,5},{5,4},{6,7},{7,6},{8,9},{9,8},{10,11... | collective-permute-start | bytes 11010056 | tf_op jit(solution)/shard_map/ppermute | solution.py:47
  17.1 6.1 %collective-permute-start.8 = (bf16[8,7296]{1,0:T(8,128)(2,1)S(1)}, bf16[8,7296]{1,0:T(8,128)(2,1)S(1)}, u32[]{:S(2)}, u32[]{:S(2)}) collective-permute-start(bf16[8,7296]{1,0:T(8,128)(2,1)S(1)} %collective-permute-done.1), channel_id=1, source_target_pairs={{0,48},{1,13},{2,50},{3,15},{4,52},{5,9},{6,54},{7,11},{8,56},{9,5... | collective-permute-start | bytes 350216 | tf_op jit(solution)/shard_map/ppermute | solution.py:47
  20.7 5.8 %collective-permute-start.9 = (bf16[8,7296]{1,0:T(8,128)(2,1)S(1)}, bf16[8,7296]{1,0:T(8,128)(2,1)S(1)}, u32[]{:S(2)}, u32[]{:S(2)}) collective-permute-start(bf16[8,7296]{1,0:T(8,128)(2,1)S(1)} %collective-permute-done.5), channel_id=1, source_target_pairs={{0,48},{1,13},{2,50},{3,15},{4,52},{5,9},{6,54},{7,11},{8,56},{9,5... | collective-permute-start | bytes 350216 | tf_op jit(solution)/shard_map/ppermute | solution.py:47
  27.2 7.8 %collective-permute-start.12 = (bf16[32,7296]{1,0:T(8,128)(2,1)S(1)}, bf16[32,7296]{1,0:T(8,128)(2,1)S(1)}, u32[]{:S(2)}, u32[]{:S(2)}) collective-permute-start(bf16[32,7296]{1,0:T(8,128)(2,1)S(1)} %pad_maximum_fusion.refs_0_), channel_id=1, source_target_pairs={{0,4},{1,17},{2,6},{3,19},{4,0},{5,21},{6,2},{7,23},{8,12},{9,25},... | collective-permute-start | bytes 1400840 | tf_op jit(solution)/shard_map/ppermute | solution.py:47
  28.2 8.9 %collective-permute-start.13 = (bf16[32,7296]{1,0:T(8,128)(2,1)S(1)}, bf16[32,7296]{1,0:T(8,128)(2,1)S(1)}, u32[]{:S(2)}, u32[]{:S(2)}) collective-permute-start(bf16[32,7296]{1,0:T(8,128)(2,1)S(1)} %pad_maximum_fusion.1.refs_1_), channel_id=1, source_target_pairs={{0,12},{1,49},{2,14},{3,51},{4,8},{5,53},{6,10},{7,55},{8,4},{9,57... | collective-permute-start | bytes 1400840 | tf_op jit(solution)/shard_map/ppermute | solution.py:47
  30.6 11.5 %collective-permute-start.15 = (bf16[32,7296]{1,0:T(8,128)(2,1)S(1)}, bf16[32,7296]{1,0:T(8,128)(2,1)S(1)}, u32[]{:S(2)}, u32[]{:S(2)}) collective-permute-start(bf16[32,7296]{1,0:T(8,128)(2,1)S(1)} %pad_maximum_fusion.refs_0_), channel_id=1, source_target_pairs={{0,12},{1,49},{2,14},{3,51},{4,8},{5,53},{6,10},{7,55},{8,4},{9,57... | collective-permute-start | bytes 1400840 | tf_op jit(solution)/shard_map/ppermute | solution.py:47
  31.5 10.6 %collective-permute-start.14 = (bf16[32,7296]{1,0:T(8,128)(2,1)S(1)}, bf16[32,7296]{1,0:T(8,128)(2,1)S(1)}, u32[]{:S(2)}, u32[]{:S(2)}) collective-permute-start(bf16[32,7296]{1,0:T(8,128)(2,1)S(1)} %pad_maximum_fusion.1.refs_1_), channel_id=1, source_target_pairs={{0,4},{1,17},{2,6},{3,19},{4,0},{5,21},{6,2},{7,23},{8,12},{9,25},... | collective-permute-start | bytes 1400840 | tf_op jit(solution)/shard_map/ppermute | solution.py:47
  37.1 10.0 %collective-permute-start.16 = (bf16[32,7296]{1,0:T(8,128)(2,1)S(1)}, bf16[32,7296]{1,0:T(8,128)(2,1)S(1)}, u32[]{:S(2)}, u32[]{:S(2)}) collective-permute-start(bf16[32,7296]{1,0:T(8,128)(2,1)S(1)} %collective-permute-done.12.refs_2_), channel_id=1, source_target_pairs={{0,12},{1,49},{2,14},{3,51},{4,8},{5,53},{6,10},{7,55},{8,4},{9,57... | collective-permute-start | bytes 1400840 | tf_op jit(solution)/shard_map/ppermute | solution.py:47
  39.0 8.2 %collective-permute-start.17 = (bf16[32,7296]{1,0:T(8,128)(2,1)S(1)}, bf16[32,7296]{1,0:T(8,128)(2,1)S(1)}, u32[]{:S(2)}, u32[]{:S(2)}) collective-permute-start(bf16[32,7296]{1,0:T(8,128)(2,1)S(1)} %collective-permute-done.13.refs_5_), channel_id=1, source_target_pairs={{0,4},{1,17},{2,6},{3,19},{4,0},{5,21},{6,2},{7,23},{8,12},{9,25},... | collective-permute-start | bytes 1400840 | tf_op jit(solution)/shard_map/ppermute | solution.py:47
  52.5 7.7 %collective-permute-start.22 = (bf16[32,7168]{1,0:T(8,128)(2,1)S(1)}, bf16[32,7168]{1,0:T(8,128)(2,1)S(1)}, u32[]{:S(2)}, u32[]{:S(2)}) collective-permute-start(bf16[32,7168]{1,0:T(8,128)(2,1)S(1)} %get-tuple-element.67), channel_id=1, source_target_pairs={{0,4},{1,17},{2,6},{3,19},{4,0},{5,21},{6,2},{7,23},{8,12},{9,25},... | collective-permute-start | bytes 1376264 | tf_op jit(solution)/shard_map/ppermute | solution.py:47
  52.6 42.9 %collective-permute-start.32 = (bf16[576,3584]{1,0:T(8,128)(2,1)S(1)}, bf16[576,3584]{1,0:T(8,128)(2,1)S(1)}, u32[]{:S(2)}, u32[]{:S(2)}) collective-permute-start(bf16[576,3584]{1,0:T(8,128)(2,1)S(1)} %bitcast.10), channel_id=1, source_target_pairs={{0,1},{1,0},{2,3},{3,2},{4,5},{5,4},{6,7},{7,6},{8,9},{9,8},{10,11... | collective-permute-start | bytes 12386312 | tf_op jit(solution)/shard_map/ppermute | solution.py:47
  56.7 8.8 %collective-permute-start.18 = (bf16[32,7168]{1,0:T(8,128)(2,1)S(1)}, bf16[32,7168]{1,0:T(8,128)(2,1)S(1)}, u32[]{:S(2)}, u32[]{:S(2)}) collective-permute-start(bf16[32,7168]{1,0:T(8,128)(2,1)S(1)} %get-tuple-element.62), channel_id=1, source_target_pairs={{0,12},{1,49},{2,14},{3,51},{4,8},{5,53},{6,10},{7,55},{8,4},{9,57... | collective-permute-start | bytes 1376264 | tf_op jit(solution)/shard_map/ppermute | solution.py:47
  58.2 18.8 %collective-permute-start.20 = (bf16[32,7168]{1,0:T(8,128)(2,1)S(1)}, bf16[32,7168]{1,0:T(8,128)(2,1)S(1)}, u32[]{:S(2)}, u32[]{:S(2)}) collective-permute-start(bf16[32,7168]{1,0:T(8,128)(2,1)S(1)} %get-tuple-element.63), channel_id=1, source_target_pairs={{0,12},{1,49},{2,14},{3,51},{4,8},{5,53},{6,10},{7,55},{8,4},{9,57... | collective-permute-start | bytes 1376264 | tf_op jit(solution)/shard_map/ppermute | solution.py:47
  59.4 7.6 %collective-permute-start.21 = (bf16[32,7168]{1,0:T(8,128)(2,1)S(1)}, bf16[32,7168]{1,0:T(8,128)(2,1)S(1)}, u32[]{:S(2)}, u32[]{:S(2)}) collective-permute-start(bf16[32,7168]{1,0:T(8,128)(2,1)S(1)} %get-tuple-element.65), channel_id=1, source_target_pairs={{0,4},{1,17},{2,6},{3,19},{4,0},{5,21},{6,2},{7,23},{8,12},{9,25},... | collective-permute-start | bytes 1376264 | tf_op jit(solution)/shard_map/ppermute | solution.py:47
  60.3 15.0 %collective-permute-start.23 = (bf16[32,7168]{1,0:T(8,128)(2,1)S(1)}, bf16[32,7168]{1,0:T(8,128)(2,1)S(1)}, u32[]{:S(2)}, u32[]{:S(2)}) collective-permute-start(bf16[32,7168]{1,0:T(8,128)(2,1)S(1)} %add_convert_fusion.1), channel_id=1, source_target_pairs={{0,12},{1,49},{2,14},{3,51},{4,8},{5,53},{6,10},{7,55},{8,4},{9,57... | collective-permute-start | bytes 1376264 | tf_op jit(solution)/shard_map/ppermute | solution.py:47
  65.6 11.4 %collective-permute-start.19 = (bf16[32,7168]{1,0:T(8,128)(2,1)S(1)}, bf16[32,7168]{1,0:T(8,128)(2,1)S(1)}, u32[]{:S(2)}, u32[]{:S(2)}) collective-permute-start(bf16[32,7168]{1,0:T(8,128)(2,1)S(1)} %add_convert_fusion.3), channel_id=1, source_target_pairs={{0,4},{1,17},{2,6},{3,19},{4,0},{5,21},{6,2},{7,23},{8,12},{9,25},... | collective-permute-start | bytes 1376264 | tf_op jit(solution)/shard_map/ppermute | solution.py:47
  80.7 7.8 %collective-permute-start.26 = (bf16[8,7168]{1,0:T(8,128)(2,1)S(1)}, bf16[8,7168]{1,0:T(8,128)(2,1)S(1)}, u32[]{:S(2)}, u32[]{:S(2)}) collective-permute-start(bf16[8,7168]{1,0:T(8,128)(2,1)S(1)} %get-tuple-element.81), channel_id=1, source_target_pairs={{0,48},{1,13},{2,50},{3,15},{4,52},{5,9},{6,54},{7,11},{8,56},{9,5... | collective-permute-start | bytes 344072 | tf_op jit(solution)/shard_map/ppermute | solution.py:47
  85.0 7.8 %collective-permute-start.31 = (bf16[8,7168]{1,0:T(8,128)(2,1)S(1)}, bf16[8,7168]{1,0:T(8,128)(2,1)S(1)}, u32[]{:S(2)}, u32[]{:S(2)}) collective-permute-start(bf16[8,7168]{1,0:T(8,128)(2,1)S(1)} %get-tuple-element.78), channel_id=1, source_target_pairs={{0,64},{1,65},{2,66},{3,67},{4,68},{5,69},{6,70},{7,71},{8,72},{9,... | collective-permute-start | bytes 344072 | tf_op jit(solution)/shard_map/ppermute | solution.py:47
  88.6 6.9 %collective-permute-start.27 = (bf16[8,7168]{1,0:T(8,128)(2,1)S(1)}, bf16[8,7168]{1,0:T(8,128)(2,1)S(1)}, u32[]{:S(2)}, u32[]{:S(2)}) collective-permute-start(bf16[8,7168]{1,0:T(8,128)(2,1)S(1)} %add_convert_fusion.6), channel_id=1, source_target_pairs={{0,66},{1,67},{2,64},{3,65},{4,70},{5,71},{6,68},{7,69},{8,74},{9,... | collective-permute-start | bytes 344072 | tf_op jit(solution)/shard_map/ppermute | solution.py:47
  98.4 5.4 %collective-permute-start.34 = (bf16[8,7168]{1,0:T(8,128)(2,1)S(1)}, bf16[8,7168]{1,0:T(8,128)(2,1)S(1)}, u32[]{:S(2)}, u32[]{:S(2)}) collective-permute-start(bf16[8,7168]{1,0:T(8,128)(2,1)S(1)} %get-tuple-element.73.updated_own), channel_id=1, source_target_pairs={{0,1},{1,0},{2,3},{3,2},{4,5},{5,4},{6,7},{7,6},{8,9},{9,8},{10,11... | collective-permute-start | bytes 344072 | tf_op jit(solution)/shard_map/ppermute | solution.py:47
  (19 other events, 197.3 us)

commit v5 on v4

--- a/solution.py
+++ b/solution.py
@@ -151,12 +151,12 @@
     )(scalars, *hold(operands))
 
 
-def front_kernel(place_ref, residual_hbm, gain_hbm, router_hbm, routes, out, *scratch):
-    residual, gain, router, arrived = scratch
+def front_kernel(place_ref, residual_hbm, gain_hbm, router_hbm, routes_hbm, out, *scratch):
+    residual, gain, router, routes, arrived = scratch
     copies = [
         pltpu.make_async_copy(source, target, arrived.at[k])
         for k, (source, target) in enumerate(
-            ((residual_hbm, residual), (gain_hbm, gain), (router_hbm, router))
+            ((residual_hbm, residual), (gain_hbm, gain), (router_hbm, router), (routes_hbm, routes))
         )
     ]
     for copy in copies:
@@ -191,22 +191,23 @@
 
 def front(place, residual, moe_gain, router, routes):
     shape = (residual.shape[1] // 2, residual.shape[2] + WEIGHT_LANES)
+    routes = jnp.swapaxes(routes, 1, 2)
     anywhere = pl.BlockSpec(memory_space=pltpu.HBM)
     return pl.pallas_call(
         front_kernel,
         out_shape=jax.ShapeDtypeStruct(shape, BF16),
         in_specs=[pl.BlockSpec(memory_space=pltpu.SMEM)]
-        + [anywhere] * 3
-        + [pl.BlockSpec(memory_space=pltpu.VMEM)],
+        + [anywhere] * 4,
         out_specs=pl.BlockSpec(memory_space=pltpu.VMEM),
         scratch_shapes=[
             pltpu.VMEM(residual.shape, BF16),
             pltpu.VMEM(moe_gain.shape, BF16),
             pltpu.VMEM(router.shape, BF16),
-            pltpu.SemaphoreType.DMA((3,)),
+            pltpu.VMEM(routes.shape, jnp.int32),
+            pltpu.SemaphoreType.DMA((4,)),
         ],
         compiler_params=pltpu.CompilerParams(vmem_limit_bytes=KERNEL_VMEM),
-    )(place, *hold((residual, moe_gain, router), pltpu.HBM), jnp.swapaxes(routes, 1, 2))
+    )(place, *hold((residual, moe_gain, router, routes), pltpu.HBM))
 
 
 def project_kernel(
@@ -341,13 +342,20 @@
         mass[t] = jnp.broadcast_to(total[own], mass.shape[1:])
 
 
+def hidden_units(pieces, weights):
+    sums = None
+    for start in range(0, weights[0].shape[0], CHUNK):
+        span = slice(start, start + CHUNK)
+        rows = jnp.concatenate([piece[:, span] for piece in pieces], axis=0)
+        parts = [dot(rows, weight[span, :]) for weight in weights]
+        sums = parts if sums is None else [a + b for a, b in zip(sums, parts)]
+    return [(sums[k] / (1.0 + jnp.exp(-sums[k])) * sums[2 + k]).astype(BF16) for k in range(2)]
+
+
 def roles_kernel(place_ref, lengths, *refs):
-    pieces, weights, far = refs[0:8], refs[8:14], refs[14:18]
-    outs, cached = refs[18:26], refs[26:30]
-    near, arrived = refs[30:34], refs[34]
-    down_a, down_b = weights[4:]
-    width, model_width = down_a.shape
-    spans = [slice(start, start + CHUNK) for start in range(0, model_width, CHUNK)]
+    pieces, weights, far = refs[0:6], refs[6:10], refs[10:14]
+    hidden, cached, near, arrived = refs[14], refs[15:19], refs[19:23], refs[23]
+    width = weights[0].shape[1]
 
     @pl.when(place_ref[0] == 0)
     def _():
@@ -363,50 +371,57 @@
 
     @pl.when(place_ref[0] == 1)
     def _():
-        sums = None
-        for span in spans:
-            rows = jnp.concatenate([piece[:, span] for piece in pieces], axis=0)
-            parts = [dot(rows, weight[span, :]) for weight in weights[:4]]
-            sums = parts if sums is None else [a + b for a, b in zip(sums, parts)]
-        hidden = [
-            (sums[k] / (1.0 + jnp.exp(-sums[k])) * sums[2 + k]).astype(BF16) for k in range(2)
-        ]
-        lanes = jnp.concatenate([piece[:, model_width:] for piece in pieces], axis=0).astype(F32)
-        mine = lax.broadcasted_iota(jnp.int32, lanes.shape, 1) == place_ref[2]
-        scale = jnp.sum(jnp.where(mine, lanes, 0.0), axis=1, keepdims=True)
-        for span in spans:
-            total = dot(hidden[0], down_a[:, span]) + dot(hidden[1], down_b[:, span])
-            answer = (total * scale).astype(BF16)
-            for k, out in enumerate(outs):
-                size = out.shape[0]
-                out[:, span] = answer[k * size : (k + 1) * size]
+        hidden[:, :width], hidden[:, width:] = hidden_units(pieces, weights)
 
 
 def roles(place, lengths, pieces, weights, attended):
-    model_width = weights[0].shape[0]
+    model_width, width = weights[0].shape
+    rows = sum(piece.shape[0] for piece in pieces)
     _, tokens, heads, latent = attended[0].shape
     rope = attended[3].shape[2]
     smem = pl.BlockSpec(memory_space=pltpu.SMEM)
     inside = pl.BlockSpec(memory_space=pltpu.VMEM)
     anywhere = pl.BlockSpec(memory_space=pltpu.HBM)
     wide = jax.ShapeDtypeStruct((tokens, heads, WEIGHT_LANES), F32)
-    results = pl.pallas_call(
+    hidden, *cached = pl.pallas_call(
         roles_kernel,
-        out_shape=[jax.ShapeDtypeStruct((piece.shape[0], model_width), BF16) for piece in pieces]
+        out_shape=[jax.ShapeDtypeStruct((rows, 2 * width), BF16)]
         + [jax.ShapeDtypeStruct((tokens, heads, latent), F32), wide, wide]
         + [jax.ShapeDtypeStruct((tokens, heads, rope), BF16)],
-        in_specs=[smem, smem] + [inside] * 14 + [anywhere] * 4,
-        out_specs=[inside] * 12,
+        in_specs=[smem, smem] + [inside] * 10 + [anywhere] * 4,
+        out_specs=[inside] * 5,
         scratch_shapes=[pltpu.VMEM(value.shape[1:], BF16) for value in attended]
         + [pltpu.SemaphoreType.DMA((4,))],
         compiler_params=pltpu.CompilerParams(vmem_limit_bytes=ROLES_VMEM),
         cost_estimate=pl.CostEstimate(
-            flops=3072 * model_width * weights[0].shape[1],
-            bytes_accessed=12 * model_width * weights[0].shape[1],
+            flops=8 * rows * model_width * width,
+            bytes_accessed=8 * model_width * width,
             transcendentals=0,
         ),
     )(place, lengths, *hold(pieces), *hold(weights), *hold(attended, pltpu.HBM))
-    return results[:8], results[8:]
+    return hidden, cached
+
+
+def answer_kernel(place_ref, *refs):
+    pieces, near, weights, outs = refs[0:8], refs[8], refs[9:15], refs[15:23]
+    down_a, down_b = weights[4:]
+    width, model_width = down_a.shape
+
+    @pl.when(place_ref[0] == 1)
+    def _():
+        late = hidden_units(pieces[6:], weights[:4])
+        early = near[:, :width], near[:, width:]
+        hidden = [jnp.concatenate(parts, axis=0) for parts in zip(early, late)]
+        lanes = jnp.concatenate([piece[:, model_width:] for piece in pieces], axis=0).astype(F32)
+        mine = lax.broadcasted_iota(jnp.int32, lanes.shape, 1) == place_ref[2]
+        scale = jnp.sum(jnp.where(mine, lanes, 0.0), axis=1, keepdims=True)
+        for start in range(0, model_width, CHUNK):
+            span = slice(start, start + CHUNK)
+            total = dot(hidden[0], down_a[:, span]) + dot(hidden[1], down_b[:, span])
+            answer = (total * scale).astype(BF16)
+            for k, out in enumerate(outs):
+                size = out.shape[0]
+                out[:, span] = answer[k * size : (k + 1) * size]
 
 
 def rms_scale(values):
@@ -465,12 +480,14 @@
     kv_other = send(kv_own, other_core)
     *pieces, downs = gather_ring(*column, 1, stage(1, place, (down_own,)))
 
-    answers, cached = roles(
+    gates = (gates[0], gate_other, gates[1], up_other)
+    attended = (query_latent, query_rope, cache_latent, cache_rope)
+    hidden, cached = roles(place, lengths, pieces[:6], gates, attended)
+    answers = call_inside(
+        answer_kernel,
+        [jax.ShapeDtypeStruct((piece.shape[0], model_width), BF16) for piece in pieces],
         place,
-        lengths,
-        pieces,
-        (gates[0], gate_other, gates[1], up_other, downs[0], down_other),
-        (query_latent, query_rope, cache_latent, cache_rope),
+        (*pieces, hidden, *gates, downs[0], down_other),
     )
     back_flip, back_straight = scatter_ring(split_pairs(*scatter_ring(answers, 1)), 0)
     back_flip = send(back_flip, across(1))

time: 106 us -> 104 us (0.981)
  waiting for transfers between devices: 40.8 us -> 36.2 us
  starting transfers between devices: 47.9 us -> 49.3 us
    ppermute x35, waiting for transfers between devices: 40.8 us -> 36.2 us  [send(): return lax.ppermute(value, AXES, pairs_of(partner))]
    ppermute x35, starting transfers between devices: 47.9 us -> 49.3 us  [send(): return lax.ppermute(value, AXES, pairs_of(partner))]
    pallas_call x2 -> x3, Pallas kernels: 4.81 us -> 5.55 us  [call_inside(): pl.pallas_call(kernel, out_shape=out_shapes, in_specs=[pl.BlockSpec(memor...]
  transfers between devices with their start and end apart: 35 -> 35, of which waited for: 20 -> 16; matrix products, arithmetic and copies ran while one was open for 2% -> 2% of each run, Pallas kernels for 3% -> 9%
where the time goes in v5:
time: 104 us
  starting transfers between devices  49.3 us (47%)
  waiting for transfers between devices  36.2 us (35%)
  Pallas kernels  14.4 us (14%)
  other arithmetic  1.63 us (2%)
  local copies, waits for them, and re-layouts  1.38 us (1%)
    ppermute x35, starting transfers between devices, send(): return lax.ppermute(value, AXES, pairs_of(partner))  49.3 us
    ppermute x35, waiting for transfers between devices, send(): return lax.ppermute(value, AXES, pairs_of(partner))  36.2 us
    pallas_call x3, Pallas kernels, call_inside(): pl.pallas_call(kernel, out_shape=out_shapes, in_specs=[pl.BlockSpec(memor...  5.55 us
    pallas_call x1, Pallas kernels, roles(): pl.pallas_call(roles_kernel, out_shape=[jax.ShapeDtypeStruct((rows, 2 * w...  5.16 us
    pallas_call x1, Pallas kernels, front(): pl.pallas_call(front_kernel, out_shape=jax.ShapeDtypeStruct(shape, BF16),...  2.55 us
  transfers between devices with their start and end apart: 35, of which 16 were waited for; matrix products, arithmetic and copies ran while one was open for 2% of the time, Pallas kernels for 9%

profile of v5, /device:TPU:1, one launch (start us, length us, event | category | flops | bytes accessed | tf_op | source)
XLA Modules:
  0.0 103.7 jit_solution(5558596196553192515)
XLA Ops:
  2.3 2.5 %shard_map.174 = bf16[8,7296]{1,0:T(8,128)(2,1)S(1)} custom-call(s32[3]{0:T(128)S(1)} %pad_add_fusion.place_ref, bf16[1,16,7168]{2,1,0:T(8,128)(2,1)} %residual.1, bf16[1,7168]{1,0:T(2,128)(2,1)} %gain_hbm.1, bf16[1,16,7168]{2,1,0:T(8,128)(2,1)} %router_hbm.1, s32[1,8,16]{2,1,0:T(8,128)} %bitcast.17), custom_call_target="tpu_custom_call" | custom-call | tf_op jit(solution)/shard_map/pallas_call | solution.py:196
  4.8 3.1 %collective-permute-start.1 = (bf16[8,7296]{1,0:T(8,128)(2,1)S(1)}, bf16[8,7296]{1,0:T(8,128)(2,1)S(1)}, u32[]{:S(2)}, u32[]{:S(2)}) collective-permute-start(bf16[8,7296]{1,0:T(8,128)(2,1)S(1)} %shard_map.174), channel_id=1, source_target_pairs={{0,64},{1,65},{2,66},{3,67},{4,68},{5,69},{6,70},{7,71},{8,72},{9,... | collective-permute-start | bytes 350216 | tf_op jit(solution)/shard_map/ppermute | solution.py:47
  11.0 2.7 %collective-permute-done.2.gain_other = bf16[1,3584]{1,0:T(2,128)(2,1)S(1)} collective-permute-done((bf16[1,3584]{1,0:T(2,128)(2,1)}, bf16[1,3584]{1,0:T(2,128)(2,1)S(1)}, u32[]{:S(2)}, u32[]{:S(2)}) %collective-permute-start.2) | collective-permute-done | bytes 7200 | tf_op jit(solution)/shard_map/ppermute | solution.py:47
  14.8 1.6 %collective-permute-start.5 = (bf16[8,7296]{1,0:T(8,128)(2,1)S(1)}, bf16[8,7296]{1,0:T(8,128)(2,1)S(1)}, u32[]{:S(2)}, u32[]{:S(2)}) collective-permute-start(bf16[8,7296]{1,0:T(8,128)(2,1)S(1)} %collective-permute-done), channel_id=1, source_target_pairs={{0,16},{1,5},{2,18},{3,7},{4,20},{5,1},{6,22},{7,3},{8,24},{9,13},... | collective-permute-start | bytes 350216 | tf_op jit(solution)/shard_map/ppermute | solution.py:47
  16.4 2.2 %collective-permute-start.8 = (bf16[8,7296]{1,0:T(8,128)(2,1)S(1)}, bf16[8,7296]{1,0:T(8,128)(2,1)S(1)}, u32[]{:S(2)}, u32[]{:S(2)}) collective-permute-start(bf16[8,7296]{1,0:T(8,128)(2,1)S(1)} %collective-permute-done.1), channel_id=1, source_target_pairs={{0,48},{1,13},{2,50},{3,15},{4,52},{5,9},{6,54},{7,11},{8,56},{9,5... | collective-permute-start | bytes 350216 | tf_op jit(solution)/shard_map/ppermute | solution.py:47
  20.0 2.5 %collective-permute-start.9 = (bf16[8,7296]{1,0:T(8,128)(2,1)S(1)}, bf16[8,7296]{1,0:T(8,128)(2,1)S(1)}, u32[]{:S(2)}, u32[]{:S(2)}) collective-permute-start(bf16[8,7296]{1,0:T(8,128)(2,1)S(1)} %collective-permute-done.5), channel_id=1, source_target_pairs={{0,48},{1,13},{2,50},{3,15},{4,52},{5,9},{6,54},{7,11},{8,56},{9,5... | collective-permute-start | bytes 350216 | tf_op jit(solution)/shard_map/ppermute | solution.py:47
  22.7 1.9 %collective-permute-done.7 = bf16[8,7296]{1,0:T(8,128)(2,1)S(1)} collective-permute-done((bf16[8,7296]{1,0:T(8,128)(2,1)S(1)}, bf16[8,7296]{1,0:T(8,128)(2,1)S(1)}, u32[]{:S(2)}, u32[]{:S(2)}) %collective-permute-start.7) | collective-permute-done | bytes 116768 | tf_op jit(solution)/shard_map/ppermute | solution.py:47
  27.5 1.8 %collective-permute-start.13 = (bf16[32,7296]{1,0:T(8,128)(2,1)S(1)}, bf16[32,7296]{1,0:T(8,128)(2,1)S(1)}, u32[]{:S(2)}, u32[]{:S(2)}) collective-permute-start(bf16[32,7296]{1,0:T(8,128)(2,1)S(1)} %pad_maximum_fusion.1.refs_1_), channel_id=1, source_target_pairs={{0,12},{1,49},{2,14},{3,51},{4,8},{5,53},{6,10},{7,55},{8,4},{9,57... | collective-permute-start | bytes 1400840 | tf_op jit(solution)/shard_map/ppermute | solution.py:47
  30.8 3.6 %collective-permute-done.12.refs_2_ = bf16[32,7296]{1,0:T(8,128)(2,1)S(1)} collective-permute-done((bf16[32,7296]{1,0:T(8,128)(2,1)S(1)}, bf16[32,7296]{1,0:T(8,128)(2,1)S(1)}, u32[]{:S(2)}, u32[]{:S(2)}) %collective-permute-start.12) | collective-permute-done | bytes 466976 | tf_op jit(solution)/shard_map/ppermute | solution.py:47
  34.3 2.1 %collective-permute-done.13.refs_5_ = bf16[32,7296]{1,0:T(8,128)(2,1)S(1)} collective-permute-done((bf16[32,7296]{1,0:T(8,128)(2,1)S(1)}, bf16[32,7296]{1,0:T(8,128)(2,1)S(1)}, u32[]{:S(2)}, u32[]{:S(2)}) %collective-permute-start.13) | collective-permute-done | bytes 466976 | tf_op jit(solution)/shard_map/ppermute | solution.py:47
  36.5 1.8 %collective-permute-start.16 = (bf16[32,7296]{1,0:T(8,128)(2,1)S(1)}, bf16[32,7296]{1,0:T(8,128)(2,1)S(1)}, u32[]{:S(2)}, u32[]{:S(2)}) collective-permute-start(bf16[32,7296]{1,0:T(8,128)(2,1)S(1)} %collective-permute-done.12.refs_2_), channel_id=1, source_target_pairs={{0,12},{1,49},{2,14},{3,51},{4,8},{5,53},{6,10},{7,55},{8,4},{9,57... | collective-permute-start | bytes 1400840 | tf_op jit(solution)/shard_map/ppermute | solution.py:47
  38.3 3.2 %collective-permute-done.15.refs_4_ = bf16[32,7296]{1,0:T(8,128)(2,1)S(1)} collective-permute-done((bf16[32,7296]{1,0:T(8,128)(2,1)S(1)}, bf16[32,7296]{1,0:T(8,128)(2,1)S(1)}, u32[]{:S(2)}, u32[]{:S(2)}) %collective-permute-start.15) | collective-permute-done | bytes 466976 | tf_op jit(solution)/shard_map/ppermute | solution.py:47
  41.5 5.2 %shard_map.177 = (bf16[192,512]{1,0:T(8,128)(2,1)S(1)}, f32[16,32,512]{2,1,0:T(8,128)S(1)}, f32[16,32,128]{2,1,0:T(8,128)S(1)}, f32[16,32,128]{2,1,0:T(8,128)S(1)}, bf16[16,32,64]{2,1,0:T(8,128)(2,1)S(1)}) custom-call(s32[3]{0:T(128)S(1)} %pad_add_fusion.place_ref, s32[1,16]{1,0:T(1,128)S(1)} %copy-done.5, bf16[32,7296]{1,0:T(8,128)(2,1)S(1)} %pad_maximum_fusion.refs_0_, ...), custom_call_target="tpu_custom_call" | custom-call | flops 2818572288 | bytes 14680064 | tf_op jit(solution)/shard_map/pallas_call | solution.py:386
  48.8 3.8 %collective-permute-start.32 = (bf16[576,3584]{1,0:T(8,128)(2,1)S(1)}, bf16[576,3584]{1,0:T(8,128)(2,1)S(1)}, u32[]{:S(2)}, u32[]{:S(2)}) collective-permute-start(bf16[576,3584]{1,0:T(8,128)(2,1)S(1)} %bitcast.10), channel_id=1, source_target_pairs={{0,1},{1,0},{2,3},{3,2},{4,5},{5,4},{6,7},{7,6},{8,9},{9,8},{10,11... | collective-permute-start | bytes 12386312 | tf_op jit(solution)/shard_map/ppermute | solution.py:47
  55.5 1.7 %collective-permute-start.23 = (bf16[32,7168]{1,0:T(8,128)(2,1)S(1)}, bf16[32,7168]{1,0:T(8,128)(2,1)S(1)}, u32[]{:S(2)}, u32[]{:S(2)}) collective-permute-start(bf16[32,7168]{1,0:T(8,128)(2,1)S(1)} %add_convert_fusion.1), channel_id=1, source_target_pairs={{0,12},{1,49},{2,14},{3,51},{4,8},{5,53},{6,10},{7,55},{8,4},{9,57... | collective-permute-start | bytes 1376264 | tf_op jit(solution)/shard_map/ppermute | solution.py:47
  57.1 4.4 %collective-permute-done.18 = bf16[32,7168]{1,0:T(8,128)(2,1)S(1)} collective-permute-done((bf16[32,7168]{1,0:T(8,128)(2,1)S(1)}, bf16[32,7168]{1,0:T(8,128)(2,1)S(1)}, u32[]{:S(2)}, u32[]{:S(2)}) %collective-permute-start.18) | collective-permute-done | bytes 458784 | tf_op jit(solution)/shard_map/ppermute | solution.py:47
  63.0 8.4 %collective-permute-done.23 = bf16[32,7168]{1,0:T(8,128)(2,1)S(1)} collective-permute-done((bf16[32,7168]{1,0:T(8,128)(2,1)S(1)}, bf16[32,7168]{1,0:T(8,128)(2,1)S(1)}, u32[]{:S(2)}, u32[]{:S(2)}) %collective-permute-start.23) | collective-permute-done | bytes 458784 | tf_op jit(solution)/shard_map/ppermute | solution.py:47
  78.2 2.2 %collective-permute-done.30 = bf16[8,7168]{1,0:T(8,128)(2,1)S(1)} collective-permute-done((bf16[8,7168]{1,0:T(8,128)(2,1)S(1)}, bf16[8,7168]{1,0:T(8,128)(2,1)S(1)}, u32[]{:S(2)}, u32[]{:S(2)}) %collective-permute-start.30) | collective-permute-done | bytes 114720 | tf_op jit(solution)/shard_map/ppermute | solution.py:47
  80.5 6.3 %collective-permute-start.31 = (bf16[8,7168]{1,0:T(8,128)(2,1)S(1)}, bf16[8,7168]{1,0:T(8,128)(2,1)S(1)}, u32[]{:S(2)}, u32[]{:S(2)}) collective-permute-start(bf16[8,7168]{1,0:T(8,128)(2,1)S(1)} %get-tuple-element.80), channel_id=1, source_target_pairs={{0,64},{1,65},{2,66},{3,67},{4,68},{5,69},{6,70},{7,71},{8,72},{9,... | collective-permute-start | bytes 344072 | tf_op jit(solution)/shard_map/ppermute | solution.py:47
  86.9 3.8 %collective-permute-start.27 = (bf16[8,7168]{1,0:T(8,128)(2,1)S(1)}, bf16[8,7168]{1,0:T(8,128)(2,1)S(1)}, u32[]{:S(2)}, u32[]{:S(2)}) collective-permute-start(bf16[8,7168]{1,0:T(8,128)(2,1)S(1)} %add_convert_fusion.6), channel_id=1, source_target_pairs={{0,66},{1,67},{2,64},{3,65},{4,70},{5,71},{6,68},{7,69},{8,74},{9,... | collective-permute-start | bytes 344072 | tf_op jit(solution)/shard_map/ppermute | solution.py:47
  90.8 2.7 %collective-permute-done.27.back_flip = bf16[8,7168]{1,0:T(8,128)(2,1)S(1)} collective-permute-done((bf16[8,7168]{1,0:T(8,128)(2,1)S(1)}, bf16[8,7168]{1,0:T(8,128)(2,1)S(1)}, u32[]{:S(2)}, u32[]{:S(2)}) %collective-permute-start.27) | collective-permute-done | bytes 114720 | tf_op jit(solution)/shard_map/ppermute | solution.py:47
  93.5 2.9 %shard_map.179 = (bf16[8,7168]{1,0:T(8,128)(2,1)S(1)}, bf16[8,576]{1,0:T(8,128)(2,1)S(1)}) custom-call(s32[3]{0:T(128)S(1)} %pad_add_fusion.place_ref, bf16[1,16,7168]{2,1,0:T(8,128)(2,1)S(1)} %copy-done.2, bf16[8,7168]{1,0:T(8,128)(2,1)S(1)} %collective-permute-done.27.back_flip, bf16[8,7168]{1,0:T(8,128)(2,1)S(1)} %collective-permute-done.31.back_straight, ...), custom_call_target="tpu_custom_call" | custom-call | tf_op jit(solution)/shard_map/pallas_call | solution.py:145
  96.4 4.2 %collective-permute-start.34 = (bf16[8,7168]{1,0:T(8,128)(2,1)S(1)}, bf16[8,7168]{1,0:T(8,128)(2,1)S(1)}, u32[]{:S(2)}, u32[]{:S(2)}) collective-permute-start(bf16[8,7168]{1,0:T(8,128)(2,1)S(1)} %get-tuple-element.75.updated_own), channel_id=1, source_target_pairs={{0,1},{1,0},{2,3},{3,2},{4,5},{5,4},{6,7},{7,6},{8,9},{9,8},{10,11... | collective-permute-start | bytes 344072 | tf_op jit(solution)/shard_map/ppermute | solution.py:47
  101.8 1.9 %shard_map.180 = (bf16[1,16,7168]{2,1,0:T(8,128)(2,1)}, bf16[1,16,512]{2,1,0:T(8,128)(2,1)}, bf16[1,16,64]{2,1,0:T(8,128)(2,1)}, bf16[1,16,32,512]{3,2,1,0:T(8,128)(2,1)}) custom-call(s32[3]{0:T(128)S(1)} %pad_add_fusion.place_ref, bf16[8,576]{1,0:T(8,128)(2,1)S(1)} %get-tuple-element.74.fresh_own, bf16[8,576]{1,0:T(8,128)(2,1)S(1)} %collective-permute-done.33.fresh_other, ...), custom_call_target="tpu_custom_call" | custom-call | tf_op jit(solution)/shard_map/pallas_call | solution.py:145
  (82 shorter events, 26.3 us)
Async XLA Ops:
  0.7 13.0 %collective-permute-start.3 = (bf16[7168,256]{1,0:T(8,128)(2,1)}, bf16[7168,256]{1,0:T(8,128)(2,1)S(1)}, u32[]{:S(2)}, u32[]{:S(2)}) collective-permute-start(bf16[7168,256]{1,0:T(8,128)(2,1)} %bitcast.11), channel_id=1, source_target_pairs={{0,1},{1,0},{2,3},{3,2},{4,5},{5,4},{6,7},{7,6},{8,9},{9,8},{10,11... | collective-permute-start | bytes 11010056 | tf_op jit(solution)/shard_map/ppermute | solution.py:47
  2.2 11.5 %collective-permute-start.4 = (bf16[7168,256]{1,0:T(8,128)(2,1)}, bf16[7168,256]{1,0:T(8,128)(2,1)S(1)}, u32[]{:S(2)}, u32[]{:S(2)}) collective-permute-start(bf16[7168,256]{1,0:T(8,128)(2,1)} %bitcast.13), channel_id=1, source_target_pairs={{0,1},{1,0},{2,3},{3,2},{4,5},{5,4},{6,7},{7,6},{8,9},{9,8},{10,11... | collective-permute-start | bytes 11010056 | tf_op jit(solution)/shard_map/ppermute | solution.py:47
  4.8 8.9 %collective-permute-start.1 = (bf16[8,7296]{1,0:T(8,128)(2,1)S(1)}, bf16[8,7296]{1,0:T(8,128)(2,1)S(1)}, u32[]{:S(2)}, u32[]{:S(2)}) collective-permute-start(bf16[8,7296]{1,0:T(8,128)(2,1)S(1)} %shard_map.174), channel_id=1, source_target_pairs={{0,64},{1,65},{2,66},{3,67},{4,68},{5,69},{6,70},{7,71},{8,72},{9,... | collective-permute-start | bytes 350216 | tf_op jit(solution)/shard_map/ppermute | solution.py:47
  13.7 12.8 %collective-permute-start.11 = (bf16[256,7168]{1,0:T(8,128)(2,1)S(1)}, bf16[256,7168]{1,0:T(8,128)(2,1)S(1)}, u32[]{:S(2)}, u32[]{:S(2)}) collective-permute-start(bf16[256,7168]{1,0:T(8,128)(2,1)S(1)} %bitcast.16), channel_id=1, source_target_pairs={{0,1},{1,0},{2,3},{3,2},{4,5},{5,4},{6,7},{7,6},{8,9},{9,8},{10,11... | collective-permute-start | bytes 11010056 | tf_op jit(solution)/shard_map/ppermute | solution.py:47
  16.4 6.1 %collective-permute-start.8 = (bf16[8,7296]{1,0:T(8,128)(2,1)S(1)}, bf16[8,7296]{1,0:T(8,128)(2,1)S(1)}, u32[]{:S(2)}, u32[]{:S(2)}) collective-permute-start(bf16[8,7296]{1,0:T(8,128)(2,1)S(1)} %collective-permute-done.1), channel_id=1, source_target_pairs={{0,48},{1,13},{2,50},{3,15},{4,52},{5,9},{6,54},{7,11},{8,56},{9,5... | collective-permute-start | bytes 350216 | tf_op jit(solution)/shard_map/ppermute | solution.py:47
  20.0 5.8 %collective-permute-start.9 = (bf16[8,7296]{1,0:T(8,128)(2,1)S(1)}, bf16[8,7296]{1,0:T(8,128)(2,1)S(1)}, u32[]{:S(2)}, u32[]{:S(2)}) collective-permute-start(bf16[8,7296]{1,0:T(8,128)(2,1)S(1)} %collective-permute-done.5), channel_id=1, source_target_pairs={{0,48},{1,13},{2,50},{3,15},{4,52},{5,9},{6,54},{7,11},{8,56},{9,5... | collective-permute-start | bytes 350216 | tf_op jit(solution)/shard_map/ppermute | solution.py:47
  26.5 7.8 %collective-permute-start.12 = (bf16[32,7296]{1,0:T(8,128)(2,1)S(1)}, bf16[32,7296]{1,0:T(8,128)(2,1)S(1)}, u32[]{:S(2)}, u32[]{:S(2)}) collective-permute-start(bf16[32,7296]{1,0:T(8,128)(2,1)S(1)} %pad_maximum_fusion.refs_0_), channel_id=1, source_target_pairs={{0,4},{1,17},{2,6},{3,19},{4,0},{5,21},{6,2},{7,23},{8,12},{9,25},... | collective-permute-start | bytes 1400840 | tf_op jit(solution)/shard_map/ppermute | solution.py:47
  27.5 8.9 %collective-permute-start.13 = (bf16[32,7296]{1,0:T(8,128)(2,1)S(1)}, bf16[32,7296]{1,0:T(8,128)(2,1)S(1)}, u32[]{:S(2)}, u32[]{:S(2)}) collective-permute-start(bf16[32,7296]{1,0:T(8,128)(2,1)S(1)} %pad_maximum_fusion.1.refs_1_), channel_id=1, source_target_pairs={{0,12},{1,49},{2,14},{3,51},{4,8},{5,53},{6,10},{7,55},{8,4},{9,57... | collective-permute-start | bytes 1400840 | tf_op jit(solution)/shard_map/ppermute | solution.py:47
  29.4 12.1 %collective-permute-start.15 = (bf16[32,7296]{1,0:T(8,128)(2,1)S(1)}, bf16[32,7296]{1,0:T(8,128)(2,1)S(1)}, u32[]{:S(2)}, u32[]{:S(2)}) collective-permute-start(bf16[32,7296]{1,0:T(8,128)(2,1)S(1)} %pad_maximum_fusion.refs_0_), channel_id=1, source_target_pairs={{0,12},{1,49},{2,14},{3,51},{4,8},{5,53},{6,10},{7,55},{8,4},{9,57... | collective-permute-start | bytes 1400840 | tf_op jit(solution)/shard_map/ppermute | solution.py:47
  30.2 11.3 %collective-permute-start.14 = (bf16[32,7296]{1,0:T(8,128)(2,1)S(1)}, bf16[32,7296]{1,0:T(8,128)(2,1)S(1)}, u32[]{:S(2)}, u32[]{:S(2)}) collective-permute-start(bf16[32,7296]{1,0:T(8,128)(2,1)S(1)} %pad_maximum_fusion.1.refs_1_), channel_id=1, source_target_pairs={{0,4},{1,17},{2,6},{3,19},{4,0},{5,21},{6,2},{7,23},{8,12},{9,25},... | collective-permute-start | bytes 1400840 | tf_op jit(solution)/shard_map/ppermute | solution.py:47
  36.5 10.2 %collective-permute-start.16 = (bf16[32,7296]{1,0:T(8,128)(2,1)S(1)}, bf16[32,7296]{1,0:T(8,128)(2,1)S(1)}, u32[]{:S(2)}, u32[]{:S(2)}) collective-permute-start(bf16[32,7296]{1,0:T(8,128)(2,1)S(1)} %collective-permute-done.12.refs_2_), channel_id=1, source_target_pairs={{0,12},{1,49},{2,14},{3,51},{4,8},{5,53},{6,10},{7,55},{8,4},{9,57... | collective-permute-start | bytes 1400840 | tf_op jit(solution)/shard_map/ppermute | solution.py:47
  38.3 8.4 %collective-permute-start.17 = (bf16[32,7296]{1,0:T(8,128)(2,1)S(1)}, bf16[32,7296]{1,0:T(8,128)(2,1)S(1)}, u32[]{:S(2)}, u32[]{:S(2)}) collective-permute-start(bf16[32,7296]{1,0:T(8,128)(2,1)S(1)} %collective-permute-done.13.refs_5_), channel_id=1, source_target_pairs={{0,4},{1,17},{2,6},{3,19},{4,0},{5,21},{6,2},{7,23},{8,12},{9,25},... | collective-permute-start | bytes 1400840 | tf_op jit(solution)/shard_map/ppermute | solution.py:47
  47.4 7.9 %collective-permute-start.22 = (bf16[32,7168]{1,0:T(8,128)(2,1)S(1)}, bf16[32,7168]{1,0:T(8,128)(2,1)S(1)}, u32[]{:S(2)}, u32[]{:S(2)}) collective-permute-start(bf16[32,7168]{1,0:T(8,128)(2,1)S(1)} %get-tuple-element.69), channel_id=1, source_target_pairs={{0,4},{1,17},{2,6},{3,19},{4,0},{5,21},{6,2},{7,23},{8,12},{9,25},... | collective-permute-start | bytes 1376264 | tf_op jit(solution)/shard_map/ppermute | solution.py:47
  48.8 44.7 %collective-permute-start.32 = (bf16[576,3584]{1,0:T(8,128)(2,1)S(1)}, bf16[576,3584]{1,0:T(8,128)(2,1)S(1)}, u32[]{:S(2)}, u32[]{:S(2)}) collective-permute-start(bf16[576,3584]{1,0:T(8,128)(2,1)S(1)} %bitcast.10), channel_id=1, source_target_pairs={{0,1},{1,0},{2,3},{3,2},{4,5},{5,4},{6,7},{7,6},{8,9},{9,8},{10,11... | collective-permute-start | bytes 12386312 | tf_op jit(solution)/shard_map/ppermute | solution.py:47
  52.7 8.8 %collective-permute-start.18 = (bf16[32,7168]{1,0:T(8,128)(2,1)S(1)}, bf16[32,7168]{1,0:T(8,128)(2,1)S(1)}, u32[]{:S(2)}, u32[]{:S(2)}) collective-permute-start(bf16[32,7168]{1,0:T(8,128)(2,1)S(1)} %get-tuple-element.64), channel_id=1, source_target_pairs={{0,12},{1,49},{2,14},{3,51},{4,8},{5,53},{6,10},{7,55},{8,4},{9,57... | collective-permute-start | bytes 1376264 | tf_op jit(solution)/shard_map/ppermute | solution.py:47
  54.1 17.6 %collective-permute-start.20 = (bf16[32,7168]{1,0:T(8,128)(2,1)S(1)}, bf16[32,7168]{1,0:T(8,128)(2,1)S(1)}, u32[]{:S(2)}, u32[]{:S(2)}) collective-permute-start(bf16[32,7168]{1,0:T(8,128)(2,1)S(1)} %get-tuple-element.65), channel_id=1, source_target_pairs={{0,12},{1,49},{2,14},{3,51},{4,8},{5,53},{6,10},{7,55},{8,4},{9,57... | collective-permute-start | bytes 1376264 | tf_op jit(solution)/shard_map/ppermute | solution.py:47
  55.3 7.6 %collective-permute-start.21 = (bf16[32,7168]{1,0:T(8,128)(2,1)S(1)}, bf16[32,7168]{1,0:T(8,128)(2,1)S(1)}, u32[]{:S(2)}, u32[]{:S(2)}) collective-permute-start(bf16[32,7168]{1,0:T(8,128)(2,1)S(1)} %get-tuple-element.67), channel_id=1, source_target_pairs={{0,4},{1,17},{2,6},{3,19},{4,0},{5,21},{6,2},{7,23},{8,12},{9,25},... | collective-permute-start | bytes 1376264 | tf_op jit(solution)/shard_map/ppermute | solution.py:47
  55.5 15.9 %collective-permute-start.23 = (bf16[32,7168]{1,0:T(8,128)(2,1)S(1)}, bf16[32,7168]{1,0:T(8,128)(2,1)S(1)}, u32[]{:S(2)}, u32[]{:S(2)}) collective-permute-start(bf16[32,7168]{1,0:T(8,128)(2,1)S(1)} %add_convert_fusion.1), channel_id=1, source_target_pairs={{0,12},{1,49},{2,14},{3,51},{4,8},{5,53},{6,10},{7,55},{8,4},{9,57... | collective-permute-start | bytes 1376264 | tf_op jit(solution)/shard_map/ppermute | solution.py:47
  61.6 10.1 %collective-permute-start.19 = (bf16[32,7168]{1,0:T(8,128)(2,1)S(1)}, bf16[32,7168]{1,0:T(8,128)(2,1)S(1)}, u32[]{:S(2)}, u32[]{:S(2)}) collective-permute-start(bf16[32,7168]{1,0:T(8,128)(2,1)S(1)} %add_convert_fusion.3), channel_id=1, source_target_pairs={{0,4},{1,17},{2,6},{3,19},{4,0},{5,21},{6,2},{7,23},{8,12},{9,25},... | collective-permute-start | bytes 1376264 | tf_op jit(solution)/shard_map/ppermute | solution.py:47
  71.9 6.1 %collective-permute-start.28 = (bf16[8,7168]{1,0:T(8,128)(2,1)S(1)}, bf16[8,7168]{1,0:T(8,128)(2,1)S(1)}, u32[]{:S(2)}, u32[]{:S(2)}) collective-permute-start(bf16[8,7168]{1,0:T(8,128)(2,1)S(1)} %slice.37), channel_id=1, source_target_pairs={{0,16},{1,5},{2,18},{3,7},{4,20},{5,1},{6,22},{7,3},{8,24},{9,13},... | collective-permute-start | bytes 344072 | tf_op jit(solution)/shard_map/ppermute | solution.py:47
  76.7 10.2 %collective-permute-start.26 = (bf16[8,7168]{1,0:T(8,128)(2,1)S(1)}, bf16[8,7168]{1,0:T(8,128)(2,1)S(1)}, u32[]{:S(2)}, u32[]{:S(2)}) collective-permute-start(bf16[8,7168]{1,0:T(8,128)(2,1)S(1)} %get-tuple-element.83), channel_id=1, source_target_pairs={{0,48},{1,13},{2,50},{3,15},{4,52},{5,9},{6,54},{7,11},{8,56},{9,5... | collective-permute-start | bytes 344072 | tf_op jit(solution)/shard_map/ppermute | solution.py:47
  80.5 6.4 %collective-permute-start.25 = (bf16[8,7168]{1,0:T(8,128)(2,1)S(1)}, bf16[8,7168]{1,0:T(8,128)(2,1)S(1)}, u32[]{:S(2)}, u32[]{:S(2)}) collective-permute-start(bf16[8,7168]{1,0:T(8,128)(2,1)S(1)} %get-tuple-element.81), channel_id=1, source_target_pairs={{0,16},{1,5},{2,18},{3,7},{4,20},{5,1},{6,22},{7,3},{8,24},{9,13},... | collective-permute-start | bytes 344072 | tf_op jit(solution)/shard_map/ppermute | solution.py:47
  80.5 10.2 %collective-permute-start.31 = (bf16[8,7168]{1,0:T(8,128)(2,1)S(1)}, bf16[8,7168]{1,0:T(8,128)(2,1)S(1)}, u32[]{:S(2)}, u32[]{:S(2)}) collective-permute-start(bf16[8,7168]{1,0:T(8,128)(2,1)S(1)} %get-tuple-element.80), channel_id=1, source_target_pairs={{0,64},{1,65},{2,66},{3,67},{4,68},{5,69},{6,70},{7,71},{8,72},{9,... | collective-permute-start | bytes 344072 | tf_op jit(solution)/shard_map/ppermute | solution.py:47
  86.9 6.6 %collective-permute-start.27 = (bf16[8,7168]{1,0:T(8,128)(2,1)S(1)}, bf16[8,7168]{1,0:T(8,128)(2,1)S(1)}, u32[]{:S(2)}, u32[]{:S(2)}) collective-permute-start(bf16[8,7168]{1,0:T(8,128)(2,1)S(1)} %add_convert_fusion.6), channel_id=1, source_target_pairs={{0,66},{1,67},{2,64},{3,65},{4,70},{5,71},{6,68},{7,69},{8,74},{9,... | collective-permute-start | bytes 344072 | tf_op jit(solution)/shard_map/ppermute | solution.py:47
  (18 other events, 180.7 us)

commit v6 on v5

--- a/solution.py
+++ b/solution.py
@@ -483,6 +483,7 @@
     gates = (gates[0], gate_other, gates[1], up_other)
     attended = (query_latent, query_rope, cache_latent, cache_rope)
     hidden, cached = roles(place, lengths, pieces[:6], gates, attended)
+    hidden, kv_other = barrier((hidden, kv_other))
     answers = call_inside(
         answer_kernel,
         [jax.ShapeDtypeStruct((piece.shape[0], model_width), BF16) for piece in pieces],

time: 104 us -> 104 us (level)
  starting transfers between devices: 49.3 us -> 51.1 us
  local copies, waits for them, and re-layouts: 1.38 us -> 0.07 us
    ppermute x35, starting transfers between devices: 49.3 us -> 51.1 us  [send(): return lax.ppermute(value, AXES, pairs_of(partner))]
    unnamed x14, local copies, waits for them, and re-layouts: 1.35 us -> 0.03 us
  transfers between devices with their start and end apart: 35 -> 35, of which waited for: 16 -> 14; matrix products, arithmetic and copies ran while one was open for 2% -> 2% of each run, Pallas kernels for 9% -> 9%
where the time goes in v6:
time: 104 us
  starting transfers between devices  51.1 us (49%)
  waiting for transfers between devices  35.4 us (34%)
  Pallas kernels  14.6 us (14%)
  other arithmetic  1.64 us (2%)
    ppermute x35, starting transfers between devices, send(): return lax.ppermute(value, AXES, pairs_of(partner))  51.1 us
    ppermute x35, waiting for transfers between devices, send(): return lax.ppermute(value, AXES, pairs_of(partner))  35.4 us
    pallas_call x3, Pallas kernels, call_inside(): pl.pallas_call(kernel, out_shape=out_shapes, in_specs=[pl.BlockSpec(memor...  5.55 us
    pallas_call x1, Pallas kernels, roles(): pl.pallas_call(roles_kernel, out_shape=[jax.ShapeDtypeStruct((rows, 2 * w...  5.16 us
    pallas_call x1, Pallas kernels, front(): pl.pallas_call(front_kernel, out_shape=jax.ShapeDtypeStruct(shape, BF16),...  2.81 us
  transfers between devices with their start and end apart: 35, of which 14 were waited for; matrix products, arithmetic and copies ran while one was open for 2% of the time, Pallas kernels for 9%

profile of v6, /device:TPU:1, one launch (start us, length us, event | category | flops | bytes accessed | tf_op | source)
XLA Modules:
  0.0 103.8 jit_solution(15736042726233164703)
XLA Ops:
  2.3 2.8 %shard_map.174 = bf16[8,7296]{1,0:T(8,128)(2,1)S(1)} custom-call(s32[3]{0:T(128)S(1)} %pad_add_fusion.place_ref, bf16[1,16,7168]{2,1,0:T(8,128)(2,1)} %residual.1, bf16[1,7168]{1,0:T(2,128)(2,1)} %gain_hbm.1, bf16[1,16,7168]{2,1,0:T(8,128)(2,1)} %router_hbm.1, s32[1,8,16]{2,1,0:T(8,128)} %bitcast.17), custom_call_target="tpu_custom_call" | custom-call | tf_op jit(solution)/shard_map/pallas_call | solution.py:196
  5.1 3.1 %collective-permute-start.1 = (bf16[8,7296]{1,0:T(8,128)(2,1)S(1)}, bf16[8,7296]{1,0:T(8,128)(2,1)S(1)}, u32[]{:S(2)}, u32[]{:S(2)}) collective-permute-start(bf16[8,7296]{1,0:T(8,128)(2,1)S(1)} %shard_map.174), channel_id=1, source_target_pairs={{0,64},{1,65},{2,66},{3,67},{4,68},{5,69},{6,70},{7,71},{8,72},{9,... | collective-permute-start | bytes 350216 | tf_op jit(solution)/shard_map/ppermute | solution.py:47
  11.3 2.4 %collective-permute-done.2.gain_other = bf16[1,3584]{1,0:T(2,128)(2,1)S(1)} collective-permute-done((bf16[1,3584]{1,0:T(2,128)(2,1)}, bf16[1,3584]{1,0:T(2,128)(2,1)S(1)}, u32[]{:S(2)}, u32[]{:S(2)}) %collective-permute-start.2) | collective-permute-done | bytes 7200 | tf_op jit(solution)/shard_map/ppermute | solution.py:47
  16.7 2.2 %collective-permute-start.8 = (bf16[8,7296]{1,0:T(8,128)(2,1)S(1)}, bf16[8,7296]{1,0:T(8,128)(2,1)S(1)}, u32[]{:S(2)}, u32[]{:S(2)}) collective-permute-start(bf16[8,7296]{1,0:T(8,128)(2,1)S(1)} %collective-permute-done.1), channel_id=1, source_target_pairs={{0,48},{1,13},{2,50},{3,15},{4,52},{5,9},{6,54},{7,11},{8,56},{9,5... | collective-permute-start | bytes 350216 | tf_op jit(solution)/shard_map/ppermute | solution.py:47
  20.3 2.5 %collective-permute-start.9 = (bf16[8,7296]{1,0:T(8,128)(2,1)S(1)}, bf16[8,7296]{1,0:T(8,128)(2,1)S(1)}, u32[]{:S(2)}, u32[]{:S(2)}) collective-permute-start(bf16[8,7296]{1,0:T(8,128)(2,1)S(1)} %collective-permute-done.5), channel_id=1, source_target_pairs={{0,48},{1,13},{2,50},{3,15},{4,52},{5,9},{6,54},{7,11},{8,56},{9,5... | collective-permute-start | bytes 350216 | tf_op jit(solution)/shard_map/ppermute | solution.py:47
  22.9 1.9 %collective-permute-done.7 = bf16[8,7296]{1,0:T(8,128)(2,1)S(1)} collective-permute-done((bf16[8,7296]{1,0:T(8,128)(2,1)S(1)}, bf16[8,7296]{1,0:T(8,128)(2,1)S(1)}, u32[]{:S(2)}, u32[]{:S(2)}) %collective-permute-start.7) | collective-permute-done | bytes 116768 | tf_op jit(solution)/shard_map/ppermute | solution.py:47
  27.9 1.8 %collective-permute-start.13 = (bf16[32,7296]{1,0:T(8,128)(2,1)S(1)}, bf16[32,7296]{1,0:T(8,128)(2,1)S(1)}, u32[]{:S(2)}, u32[]{:S(2)}) collective-permute-start(bf16[32,7296]{1,0:T(8,128)(2,1)S(1)} %pad_maximum_fusion.1.refs_1_), channel_id=1, source_target_pairs={{0,12},{1,49},{2,14},{3,51},{4,8},{5,53},{6,10},{7,55},{8,4},{9,57... | collective-permute-start | bytes 1400840 | tf_op jit(solution)/shard_map/ppermute | solution.py:47
  31.2 4.2 %collective-permute-done.12.refs_2_ = bf16[32,7296]{1,0:T(8,128)(2,1)S(1)} collective-permute-done((bf16[32,7296]{1,0:T(8,128)(2,1)S(1)}, bf16[32,7296]{1,0:T(8,128)(2,1)S(1)}, u32[]{:S(2)}, u32[]{:S(2)}) %collective-permute-start.12) | collective-permute-done | bytes 466976 | tf_op jit(solution)/shard_map/ppermute | solution.py:47
  38.6 3.2 %collective-permute-done.15.refs_4_ = bf16[32,7296]{1,0:T(8,128)(2,1)S(1)} collective-permute-done((bf16[32,7296]{1,0:T(8,128)(2,1)S(1)}, bf16[32,7296]{1,0:T(8,128)(2,1)S(1)}, u32[]{:S(2)}, u32[]{:S(2)}) %collective-permute-start.15) | collective-permute-done | bytes 466976 | tf_op jit(solution)/shard_map/ppermute | solution.py:47
  41.8 5.2 %shard_map.177 = (bf16[192,512]{1,0:T(8,128)(2,1)S(1)}, f32[16,32,512]{2,1,0:T(8,128)S(1)}, f32[16,32,128]{2,1,0:T(8,128)S(1)}, f32[16,32,128]{2,1,0:T(8,128)S(1)}, bf16[16,32,64]{2,1,0:T(8,128)(2,1)S(1)}) custom-call(s32[3]{0:T(128)S(1)} %pad_add_fusion.place_ref, s32[1,16]{1,0:T(1,128)S(1)} %copy-done.5, bf16[32,7296]{1,0:T(8,128)(2,1)S(1)} %pad_maximum_fusion.refs_0_, ...), custom_call_target="tpu_custom_call" | custom-call | flops 2818572288 | bytes 14680064 | tf_op jit(solution)/shard_map/pallas_call | solution.py:386
  47.9 1.9 %collective-permute-start.19 = (bf16[32,7168]{1,0:T(8,128)(2,1)S(1)}, bf16[32,7168]{1,0:T(8,128)(2,1)S(1)}, u32[]{:S(2)}, u32[]{:S(2)}) collective-permute-start(bf16[32,7168]{1,0:T(8,128)(2,1)S(1)} %get-tuple-element.68), channel_id=1, source_target_pairs={{0,12},{1,49},{2,14},{3,51},{4,8},{5,53},{6,10},{7,55},{8,4},{9,57... | collective-permute-start | bytes 1376264 | tf_op jit(solution)/shard_map/ppermute | solution.py:47
  50.8 4.7 %collective-permute-done.23 = bf16[32,7168]{1,0:T(8,128)(2,1)S(1)} collective-permute-done((bf16[32,7168]{1,0:T(8,128)(2,1)S(1)}, bf16[32,7168]{1,0:T(8,128)(2,1)S(1)}, u32[]{:S(2)}, u32[]{:S(2)}) %collective-permute-start.23) | collective-permute-done | bytes 458784 | tf_op jit(solution)/shard_map/ppermute | solution.py:47
  55.6 1.9 %collective-permute-start.24 = (bf16[32,7168]{1,0:T(8,128)(2,1)S(1)}, bf16[32,7168]{1,0:T(8,128)(2,1)S(1)}, u32[]{:S(2)}, u32[]{:S(2)}) collective-permute-start(bf16[32,7168]{1,0:T(8,128)(2,1)S(1)} %add_convert_fusion.1), channel_id=1, source_target_pairs={{0,12},{1,49},{2,14},{3,51},{4,8},{5,53},{6,10},{7,55},{8,4},{9,57... | collective-permute-start | bytes 1376264 | tf_op jit(solution)/shard_map/ppermute | solution.py:47
  57.7 2.7 %collective-permute-done.22 = bf16[32,7168]{1,0:T(8,128)(2,1)S(1)} collective-permute-done((bf16[32,7168]{1,0:T(8,128)(2,1)S(1)}, bf16[32,7168]{1,0:T(8,128)(2,1)S(1)}, u32[]{:S(2)}, u32[]{:S(2)}) %collective-permute-start.22) | collective-permute-done | bytes 458784 | tf_op jit(solution)/shard_map/ppermute | solution.py:47
  60.4 6.2 %collective-permute-done.24 = bf16[32,7168]{1,0:T(8,128)(2,1)S(1)} collective-permute-done((bf16[32,7168]{1,0:T(8,128)(2,1)S(1)}, bf16[32,7168]{1,0:T(8,128)(2,1)S(1)}, u32[]{:S(2)}, u32[]{:S(2)}) %collective-permute-start.24) | collective-permute-done | bytes 458784 | tf_op jit(solution)/shard_map/ppermute | solution.py:47
  68.6 3.7 %collective-permute-start.25 = (bf16[8,7168]{1,0:T(8,128)(2,1)S(1)}, bf16[8,7168]{1,0:T(8,128)(2,1)S(1)}, u32[]{:S(2)}, u32[]{:S(2)}) collective-permute-start(bf16[8,7168]{1,0:T(8,128)(2,1)S(1)} %get-tuple-element.88), channel_id=1, source_target_pairs={{0,48},{1,13},{2,50},{3,15},{4,52},{5,9},{6,54},{7,11},{8,56},{9,5... | collective-permute-start | bytes 344072 | tf_op jit(solution)/shard_map/ppermute | solution.py:47
  72.4 2.0 %collective-permute-start.31 = (bf16[8,7168]{1,0:T(8,128)(2,1)S(1)}, bf16[8,7168]{1,0:T(8,128)(2,1)S(1)}, u32[]{:S(2)}, u32[]{:S(2)}) collective-permute-start(bf16[8,7168]{1,0:T(8,128)(2,1)S(1)} %add_convert_fusion.5), channel_id=1, source_target_pairs={{0,48},{1,13},{2,50},{3,15},{4,52},{5,9},{6,54},{7,11},{8,56},{9,5... | collective-permute-start | bytes 344072 | tf_op jit(solution)/shard_map/ppermute | solution.py:47
  75.2 2.2 %collective-permute-done.31 = bf16[8,7168]{1,0:T(8,128)(2,1)S(1)} collective-permute-done((bf16[8,7168]{1,0:T(8,128)(2,1)S(1)}, bf16[8,7168]{1,0:T(8,128)(2,1)S(1)}, u32[]{:S(2)}, u32[]{:S(2)}) %collective-permute-start.31) | collective-permute-done | bytes 114720 | tf_op jit(solution)/shard_map/ppermute | solution.py:47
  77.5 6.8 %collective-permute-start.32 = (bf16[8,7168]{1,0:T(8,128)(2,1)S(1)}, bf16[8,7168]{1,0:T(8,128)(2,1)S(1)}, u32[]{:S(2)}, u32[]{:S(2)}) collective-permute-start(bf16[8,7168]{1,0:T(8,128)(2,1)S(1)} %get-tuple-element.84), channel_id=1, source_target_pairs={{0,64},{1,65},{2,66},{3,67},{4,68},{5,69},{6,70},{7,71},{8,72},{9,... | collective-permute-start | bytes 344072 | tf_op jit(solution)/shard_map/ppermute | solution.py:47
  84.3 4.4 %collective-permute-start.28 = (bf16[8,7168]{1,0:T(8,128)(2,1)S(1)}, bf16[8,7168]{1,0:T(8,128)(2,1)S(1)}, u32[]{:S(2)}, u32[]{:S(2)}) collective-permute-start(bf16[8,7168]{1,0:T(8,128)(2,1)S(1)} %add_convert_fusion.6), channel_id=1, source_target_pairs={{0,66},{1,67},{2,64},{3,65},{4,70},{5,71},{6,68},{7,69},{8,74},{9,... | collective-permute-start | bytes 344072 | tf_op jit(solution)/shard_map/ppermute | solution.py:47
  88.7 3.4 %collective-permute-done.28.back_flip = bf16[8,7168]{1,0:T(8,128)(2,1)S(1)} collective-permute-done((bf16[8,7168]{1,0:T(8,128)(2,1)S(1)}, bf16[8,7168]{1,0:T(8,128)(2,1)S(1)}, u32[]{:S(2)}, u32[]{:S(2)}) %collective-permute-start.28) | collective-permute-done | bytes 114720 | tf_op jit(solution)/shard_map/ppermute | solution.py:47
  92.2 2.9 %shard_map.179 = (bf16[8,7168]{1,0:T(8,128)(2,1)S(1)}, bf16[8,576]{1,0:T(8,128)(2,1)S(1)}) custom-call(s32[3]{0:T(128)S(1)} %pad_add_fusion.place_ref, bf16[1,16,7168]{2,1,0:T(8,128)(2,1)S(1)} %copy-done.2, bf16[8,7168]{1,0:T(8,128)(2,1)S(1)} %collective-permute-done.28.back_flip, bf16[8,7168]{1,0:T(8,128)(2,1)S(1)} %collective-permute-done.32.back_straight, ...), custom_call_target="tpu_custom_call" | custom-call | tf_op jit(solution)/shard_map/pallas_call | solution.py:145
  95.0 5.6 %collective-permute-start.34 = (bf16[8,7168]{1,0:T(8,128)(2,1)S(1)}, bf16[8,7168]{1,0:T(8,128)(2,1)S(1)}, u32[]{:S(2)}, u32[]{:S(2)}) collective-permute-start(bf16[8,7168]{1,0:T(8,128)(2,1)S(1)} %get-tuple-element.79.updated_own), channel_id=1, source_target_pairs={{0,1},{1,0},{2,3},{3,2},{4,5},{5,4},{6,7},{7,6},{8,9},{9,8},{10,11... | collective-permute-start | bytes 344072 | tf_op jit(solution)/shard_map/ppermute | solution.py:47
  101.8 1.9 %shard_map.180 = (bf16[1,16,7168]{2,1,0:T(8,128)(2,1)}, bf16[1,16,512]{2,1,0:T(8,128)(2,1)}, bf16[1,16,64]{2,1,0:T(8,128)(2,1)}, bf16[1,16,32,512]{3,2,1,0:T(8,128)(2,1)}) custom-call(s32[3]{0:T(128)S(1)} %pad_add_fusion.place_ref, bf16[8,576]{1,0:T(8,128)(2,1)S(1)} %get-tuple-element.78.fresh_own, bf16[8,576]{1,0:T(8,128)(2,1)S(1)} %collective-permute-done.33.fresh_other, ...), custom_call_target="tpu_custom_call" | custom-call | tf_op jit(solution)/shard_map/pallas_call | solution.py:145
  (82 shorter events, 23.4 us)
Async XLA Ops:
  0.7 13.0 %collective-permute-start.3 = (bf16[7168,256]{1,0:T(8,128)(2,1)}, bf16[7168,256]{1,0:T(8,128)(2,1)S(1)}, u32[]{:S(2)}, u32[]{:S(2)}) collective-permute-start(bf16[7168,256]{1,0:T(8,128)(2,1)} %bitcast.11), channel_id=1, source_target_pairs={{0,1},{1,0},{2,3},{3,2},{4,5},{5,4},{6,7},{7,6},{8,9},{9,8},{10,11... | collective-permute-start | bytes 11010056 | tf_op jit(solution)/shard_map/ppermute | solution.py:47
  2.2 11.5 %collective-permute-start.4 = (bf16[7168,256]{1,0:T(8,128)(2,1)}, bf16[7168,256]{1,0:T(8,128)(2,1)S(1)}, u32[]{:S(2)}, u32[]{:S(2)}) collective-permute-start(bf16[7168,256]{1,0:T(8,128)(2,1)} %bitcast.13), channel_id=1, source_target_pairs={{0,1},{1,0},{2,3},{3,2},{4,5},{5,4},{6,7},{7,6},{8,9},{9,8},{10,11... | collective-permute-start | bytes 11010056 | tf_op jit(solution)/shard_map/ppermute | solution.py:47
  5.1 8.6 %collective-permute-start.1 = (bf16[8,7296]{1,0:T(8,128)(2,1)S(1)}, bf16[8,7296]{1,0:T(8,128)(2,1)S(1)}, u32[]{:S(2)}, u32[]{:S(2)}) collective-permute-start(bf16[8,7296]{1,0:T(8,128)(2,1)S(1)} %shard_map.174), channel_id=1, source_target_pairs={{0,64},{1,65},{2,66},{3,67},{4,68},{5,69},{6,70},{7,71},{8,72},{9,... | collective-permute-start | bytes 350216 | tf_op jit(solution)/shard_map/ppermute | solution.py:47
  13.7 13.1 %collective-permute-start.11 = (bf16[256,7168]{1,0:T(8,128)(2,1)S(1)}, bf16[256,7168]{1,0:T(8,128)(2,1)S(1)}, u32[]{:S(2)}, u32[]{:S(2)}) collective-permute-start(bf16[256,7168]{1,0:T(8,128)(2,1)S(1)} %bitcast.16), channel_id=1, source_target_pairs={{0,1},{1,0},{2,3},{3,2},{4,5},{5,4},{6,7},{7,6},{8,9},{9,8},{10,11... | collective-permute-start | bytes 11010056 | tf_op jit(solution)/shard_map/ppermute | solution.py:47
  26.8 20.2 %collective-permute-start.18 = (bf16[576,3584]{1,0:T(8,128)(2,1)S(1)}, bf16[576,3584]{1,0:T(8,128)(2,1)S(1)}, u32[]{:S(2)}, u32[]{:S(2)}) collective-permute-start(bf16[576,3584]{1,0:T(8,128)(2,1)S(1)} %bitcast.10), channel_id=1, source_target_pairs={{0,1},{1,0},{2,3},{3,2},{4,5},{5,4},{6,7},{7,6},{8,9},{9,8},{10,11... | collective-permute-start | bytes 12386312 | tf_op jit(solution)/shard_map/ppermute | solution.py:47
  27.7 7.7 %collective-permute-start.12 = (bf16[32,7296]{1,0:T(8,128)(2,1)S(1)}, bf16[32,7296]{1,0:T(8,128)(2,1)S(1)}, u32[]{:S(2)}, u32[]{:S(2)}) collective-permute-start(bf16[32,7296]{1,0:T(8,128)(2,1)S(1)} %pad_maximum_fusion.refs_0_), channel_id=1, source_target_pairs={{0,4},{1,17},{2,6},{3,19},{4,0},{5,21},{6,2},{7,23},{8,12},{9,25},... | collective-permute-start | bytes 1400840 | tf_op jit(solution)/shard_map/ppermute | solution.py:47
  27.9 8.9 %collective-permute-start.13 = (bf16[32,7296]{1,0:T(8,128)(2,1)S(1)}, bf16[32,7296]{1,0:T(8,128)(2,1)S(1)}, u32[]{:S(2)}, u32[]{:S(2)}) collective-permute-start(bf16[32,7296]{1,0:T(8,128)(2,1)S(1)} %pad_maximum_fusion.1.refs_1_), channel_id=1, source_target_pairs={{0,12},{1,49},{2,14},{3,51},{4,8},{5,53},{6,10},{7,55},{8,4},{9,57... | collective-permute-start | bytes 1400840 | tf_op jit(solution)/shard_map/ppermute | solution.py:47
  29.7 12.1 %collective-permute-start.15 = (bf16[32,7296]{1,0:T(8,128)(2,1)S(1)}, bf16[32,7296]{1,0:T(8,128)(2,1)S(1)}, u32[]{:S(2)}, u32[]{:S(2)}) collective-permute-start(bf16[32,7296]{1,0:T(8,128)(2,1)S(1)} %pad_maximum_fusion.refs_0_), channel_id=1, source_target_pairs={{0,12},{1,49},{2,14},{3,51},{4,8},{5,53},{6,10},{7,55},{8,4},{9,57... | collective-permute-start | bytes 1400840 | tf_op jit(solution)/shard_map/ppermute | solution.py:47
  30.6 11.3 %collective-permute-start.14 = (bf16[32,7296]{1,0:T(8,128)(2,1)S(1)}, bf16[32,7296]{1,0:T(8,128)(2,1)S(1)}, u32[]{:S(2)}, u32[]{:S(2)}) collective-permute-start(bf16[32,7296]{1,0:T(8,128)(2,1)S(1)} %pad_maximum_fusion.1.refs_1_), channel_id=1, source_target_pairs={{0,4},{1,17},{2,6},{3,19},{4,0},{5,21},{6,2},{7,23},{8,12},{9,25},... | collective-permute-start | bytes 1400840 | tf_op jit(solution)/shard_map/ppermute | solution.py:47
  36.8 10.2 %collective-permute-start.16 = (bf16[32,7296]{1,0:T(8,128)(2,1)S(1)}, bf16[32,7296]{1,0:T(8,128)(2,1)S(1)}, u32[]{:S(2)}, u32[]{:S(2)}) collective-permute-start(bf16[32,7296]{1,0:T(8,128)(2,1)S(1)} %collective-permute-done.12.refs_2_), channel_id=1, source_target_pairs={{0,12},{1,49},{2,14},{3,51},{4,8},{5,53},{6,10},{7,55},{8,4},{9,57... | collective-permute-start | bytes 1400840 | tf_op jit(solution)/shard_map/ppermute | solution.py:47
  38.6 8.4 %collective-permute-start.17 = (bf16[32,7296]{1,0:T(8,128)(2,1)S(1)}, bf16[32,7296]{1,0:T(8,128)(2,1)S(1)}, u32[]{:S(2)}, u32[]{:S(2)}) collective-permute-start(bf16[32,7296]{1,0:T(8,128)(2,1)S(1)} %collective-permute-done.13.refs_5_), channel_id=1, source_target_pairs={{0,4},{1,17},{2,6},{3,19},{4,0},{5,21},{6,2},{7,23},{8,12},{9,25},... | collective-permute-start | bytes 1400840 | tf_op jit(solution)/shard_map/ppermute | solution.py:47
  47.8 7.7 %collective-permute-start.23 = (bf16[32,7168]{1,0:T(8,128)(2,1)S(1)}, bf16[32,7168]{1,0:T(8,128)(2,1)S(1)}, u32[]{:S(2)}, u32[]{:S(2)}) collective-permute-start(bf16[32,7168]{1,0:T(8,128)(2,1)S(1)} %get-tuple-element.73), channel_id=1, source_target_pairs={{0,4},{1,17},{2,6},{3,19},{4,0},{5,21},{6,2},{7,23},{8,12},{9,25},... | collective-permute-start | bytes 1376264 | tf_op jit(solution)/shard_map/ppermute | solution.py:47
  47.9 9.6 %collective-permute-start.19 = (bf16[32,7168]{1,0:T(8,128)(2,1)S(1)}, bf16[32,7168]{1,0:T(8,128)(2,1)S(1)}, u32[]{:S(2)}, u32[]{:S(2)}) collective-permute-start(bf16[32,7168]{1,0:T(8,128)(2,1)S(1)} %get-tuple-element.68), channel_id=1, source_target_pairs={{0,12},{1,49},{2,14},{3,51},{4,8},{5,53},{6,10},{7,55},{8,4},{9,57... | collective-permute-start | bytes 1376264 | tf_op jit(solution)/shard_map/ppermute | solution.py:47
  49.8 18.4 %collective-permute-start.21 = (bf16[32,7168]{1,0:T(8,128)(2,1)S(1)}, bf16[32,7168]{1,0:T(8,128)(2,1)S(1)}, u32[]{:S(2)}, u32[]{:S(2)}) collective-permute-start(bf16[32,7168]{1,0:T(8,128)(2,1)S(1)} %get-tuple-element.69), channel_id=1, source_target_pairs={{0,12},{1,49},{2,14},{3,51},{4,8},{5,53},{6,10},{7,55},{8,4},{9,57... | collective-permute-start | bytes 1376264 | tf_op jit(solution)/shard_map/ppermute | solution.py:47
  50.6 9.8 %collective-permute-start.22 = (bf16[32,7168]{1,0:T(8,128)(2,1)S(1)}, bf16[32,7168]{1,0:T(8,128)(2,1)S(1)}, u32[]{:S(2)}, u32[]{:S(2)}) collective-permute-start(bf16[32,7168]{1,0:T(8,128)(2,1)S(1)} %get-tuple-element.71), channel_id=1, source_target_pairs={{0,4},{1,17},{2,6},{3,19},{4,0},{5,21},{6,2},{7,23},{8,12},{9,25},... | collective-permute-start | bytes 1376264 | tf_op jit(solution)/shard_map/ppermute | solution.py:47
  55.6 11.0 %collective-permute-start.24 = (bf16[32,7168]{1,0:T(8,128)(2,1)S(1)}, bf16[32,7168]{1,0:T(8,128)(2,1)S(1)}, u32[]{:S(2)}, u32[]{:S(2)}) collective-permute-start(bf16[32,7168]{1,0:T(8,128)(2,1)S(1)} %add_convert_fusion.1), channel_id=1, source_target_pairs={{0,12},{1,49},{2,14},{3,51},{4,8},{5,53},{6,10},{7,55},{8,4},{9,57... | collective-permute-start | bytes 1376264 | tf_op jit(solution)/shard_map/ppermute | solution.py:47
  57.6 10.6 %collective-permute-start.20 = (bf16[32,7168]{1,0:T(8,128)(2,1)S(1)}, bf16[32,7168]{1,0:T(8,128)(2,1)S(1)}, u32[]{:S(2)}, u32[]{:S(2)}) collective-permute-start(bf16[32,7168]{1,0:T(8,128)(2,1)S(1)} %add_convert_fusion.3), channel_id=1, source_target_pairs={{0,4},{1,17},{2,6},{3,19},{4,0},{5,21},{6,2},{7,23},{8,12},{9,25},... | collective-permute-start | bytes 1376264 | tf_op jit(solution)/shard_map/ppermute | solution.py:47
  68.4 6.8 %collective-permute-start.29 = (bf16[8,7168]{1,0:T(8,128)(2,1)S(1)}, bf16[8,7168]{1,0:T(8,128)(2,1)S(1)}, u32[]{:S(2)}, u32[]{:S(2)}) collective-permute-start(bf16[8,7168]{1,0:T(8,128)(2,1)S(1)} %slice.37), channel_id=1, source_target_pairs={{0,16},{1,5},{2,18},{3,7},{4,20},{5,1},{6,22},{7,3},{8,24},{9,13},... | collective-permute-start | bytes 344072 | tf_op jit(solution)/shard_map/ppermute | solution.py:47
  68.6 6.5 %collective-permute-start.25 = (bf16[8,7168]{1,0:T(8,128)(2,1)S(1)}, bf16[8,7168]{1,0:T(8,128)(2,1)S(1)}, u32[]{:S(2)}, u32[]{:S(2)}) collective-permute-start(bf16[8,7168]{1,0:T(8,128)(2,1)S(1)} %get-tuple-element.88), channel_id=1, source_target_pairs={{0,48},{1,13},{2,50},{3,15},{4,52},{5,9},{6,54},{7,11},{8,56},{9,5... | collective-permute-start | bytes 344072 | tf_op jit(solution)/shard_map/ppermute | solution.py:47
  74.4 9.9 %collective-permute-start.27 = (bf16[8,7168]{1,0:T(8,128)(2,1)S(1)}, bf16[8,7168]{1,0:T(8,128)(2,1)S(1)}, u32[]{:S(2)}, u32[]{:S(2)}) collective-permute-start(bf16[8,7168]{1,0:T(8,128)(2,1)S(1)} %get-tuple-element.87), channel_id=1, source_target_pairs={{0,48},{1,13},{2,50},{3,15},{4,52},{5,9},{6,54},{7,11},{8,56},{9,5... | collective-permute-start | bytes 344072 | tf_op jit(solution)/shard_map/ppermute | solution.py:47
  77.4 6.9 %collective-permute-start.26 = (bf16[8,7168]{1,0:T(8,128)(2,1)S(1)}, bf16[8,7168]{1,0:T(8,128)(2,1)S(1)}, u32[]{:S(2)}, u32[]{:S(2)}) collective-permute-start(bf16[8,7168]{1,0:T(8,128)(2,1)S(1)} %get-tuple-element.85), channel_id=1, source_target_pairs={{0,16},{1,5},{2,18},{3,7},{4,20},{5,1},{6,22},{7,3},{8,24},{9,13},... | collective-permute-start | bytes 344072 | tf_op jit(solution)/shard_map/ppermute | solution.py:47
  77.5 11.2 %collective-permute-start.32 = (bf16[8,7168]{1,0:T(8,128)(2,1)S(1)}, bf16[8,7168]{1,0:T(8,128)(2,1)S(1)}, u32[]{:S(2)}, u32[]{:S(2)}) collective-permute-start(bf16[8,7168]{1,0:T(8,128)(2,1)S(1)} %get-tuple-element.84), channel_id=1, source_target_pairs={{0,64},{1,65},{2,66},{3,67},{4,68},{5,69},{6,70},{7,71},{8,72},{9,... | collective-permute-start | bytes 344072 | tf_op jit(solution)/shard_map/ppermute | solution.py:47
  84.3 7.8 %collective-permute-start.28 = (bf16[8,7168]{1,0:T(8,128)(2,1)S(1)}, bf16[8,7168]{1,0:T(8,128)(2,1)S(1)}, u32[]{:S(2)}, u32[]{:S(2)}) collective-permute-start(bf16[8,7168]{1,0:T(8,128)(2,1)S(1)} %add_convert_fusion.6), channel_id=1, source_target_pairs={{0,66},{1,67},{2,64},{3,65},{4,70},{5,71},{6,68},{7,69},{8,74},{9,... | collective-permute-start | bytes 344072 | tf_op jit(solution)/shard_map/ppermute | solution.py:47
  95.0 6.8 %collective-permute-start.34 = (bf16[8,7168]{1,0:T(8,128)(2,1)S(1)}, bf16[8,7168]{1,0:T(8,128)(2,1)S(1)}, u32[]{:S(2)}, u32[]{:S(2)}) collective-permute-start(bf16[8,7168]{1,0:T(8,128)(2,1)S(1)} %get-tuple-element.79.updated_own), channel_id=1, source_target_pairs={{0,1},{1,0},{2,3},{3,2},{4,5},{5,4},{6,7},{7,6},{8,9},{9,8},{10,11... | collective-permute-start | bytes 344072 | tf_op jit(solution)/shard_map/ppermute | solution.py:47
  (18 other events, 216.1 us)
